TPU v7x, 512 devices: a whole 4x8x8 slice. The times are simulated.
512 devices in a mesh: harm: 64 (over z, x, core), bus: 8 (over y).
Axes of the slice: x: 4, y: 8, z: 8, core: 2. Of those that a mesh axis runs over, the one named last changes fastest.
Arguments:
- conv_volt: bfloat16 [2, 64, 2048, 128], P(None, None, ('bus', 'harm')), may hold values from -0.75 to 0.75
- conv_power: float32 [2048, 128], P(('bus', 'harm')), may hold values from 0.2 to 2
- conv_type: int32 [2048], P(('bus', 'harm')), may hold values from 0 to 7
- type_steep: float32 [8], replicated, may hold values from 0.5 to 4
- conv_bus: int32 [2048], P(('bus', 'harm')), may hold values from 0 to 8191, as said below
- admittance: float32 [2, 4, 64, 8192], P(None, None, 'harm', 'bus'), may hold values from -0.5 to 1
- link_offset: int32 [3, 8192], P(None, 'bus'), may hold values from -8 to 8, as said below
Outputs:
- bus_volt: bfloat16 [2, 64, 8192, 128], P(None, 'harm', 'bus')
- conv_next: bfloat16 [2, 64, 2048, 128], P(None, None, ('bus', 'harm'))
Inputs may be any that keep to these rules, and one draw needn't show every extreme that they name: `conv_bus`: converter c is attached to one of the buses from (c // 4) * 16 to (c // 4 + 1) * 16 - 1; a bus may carry several converters. `link_offset`: the first line of every bus spans exactly 8 buses, up or down; the others span 1 to 8 buses; no offset is zero.
All inputs are finite; a program needn't handle non-finite values.
Results may differ from a plain program's by a relative error of at most 0.0057.
Values may be sent and summed in bfloat16 or wider, within the bound.
No kernel may reach another device: no remote copies, remote signals or barrier semaphores. Data moves between devices by JAX's collectives and lax.ppermute only.
A program may use at most 64 MiB of HBM per device.

v0:
```python
import math

import jax
import jax.numpy as jnp
from jax import lax
from jax.sharding import PartitionSpec as P

H = 64
NT = 1024
REACH = 8
ITERS = 3


def as_sent(array):
    return jax.tree.map(lambda a: a.astype(jnp.bfloat16) if a.dtype == jnp.float32 else a, array)


def extended_2(cells, sides, width):
    for axis, dim in sides:
        count = lax.axis_size(axis)
        ends = count - 1
        head = lax.slice_in_dim(cells, 0, width, axis=dim)
        tail = lax.slice_in_dim(cells, cells.shape[dim] - width, cells.shape[dim], axis=dim)
        cells = jnp.concatenate(
            [
                lax.ppermute(tail, axis, [(i, (i + 1) % count) for i in range(ends)]),
                cells,
                lax.ppermute(head, axis, [((i + 1) % count, i) for i in range(ends)]),
            ],
            axis=dim,
        )
    return cells


def make_basis():
    orders = jnp.arange(1, H + 1, dtype=jnp.int32)
    samples = jnp.arange(NT, dtype=jnp.int32)
    phases = (orders[:, None] * samples[None, :] % NT).astype(jnp.float32) * (2.0 * math.pi / NT)
    return jnp.concatenate([jnp.cos(phases), -jnp.sin(phases)], axis=0).astype(jnp.bfloat16)


def complex_product(left_real, left_imag, right_real, right_imag):
    return (
        left_real * right_real - left_imag * right_imag,
        left_real * right_imag + left_imag * right_real,
    )


def line_sum(inject_real, inject_imag, volt_real, volt_imag, lines_real, lines_imag, targets):
    total_real, total_imag = (inject_real, inject_imag)
    for line_num in range(targets.shape[0]):
        near_real = jnp.take(volt_real, targets[line_num], axis=1)
        near_imag = jnp.take(volt_imag, targets[line_num], axis=1)
        term_real, term_imag = complex_product(
            lines_real[line_num][:, :, None], lines_imag[line_num][:, :, None], near_real, near_imag
        )
        total_real = total_real + term_real
        total_imag = total_imag + term_imag
    return (total_real, total_imag)


def local(conv_volt, conv_power, conv_type, type_steep, conv_bus, admittance, link_offset):
    harm_count = lax.axis_size("harm")
    block_rows = admittance.shape[3]
    sub_rows = block_rows // harm_count
    conv_count = conv_volt.shape[2]
    snapshots = conv_volt.shape[3]
    first_bus = lax.axis_index("bus") * block_rows
    local_bus = conv_bus - (first_bus + lax.axis_index("harm") * sub_rows)
    harmonic_basis = make_basis()
    matches = conv_type[:, None] == jnp.arange(type_steep.shape[0], dtype=jnp.int32)[None, :]
    steepness = jnp.sum(jnp.where(matches, type_steep[None, :], 0.0), axis=1)
    volt_rows = conv_volt.reshape(2 * H, conv_count, snapshots)
    block_size = min(conv_count, 4)
    waveform = jnp.einsum(
        "kcs,kn->csn", volt_rows, harmonic_basis, preferred_element_type=jnp.float32
    )
    current = (
        conv_power[0:block_size, :, None] * jnp.tanh(steepness[0:block_size, None, None] * waveform)
    ).astype(jnp.bfloat16)
    spectra = jnp.einsum(
        "csn,kn->kcs", current, harmonic_basis, preferred_element_type=jnp.float32
    ) * NT ** (-0.5)
    pieces = spectra.astype(jnp.bfloat16)
    spectra = pieces.reshape(2, H, conv_count, snapshots)
    owners = (local_bus[None, :] == jnp.arange(sub_rows, dtype=jnp.int32)[:, None]).astype(
        jnp.bfloat16
    )
    summed = jnp.einsum("uc,phcs->phus", owners, spectra, preferred_element_type=jnp.float32)
    injection = lax.all_to_all(
        summed.astype(jnp.bfloat16), "harm", split_axis=1, concat_axis=2, tiled=True
    )
    inject_real = injection[0].astype(jnp.float32)
    inject_imag = injection[1].astype(jnp.float32)
    inverse_real = admittance[0, 0][:, :, None]
    inverse_imag = admittance[1, 0][:, :, None]
    volt_real, volt_imag = complex_product(inverse_real, inverse_imag, inject_real, inject_imag)
    targets = jnp.arange(block_rows, dtype=jnp.int32)[None, :] + REACH + link_offset
    for sweep_index in range(ITERS - 1):
        extended = extended_2(as_sent(jnp.stack([volt_real, volt_imag])), (("bus", 2),), REACH)
        total_real, total_imag = line_sum(
            inject_real,
            inject_imag,
            extended[0],
            extended[1],
            admittance[0, 1:],
            admittance[1, 1:],
            targets,
        )
        volt_real, volt_imag = complex_product(inverse_real, inverse_imag, total_real, total_imag)
    bus_volt = jnp.stack([volt_real, volt_imag]).astype(jnp.bfloat16)
    returned = lax.all_to_all(bus_volt, "harm", split_axis=2, concat_axis=1, tiled=True)
    conv_next = jnp.take(returned, local_bus, axis=2)
    return (bus_volt, conv_next)


def solution(mesh):
    in_specs = (
        P(None, None, ("bus", "harm"), None),
        P(("bus", "harm"), None),
        P(("bus", "harm")),
        P(),
        P(("bus", "harm")),
        P(None, None, "harm", "bus"),
        P(None, "bus"),
    )
    out_specs = (P(None, "harm", "bus", None), P(None, None, ("bus", "harm"), None))
    return jax.shard_map(local, mesh=mesh, in_specs=in_specs, out_specs=out_specs, check_vma=False)
```

profile of v0, /device:TPU:17, one launch (start us, length us, event | category | flops | bytes accessed | tf_op | source)
XLA Modules:
  0.0 128.5 jit_solution(18123431177943175407)
XLA Ops:
  0.6 0.0 copy-start
  0.7 1.2 cosine_convert_fusion
  1.9 0.7 compare_and_fusion.3
  2.6 0.9 select_reduce_fusion
  3.4 0.0 copy-done
  3.4 1.3 %fusion.4 = bf16[128,4,128]{2,0,1:T(8,128)(2,1)S(1)} fusion(f32[4]{0:T(128)S(1)} %select_reduce_fusion, f32[4,128]{1,0:T(4,128)} %param.10, bf16[64,1024]{1,0:T(8,128)(2,1)S(1)} %get-tuple-element.47, bf16[64,1024]{1,0:T(8,128)(2,1)S(1)} %get-tuple-element.46, bf16[128,4,128]{2,1,0:T(4,128)(2,1)S(1)} %bitcast.172), kind=kOutput, calls=%fused_computation.19 | convolution fusion | flops 271187968 | bytes 526352 | tf_op jit(solution)/shard_map/csn,kn->kcs/dot_general | solution.py:81
  4.8 0.4 fusion.2
  5.2 0.8 copy.51
  6.0 0.0 copy-start.3
  6.0 0.0 copy-start.2
  6.0 14.1 %all-to-all-start = ((bf16[2,64,16,128]{3,2,0,1:T(8,128)(2,1)}), bf16[2,64,16,128]{3,2,0,1:T(8,128)(2,1)S(1)}, u32[]{:S(2)}, u32[]{:S(2)}) async-start(bf16[2,64,16,128]{3,2,0,1:T(8,128)(2,1)} %copy.51), calls=%async_computation | async-start | bytes 1048576 | tf_op jit(solution)/shard_map/all_to_all | solution.py:90
  20.2 0.0 copy-done.3
  20.3 0.0 copy-done.2
  20.3 17.6 %all-to-all-done = bf16[2,64,16,128]{3,2,0,1:T(8,128)(2,1)S(1)} async-done(((bf16[2,64,16,128]{3,2,0,1:T(8,128)(2,1)}), bf16[2,64,16,128]{3,2,0,1:T(8,128)(2,1)S(1)}, u32[]{:S(2)}, u32[]{:S(2)}) %all-to-all-start) | async-done | bytes 524320 | tf_op jit(solution)/shard_map/all_to_all | solution.py:90
  37.9 0.3 fusion.39
  38.3 3.2 %collective-permute-start = (bf16[2,1,8,128]{3,2,1,0:T(8,128)(2,1)S(1)}, bf16[2,1,8,128]{3,2,1,0:T(8,128)(2,1)S(1)}, u32[]{:S(2)}, u32[]{:S(2)}) collective-permute-start(bf16[2,1,8,128]{3,2,1,0:T(8,128)(2,1)S(1)} %get-tuple-element.31), channel_id=1, source_target_pairs={{0,1},{1,2},{2,3},{3,4},{4,5},{5,6},{6,7},{8,9},{9,10},{10,11},{11... | collective-permute-start | bytes 12296 | tf_op jit(solution)/shard_map/ppermute | solution.py:26
  41.5 2.1 %collective-permute-start.1 = (bf16[2,1,8,128]{3,2,1,0:T(8,128)(2,1)S(1)}, bf16[2,1,8,128]{3,2,1,0:T(8,128)(2,1)S(1)}, u32[]{:S(2)}, u32[]{:S(2)}) collective-permute-start(bf16[2,1,8,128]{3,2,1,0:T(8,128)(2,1)S(1)} %get-tuple-element.32), channel_id=1, source_target_pairs={{1,0},{2,1},{3,2},{4,3},{5,4},{6,5},{7,6},{9,8},{10,9},{11,10},{12... | collective-permute-start | bytes 12296 | tf_op jit(solution)/shard_map/ppermute | solution.py:28
  43.6 0.0 collective-permute-done
  43.6 3.3 %collective-permute-done.1 = bf16[2,1,8,128]{3,2,1,0:T(8,128)(2,1)S(1)} collective-permute-done((bf16[2,1,8,128]{3,2,1,0:T(8,128)(2,1)S(1)}, bf16[2,1,8,128]{3,2,1,0:T(8,128)(2,1)S(1)}, u32[]{:S(2)}, u32[]{:S(2)}) %collective-permute-start.1) | collective-permute-done | bytes 4128 | tf_op jit(solution)/shard_map/ppermute | solution.py:28
  47.0 3.2 %gather_fusion.1 = bf16[1024,128]{1,0:T(8,128)(2,1)S(1)} fusion(bf16[1040,128]{1,0:T(8,128)(2,1)S(1)} %get-tuple-element.26, s32[1024]{0:T(1024)S(1)} %fusion.52), kind=kCustom, calls=%fused_computation.clone | custom fusion | bytes 528384 | tf_op jit(solution)/shard_map/jit(_take)/gather | solution.py:52
  50.2 3.2 %gather_fusion.2 = bf16[1024,128]{1,0:T(8,128)(2,1)S(1)} fusion(bf16[1040,128]{1,0:T(8,128)(2,1)S(1)} %get-tuple-element.25, s32[1024]{0:T(1024)S(1)} %fusion.52), kind=kCustom, calls=%fused_computation.1.clone | custom fusion | bytes 528384 | tf_op jit(solution)/shard_map/jit(_take)/gather | solution.py:53
  53.4 3.2 %gather_fusion.3 = bf16[1024,128]{1,0:T(8,128)(2,1)S(1)} fusion(bf16[1040,128]{1,0:T(8,128)(2,1)S(1)} %get-tuple-element.26, s32[1024]{0:T(1024)S(1)} %fusion.50), kind=kCustom, calls=%fused_computation.2.clone | custom fusion | bytes 528384 | tf_op jit(solution)/shard_map/jit(_take)/gather | solution.py:52
  56.6 3.2 %gather_fusion.4 = bf16[1024,128]{1,0:T(8,128)(2,1)S(1)} fusion(bf16[1040,128]{1,0:T(8,128)(2,1)S(1)} %get-tuple-element.25, s32[1024]{0:T(1024)S(1)} %fusion.50), kind=kCustom, calls=%fused_computation.3.clone | custom fusion | bytes 528384 | tf_op jit(solution)/shard_map/jit(_take)/gather | solution.py:53
  59.9 3.2 %gather_fusion.5 = bf16[1024,128]{1,0:T(8,128)(2,1)S(1)} fusion(bf16[1040,128]{1,0:T(8,128)(2,1)S(1)} %get-tuple-element.26, s32[1024]{0:T(1024)S(1)} %fusion.51), kind=kCustom, calls=%fused_computation.4.clone | custom fusion | bytes 528384 | tf_op jit(solution)/shard_map/jit(_take)/gather | solution.py:52
  63.1 3.2 %gather_fusion.6 = bf16[1024,128]{1,0:T(8,128)(2,1)S(1)} fusion(bf16[1040,128]{1,0:T(8,128)(2,1)S(1)} %get-tuple-element.25, s32[1024]{0:T(1024)S(1)} %fusion.51), kind=kCustom, calls=%fused_computation.5.clone | custom fusion | bytes 528384 | tf_op jit(solution)/shard_map/jit(_take)/gather | solution.py:53
  66.3 1.9 %fusion.34 = (bf16[1,1,1024,128]{3,2,1,0:T(8,128)(2,1)S(1)}, f32[1,1024,128]{2,1,0:T(8,128)S(1)}, f32[1,1024,128]{2,1,0:T(8,128)S(1)}) fusion(f32[1024]{0:T(1024)S(1)} %bitcast.181, f32[1024]{0:T(1024)S(1)} %bitcast.186, bf16[1024,128]{1,0:T(8,128)(2,1)S(1)} %gather_fusion.5, f32[1024]{0:T(1024)S(1)} %bitcast.199, bf16[1024,128]{1,0:T(8,128)(2,1)S(1)} %gather_fusion.6, ...), kind=kLoop, calls=%fused_computation.95 | loop fusion | flops 5505024 | bytes 3443712 | tf_op jit(solution)/shard_map/stack | solution.py:100
  68.2 0.3 fusion.35
  68.6 4.6 %collective-permute-start.2 = (bf16[2,1,8,128]{3,2,1,0:T(8,128)(2,1)S(1)}, bf16[2,1,8,128]{3,2,1,0:T(8,128)(2,1)S(1)}, u32[]{:S(2)}, u32[]{:S(2)}) collective-permute-start(bf16[2,1,8,128]{3,2,1,0:T(8,128)(2,1)S(1)} %get-tuple-element.29), channel_id=1, source_target_pairs={{0,1},{1,2},{2,3},{3,4},{4,5},{5,6},{6,7},{8,9},{9,10},{10,11},{11... | collective-permute-start | bytes 12296 | tf_op jit(solution)/shard_map/ppermute | solution.py:26
  73.1 1.9 %collective-permute-start.3 = (bf16[2,1,8,128]{3,2,1,0:T(8,128)(2,1)S(1)}, bf16[2,1,8,128]{3,2,1,0:T(8,128)(2,1)S(1)}, u32[]{:S(2)}, u32[]{:S(2)}) collective-permute-start(bf16[2,1,8,128]{3,2,1,0:T(8,128)(2,1)S(1)} %get-tuple-element.30), channel_id=1, source_target_pairs={{1,0},{2,1},{3,2},{4,3},{5,4},{6,5},{7,6},{9,8},{10,9},{11,10},{12... | collective-permute-start | bytes 12296 | tf_op jit(solution)/shard_map/ppermute | solution.py:28
  75.1 0.0 collective-permute-done.2
  75.1 2.4 %collective-permute-done.3 = bf16[2,1,8,128]{3,2,1,0:T(8,128)(2,1)S(1)} collective-permute-done((bf16[2,1,8,128]{3,2,1,0:T(8,128)(2,1)S(1)}, bf16[2,1,8,128]{3,2,1,0:T(8,128)(2,1)S(1)}, u32[]{:S(2)}, u32[]{:S(2)}) %collective-permute-start.3) | collective-permute-done | bytes 4128 | tf_op jit(solution)/shard_map/ppermute | solution.py:28
  77.6 3.2 %gather_fusion.7 = bf16[1024,128]{1,0:T(8,128)(2,1)S(1)} fusion(bf16[1040,128]{1,0:T(8,128)(2,1)S(1)} %get-tuple-element.24, s32[1024]{0:T(1024)S(1)} %fusion.52), kind=kCustom, calls=%fused_computation.6.clone | custom fusion | bytes 528384 | tf_op jit(solution)/shard_map/jit(_take)/gather | solution.py:52
  80.8 3.2 %gather_fusion.9 = bf16[1024,128]{1,0:T(8,128)(2,1)S(1)} fusion(bf16[1040,128]{1,0:T(8,128)(2,1)S(1)} %get-tuple-element.24, s32[1024]{0:T(1024)S(1)} %fusion.50), kind=kCustom, calls=%fused_computation.8.clone | custom fusion | bytes 528384 | tf_op jit(solution)/shard_map/jit(_take)/gather | solution.py:52
  84.0 3.2 %gather_fusion.8 = bf16[1024,128]{1,0:T(8,128)(2,1)S(1)} fusion(bf16[1040,128]{1,0:T(8,128)(2,1)S(1)} %get-tuple-element.23, s32[1024]{0:T(1024)S(1)} %fusion.52), kind=kCustom, calls=%fused_computation.7.clone | custom fusion | bytes 528384 | tf_op jit(solution)/shard_map/jit(_take)/gather | solution.py:53
  87.2 3.2 %gather_fusion.10 = bf16[1024,128]{1,0:T(8,128)(2,1)S(1)} fusion(bf16[1040,128]{1,0:T(8,128)(2,1)S(1)} %get-tuple-element.23, s32[1024]{0:T(1024)S(1)} %fusion.50), kind=kCustom, calls=%fused_computation.9.clone | custom fusion | bytes 528384 | tf_op jit(solution)/shard_map/jit(_take)/gather | solution.py:53
  90.5 3.2 %gather_fusion.12 = bf16[1024,128]{1,0:T(8,128)(2,1)S(1)} fusion(bf16[1040,128]{1,0:T(8,128)(2,1)S(1)} %get-tuple-element.23, s32[1024]{0:T(1024)S(1)} %fusion.51), kind=kCustom, calls=%fused_computation.11.clone | custom fusion | bytes 528384 | tf_op jit(solution)/shard_map/jit(_take)/gather | solution.py:53
  93.7 3.2 %gather_fusion.11 = bf16[1024,128]{1,0:T(8,128)(2,1)S(1)} fusion(bf16[1040,128]{1,0:T(8,128)(2,1)S(1)} %get-tuple-element.24, s32[1024]{0:T(1024)S(1)} %fusion.51), kind=kCustom, calls=%fused_computation.10.clone | custom fusion | bytes 528384 | tf_op jit(solution)/shard_map/jit(_take)/gather | solution.py:52
  96.9 1.9 %fusion.36 = (bf16[1,1,1024,128]{3,2,1,0:T(8,128)(2,1)S(1)}, f32[1,1024,128]{2,1,0:T(8,128)S(1)}, f32[1,1024,128]{2,1,0:T(8,128)S(1)}) fusion(f32[1024]{0:T(1024)S(1)} %bitcast.183, f32[1024]{0:T(1024)S(1)} %bitcast.188, bf16[1024,128]{1,0:T(8,128)(2,1)S(1)} %gather_fusion.11, f32[1024]{0:T(1024)S(1)} %bitcast.200, bf16[1024,128]{1,0:T(8,128)(2,1)S(1)} %gather_fusion.12, ...), kind=kLoop, calls=%fused_computation.97 | loop fusion | flops 5505024 | bytes 3443712 | tf_op jit(solution)/shard_map/stack | solution.py:111
  98.8 0.3 fusion.37
  99.1 0.1 pad_maximum_fusion.2
  99.2 0.0 copy-start.1
  99.2 1.3 %copy.52 = bf16[2,1,1024,128]{3,0,1,2:T(2,128)(2,1)} copy(bf16[2,1,1024,128]{3,2,1,0:T(8,128)(2,1)S(1)} %pad_maximum_fusion.2) | data formatting | bytes 1048576 | tf_op jit(solution)/shard_map/stack | solution.py:111
  100.6 0.0 copy-done.1
  100.6 8.6 %all-to-all-start.1 = ((bf16[2,1,1024,128]{3,0,1,2:T(2,128)(2,1)}), bf16[2,1,1024,128]{3,0,1,2:T(2,128)(2,1)S(1)}, u32[]{:S(2)}, u32[]{:S(2)}) async-start(bf16[2,1,1024,128]{3,0,1,2:T(2,128)(2,1)} %copy.52), calls=%async_computation.1 | async-start | bytes 1048576 | tf_op jit(solution)/shard_map/all_to_all | solution.py:112
  109.2 17.7 %all-to-all-done.1 = bf16[2,1,1024,128]{3,0,1,2:T(2,128)(2,1)S(1)} async-done(((bf16[2,1,1024,128]{3,0,1,2:T(2,128)(2,1)}), bf16[2,1,1024,128]{3,0,1,2:T(2,128)(2,1)S(1)}, u32[]{:S(2)}, u32[]{:S(2)}) %all-to-all-start.1) | async-done | bytes 524320 | tf_op jit(solution)/shard_map/all_to_all | solution.py:112
  126.9 0.2 copy.54
  127.1 0.6 gather_fusion
  127.7 0.1 select_bitcast_fusion
  127.7 0.8 copy.55
  (19 shorter events, 0.3 us)
Async XLA Ops:
  0.6 2.8 %copy-start = (bf16[2,64,4,128]{3,2,1,0:T(4,128)(2,1)S(1)}, bf16[2,64,4,128]{3,2,1,0:T(4,128)(2,1)}, u32[]{:S(2)}) copy-start(bf16[2,64,4,128]{3,2,1,0:T(4,128)(2,1)} %param.9) | copy-start | bytes 393220
  6.0 14.2 %copy-start.3 = (s32[3,1024]{1,0:T(4,128)S(1)}, s32[3,1024]{1,0:T(4,128)}, u32[]{:S(2)}) copy-start(s32[3,1024]{1,0:T(4,128)} %param.15) | copy-start | bytes 36868
  6.0 14.3 %copy-start.2 = (f32[2,4,1,1024]{3,2,1,0:T(1,128)S(1)}, f32[2,4,1,1024]{3,2,1,0:T(1,128)}, u32[]{:S(2)}) copy-start(f32[2,4,1,1024]{3,2,1,0:T(1,128)} %param.14) | copy-start | bytes 98308
  6.0 31.9 %all-to-all-start = ((bf16[2,64,16,128]{3,2,0,1:T(8,128)(2,1)}), bf16[2,64,16,128]{3,2,0,1:T(8,128)(2,1)S(1)}, u32[]{:S(2)}, u32[]{:S(2)}) async-start(bf16[2,64,16,128]{3,2,0,1:T(8,128)(2,1)} %copy.51), calls=%async_computation | async-start | bytes 1048576 | tf_op jit(solution)/shard_map/all_to_all | solution.py:90
  38.3 5.3 %collective-permute-start = (bf16[2,1,8,128]{3,2,1,0:T(8,128)(2,1)S(1)}, bf16[2,1,8,128]{3,2,1,0:T(8,128)(2,1)S(1)}, u32[]{:S(2)}, u32[]{:S(2)}) collective-permute-start(bf16[2,1,8,128]{3,2,1,0:T(8,128)(2,1)S(1)} %get-tuple-element.31), channel_id=1, source_target_pairs={{0,1},{1,2},{2,3},{3,4},{4,5},{5,6},{6,7},{8,9},{9,10},{10,11},{11... | collective-permute-start | bytes 12296 | tf_op jit(solution)/shard_map/ppermute | solution.py:26
  41.5 5.4 %collective-permute-start.1 = (bf16[2,1,8,128]{3,2,1,0:T(8,128)(2,1)S(1)}, bf16[2,1,8,128]{3,2,1,0:T(8,128)(2,1)S(1)}, u32[]{:S(2)}, u32[]{:S(2)}) collective-permute-start(bf16[2,1,8,128]{3,2,1,0:T(8,128)(2,1)S(1)} %get-tuple-element.32), channel_id=1, source_target_pairs={{1,0},{2,1},{3,2},{4,3},{5,4},{6,5},{7,6},{9,8},{10,9},{11,10},{12... | collective-permute-start | bytes 12296 | tf_op jit(solution)/shard_map/ppermute | solution.py:28
  68.6 6.5 %collective-permute-start.2 = (bf16[2,1,8,128]{3,2,1,0:T(8,128)(2,1)S(1)}, bf16[2,1,8,128]{3,2,1,0:T(8,128)(2,1)S(1)}, u32[]{:S(2)}, u32[]{:S(2)}) collective-permute-start(bf16[2,1,8,128]{3,2,1,0:T(8,128)(2,1)S(1)} %get-tuple-element.29), channel_id=1, source_target_pairs={{0,1},{1,2},{2,3},{3,4},{4,5},{5,6},{6,7},{8,9},{9,10},{10,11},{11... | collective-permute-start | bytes 12296 | tf_op jit(solution)/shard_map/ppermute | solution.py:26
  73.1 4.4 %collective-permute-start.3 = (bf16[2,1,8,128]{3,2,1,0:T(8,128)(2,1)S(1)}, bf16[2,1,8,128]{3,2,1,0:T(8,128)(2,1)S(1)}, u32[]{:S(2)}, u32[]{:S(2)}) collective-permute-start(bf16[2,1,8,128]{3,2,1,0:T(8,128)(2,1)S(1)} %get-tuple-element.30), channel_id=1, source_target_pairs={{1,0},{2,1},{3,2},{4,3},{5,4},{6,5},{7,6},{9,8},{10,9},{11,10},{12... | collective-permute-start | bytes 12296 | tf_op jit(solution)/shard_map/ppermute | solution.py:28
  99.2 1.4 %copy-start.1 = (bf16[2,1,1024,128]{3,2,1,0:T(8,128)(2,1)}, bf16[2,1,1024,128]{3,2,1,0:T(8,128)(2,1)S(1)}, u32[]{:S(2)}) copy-start(bf16[2,1,1024,128]{3,2,1,0:T(8,128)(2,1)S(1)} %pad_maximum_fusion.2) | copy-start | bytes 1572868
  100.6 26.3 %all-to-all-start.1 = ((bf16[2,1,1024,128]{3,0,1,2:T(2,128)(2,1)}), bf16[2,1,1024,128]{3,0,1,2:T(2,128)(2,1)S(1)}, u32[]{:S(2)}, u32[]{:S(2)}) async-start(bf16[2,1,1024,128]{3,0,1,2:T(2,128)(2,1)} %copy.52), calls=%async_computation.1 | async-start | bytes 1048576 | tf_op jit(solution)/shard_map/all_to_all | solution.py:112
where the time goes:
time: 129 us
  local copies, waits for them, and re-layouts  42.4 us (33%)
  waiting for transfers between devices  41 us (32%)
  starting transfers between devices  34.5 us (27%)
  other arithmetic  7.87 us (6%)
  matrix products  1.74 us (1%)
    gather x6, local copies, waits for them, and re-layouts, line_sum(): near_real = jnp.take(volt_real, targets[line_num], axis=1)  19.3 us
    gather x6, local copies, waits for them, and re-layouts, line_sum(): near_imag = jnp.take(volt_imag, targets[line_num], axis=1)  19.3 us
    all_to_all x1, waiting for transfers between devices, local(): lax.all_to_all(bus_volt, 'harm', split_axis=2, concat_axis=1, tiled=True)  17.7 us
    all_to_all x1, waiting for transfers between devices, local(): lax.all_to_all(summed.astype(jnp.bfloat16), 'harm', split_axis=1, concat_...  17.6 us
    all_to_all x1, starting transfers between devices, local(): lax.all_to_all(summed.astype(jnp.bfloat16), 'harm', split_axis=1, concat_...  14.1 us
    all_to_all x1, starting transfers between devices, local(): lax.all_to_all(bus_volt, 'harm', split_axis=2, concat_axis=1, tiled=True)  8.58 us
    ppermute x2, starting transfers between devices, extended_2(): lax.ppermute(tail, axis, [(i, (i + 1) % count) for i in range(ends)])  7.78 us
    ppermute x2, waiting for transfers between devices, extended_2(): lax.ppermute(head, axis, [((i + 1) % count, i) for i in range(ends)])  5.71 us
  transfers between devices with their start and end apart: 6, of which 4 were waited for; matrix products, arithmetic and copies ran while one was open for 0% of the time, Pallas kernels for 0%

commit v1 on v0

v1 whole, which is shorter than its diff:
```python
import math

import jax
import jax.numpy as jnp
import numpy as np
from jax import lax
from jax.experimental import pallas as pl
from jax.experimental.pallas import tpu as pltpu
from jax.sharding import PartitionSpec as P

H = 64
NT = 1024
REACH = 8
LINKS = 3
SUB = 16
CONV = 4
EDGE = 2 * REACH
TILE = 128
WIN = 256
ROWS = 12
F32 = jnp.float32
BF16 = jnp.bfloat16


def make_basis():
    turn = np.arange(1, H + 1)[:, None] * np.arange(NT)[None, :] % NT
    angle = turn * (2.0 * math.pi / NT)
    return np.concatenate([np.cos(angle), -np.sin(angle)], axis=0).astype(BF16)


def iota(shape, dim):
    return lax.broadcasted_iota(jnp.int32, shape, dim)


def sweeps_kernel(adm_ref, off_ref, q_ref):
    inv_r, inv_i = adm_ref[0:1, :], adm_ref[4:5, :]
    steps = []
    for k in range(1, 1 + LINKS):
        line_r, line_i = adm_ref[k : k + 1, :], adm_ref[4 + k : 5 + k, :]
        steps.append((inv_r * line_r - inv_i * line_i, inv_r * line_i + inv_i * line_r))
    rows = iota((WIN, WIN), 0)
    lanes = iota((1, WIN), 1)
    same = iota((TILE, WIN), 0) + EDGE == iota((TILE, WIN), 1)
    for b in range(q_ref.shape[0]):
        win = slice(b * TILE, b * TILE + WIN)
        turned_r = jnp.zeros((WIN, WIN), F32)
        turned_i = jnp.zeros((WIN, WIN), F32)
        for k in range(LINKS):
            here = rows == lanes + off_ref[k : k + 1, win]
            turned_r += jnp.where(here, steps[k][0][:, win], 0.0)
            turned_i += jnp.where(here, steps[k][1][:, win], 0.0)
        step_r, step_i = turned_r.T, turned_i.T
        mid_r, mid_i = step_r[EDGE : EDGE + TILE], step_i[EDGE : EDGE + TILE]
        twice = jnp.dot(
            jnp.concatenate([mid_r, mid_i], axis=0).astype(BF16),
            jnp.concatenate([step_r, step_i], axis=1).astype(BF16),
            preferred_element_type=F32,
        )
        all_r = twice[:TILE, :WIN] - twice[TILE:, WIN:] + mid_r + jnp.where(same, 1.0, 0.0)
        all_i = twice[:TILE, WIN:] + twice[TILE:, :WIN] + mid_i
        dr, di = inv_r[:, win], inv_i[:, win]
        q_ref[b, :TILE, :] = (all_r * dr - all_i * di).astype(BF16)
        q_ref[b, TILE:, :] = (all_r * di + all_i * dr).astype(BF16)


def network_kernel(got_ref, low_ref, high_ref, q_ref, volt_ref, near_ref, rows, inject, out):
    harm_count = got_ref.shape[0] // ROWS
    half = harm_count // 2
    rows[...] = got_ref[...].astype(F32)

    def part(p):
        return jnp.concatenate(
            [
                rows[pl.ds(h * half * ROWS + 2 * c + p, half, stride=ROWS), :]
                for h in range(2)
                for c in range(CONV)
            ],
            axis=0,
        )

    spectra = jnp.concatenate([part(0), part(1)], axis=1).astype(BF16)
    convs = harm_count * CONV
    at = [
        jnp.sum(rows[pl.ds(h * half * ROWS + ROWS - 1, half, stride=ROWS), :], axis=0, keepdims=True)
        for h in range(2)
    ]
    at = jnp.concatenate(at, axis=1).astype(jnp.int32)
    lane = iota((1, convs), 1)
    source = lane // (CONV * half) * half + lane % half
    target = source * SUB + at
    buses = harm_count * SUB
    owner = jnp.where(iota((buses, convs), 0) == target, 1.0, 0.0).astype(BF16)
    inject[EDGE : EDGE + buses, :] = jnp.dot(owner, spectra, preferred_element_type=F32).astype(BF16)
    for ref, lane0, row0 in ((low_ref, half - 1, 0), (high_ref, 0, EDGE + buses)):
        edge = ref[...].astype(F32)
        total_r = jnp.zeros((SUB, 128), F32)
        total_i = jnp.zeros((SUB, 128), F32)
        for c in range(CONV):
            l = c * half + lane0
            bus = jnp.broadcast_to(edge[ROWS - 1 : ROWS, l : l + 1], (SUB, 128)).astype(jnp.int32)
            here = iota((SUB, 128), 0) == bus
            total_r += jnp.where(here, edge[2 * c : 2 * c + 1, :], 0.0)
            total_i += jnp.where(here, edge[2 * c + 1 : 2 * c + 2, :], 0.0)
        inject[row0 : row0 + EDGE, :] = jnp.concatenate([total_r, total_i], axis=1).astype(BF16)
    tail = 2 * EDGE + buses
    inject[tail:, :] = jnp.zeros((inject.shape[0] - tail, 256), BF16)
    volts = []
    for b in range(q_ref.shape[0]):
        acc = jnp.dot(q_ref[b], inject[b * TILE : b * TILE + WIN, :], preferred_element_type=F32)
        volt_r = (acc[:TILE, :128] - acc[TILE:, 128:]).astype(BF16)
        volt_i = (acc[:TILE, 128:] + acc[TILE:, :128]).astype(BF16)
        volt_ref[0, 0, b * TILE : b * TILE + TILE, :] = volt_r
        volt_ref[1, 0, b * TILE : b * TILE + TILE, :] = volt_i
        volts.append(jnp.concatenate([volt_r, volt_i], axis=1))
    picked = lax.dot_general(
        owner,
        jnp.concatenate(volts, axis=0),
        (((0,), (0,)), ((), ())),
        preferred_element_type=F32,
    )
    for h in range(2):
        for c in range(CONV):
            m = (h * CONV + c) * half
            for p in range(2):
                out[pl.ds(h * half * 2 * CONV + 2 * c + p, half, stride=2 * CONV), :] = picked[
                    m : m + half, p * 128 : p * 128 + 128
                ]
    near_ref[...] = out[...].astype(BF16)


def params():
    return pltpu.CompilerParams(vmem_limit_bytes=40 * 2**20)


def local(conv_volt, conv_power, conv_type, type_steep, conv_bus, admittance, link_offset):
    harm_count = lax.axis_size("harm")
    bus_count = lax.axis_size("bus")
    harm = lax.axis_index("harm")
    block = admittance.shape[3]
    snapshots = conv_volt.shape[3]
    up = [(i, i + 1) for i in range(bus_count - 1)]
    down = [(i + 1, i) for i in range(bus_count - 1)]
    half = harm_count // 2

    adm = admittance.reshape(8, block)
    edges = jnp.concatenate([adm, link_offset.astype(F32)], axis=0)
    low = lax.ppermute(edges[:, block - EDGE :], "bus", up)
    high = lax.ppermute(edges[:, :EDGE], "bus", down)
    padding = jnp.zeros((edges.shape[0], 128 - 2 * EDGE), F32)
    extended = jnp.concatenate([low, edges, high, padding], axis=1)
    adm_ext, off_ext = extended[:8], extended[8:].astype(jnp.int32)

    basis = jnp.asarray(make_basis())
    matches = conv_type[:, None] == jnp.arange(type_steep.shape[0], dtype=jnp.int32)[None, :]
    steepness = jnp.sum(jnp.where(matches, type_steep[None, :], 0.0), axis=1)
    volt_rows = conv_volt.reshape(2 * H, CONV, snapshots)
    waveform = jnp.einsum("kcs,kn->csn", volt_rows, basis, preferred_element_type=F32)
    current = (conv_power[:, :, None] * jnp.tanh(steepness[:, None, None] * waveform)).astype(BF16)
    spectra = jnp.einsum("csn,kn->kcs", current, basis, preferred_element_type=F32) * NT ** (-0.5)
    spectra = spectra.astype(BF16).reshape(2, H, CONV, snapshots)
    spectra = jnp.transpose(spectra, (1, 2, 0, 3)).reshape(H, 2 * CONV, snapshots)
    lane = jnp.arange(128, dtype=jnp.int32)
    mine = (lane[None, :] == jnp.arange(CONV)[:, None] * half + harm % half).astype(jnp.int32)
    index = jnp.sum(mine * (conv_bus % SUB)[:, None], axis=0).astype(BF16)
    index = jnp.broadcast_to(index[None, None, :], (H, 1, snapshots))
    blank = jnp.zeros((H, ROWS - 1 - 2 * CONV, snapshots), BF16)
    payload = jnp.concatenate([spectra, blank, index], axis=1).reshape(H, 3, 4, snapshots)
    got = lax.all_to_all(payload, "harm", split_axis=0, concat_axis=0, tiled=True)

    tiles = block // TILE
    q = pl.pallas_call(
        sweeps_kernel,
        out_shape=jax.ShapeDtypeStruct((tiles, 2 * TILE, WIN), BF16),
        compiler_params=params(),
        cost_estimate=pl.CostEstimate(flops=2 * tiles * 256 * 256 * 512, bytes_accessed=2**20, transcendentals=0),
        name="sweeps",
    )(adm_ext, off_ext)

    low_rows = lax.ppermute(got[harm_count - 1].reshape(ROWS, snapshots), "bus", up)
    high_rows = lax.ppermute(got[0].reshape(ROWS, snapshots), "bus", down)
    bus_volt, near = pl.pallas_call(
        network_kernel,
        out_shape=(
            jax.ShapeDtypeStruct((2, 1, block, snapshots), BF16),
            jax.ShapeDtypeStruct((harm_count * 2 * CONV, snapshots), BF16),
        ),
        scratch_shapes=[
            pltpu.VMEM((harm_count * ROWS, 128), F32),
            pltpu.VMEM((block + WIN - TILE, 256), BF16),
            pltpu.VMEM((harm_count * 2 * CONV, 128), F32),
        ],
        compiler_params=params(),
        cost_estimate=pl.CostEstimate(flops=2 * tiles * 256 * 256 * 256, bytes_accessed=2**20, transcendentals=0),
        name="network",
    )(got.reshape(harm_count * ROWS, snapshots), low_rows, high_rows, q)
    near = near.reshape(harm_count, 2 * CONV, snapshots)
    near = lax.all_to_all(near, "harm", split_axis=0, concat_axis=0, tiled=True)
    conv_next = jnp.transpose(near.reshape(H, CONV, 2, snapshots), (2, 0, 1, 3))
    return (bus_volt, conv_next)


def solution(mesh):
    in_specs = (
        P(None, None, ("bus", "harm"), None),
        P(("bus", "harm"), None),
        P(("bus", "harm")),
        P(),
        P(("bus", "harm")),
        P(None, None, "harm", "bus"),
        P(None, "bus"),
    )
    out_specs = (P(None, "harm", "bus", None), P(None, None, ("bus", "harm"), None))
    return jax.shard_map(local, mesh=mesh, in_specs=in_specs, out_specs=out_specs, check_vma=False)
```

time: 129 us -> 68.2 us (0.53)
  the two profiles are of different devices: /device:TPU:17 before, /device:TPU:25 now
where the time goes in v1:
time: 68.2 us; the launch traced here: 67.8 us
  starting transfers between devices  26.3 us (39%)
  blocking collectives  16.8 us (25%)
  waiting for transfers between devices  13 us (19%)
  Pallas kernels  3.98 us (6%)
  other arithmetic  3.39 us (5%)
  local copies, waits for them, and re-layouts  1.87 us (3%)
  matrix products  1.69 us (2%)
  between operations  0.8 us (1%)
    all_to_all x1, blocking collectives, local(): near = lax.all_to_all(near, 'harm', split_axis=0, concat_axis=0, tiled=True)  16.8 us
    all_to_all x1, starting transfers between devices, local(): lax.all_to_all(payload, 'harm', split_axis=0, concat_axis=0, tiled=True)  14.6 us
    all_to_all x1, waiting for transfers between devices, local(): lax.all_to_all(payload, 'harm', split_axis=0, concat_axis=0, tiled=True)  11.8 us
    ppermute x1, starting transfers between devices, local(): low = lax.ppermute(edges[:, block - EDGE:], 'bus', up)  4.42 us
    ppermute x1, starting transfers between devices, local(): lax.ppermute(got[harm_count - 1].reshape(ROWS, snapshots), 'bus', up)  3.19 us
    pallas_call x1, Pallas kernels, local(): pl.pallas_call(sweeps_kernel, out_shape=jax.ShapeDtypeStruct((tiles, 2 *...  2.36 us
    ppermute x1, starting transfers between devices, local(): high_rows = lax.ppermute(got[0].reshape(ROWS, snapshots), 'bus', down)  2.08 us
    ppermute x1, starting transfers between devices, local(): high = lax.ppermute(edges[:, :EDGE], 'bus', down)  2.07 us
  transfers between devices with their start and end apart: 5, of which 2 were waited for; matrix products, arithmetic and copies ran while one was open for 7% of the time, Pallas kernels for 3%

profile of v1, /device:TPU:25, one launch (start us, length us, event | category | flops | bytes accessed | tf_op | source)
XLA Modules:
  0.0 67.8 jit_solution(17099133103943011)
XLA Ops:
  0.6 0.0 copy-start
  0.6 0.8 %convert_element_type.27 = f32[3,1024]{1,0:T(4,128)S(1)} convert(s32[3,1024]{1,0:T(4,128)} %param.14) | non-fusion elementwise | flops 3072 | bytes 24576 | tf_op jit(solution)/shard_map/convert_element_type | solution.py:146
  1.4 0.8 %reduce = f32[2,4,1024]{2,1,0:T(4,128)S(1)} reduce(f32[2,4,1,1024]{3,2,1,0:T(1,128)} %param.13, f32[]{:T(128)} %constant.52), dimensions={2}, to_apply=%param.13.reduce_sub_computation | reduce | bytes 65540 | tf_op args[5]
  2.3 0.1 fusion.9
  2.3 2.1 %collective-permute-start.3 = (f32[11,16]{1,0:T(8,128)S(1)}, f32[11,16]{1,0:T(8,128)S(1)}, u32[]{:S(2)}, u32[]{:S(2)}) collective-permute-start(f32[11,16]{1,0:T(8,128)S(1)} %get-tuple-element.16), channel_id=1, source_target_pairs={{1,0},{2,1},{3,2},{4,3},{5,4},{6,5},{7,6},{9,8},{10,9},{11,10},{12... | collective-permute-start | bytes 2120 | tf_op jit(solution)/shard_map/ppermute | solution.py:148
  4.4 4.4 %collective-permute-start.2 = (f32[11,16]{1,0:T(8,128)S(1)}, f32[11,16]{1,0:T(8,128)S(1)}, u32[]{:S(2)}, u32[]{:S(2)}) collective-permute-start(f32[11,16]{1,0:T(8,128)S(1)} %get-tuple-element.17), channel_id=1, source_target_pairs={{0,1},{1,2},{2,3},{3,4},{4,5},{5,6},{6,7},{8,9},{9,10},{10,11},{11... | collective-permute-start | bytes 2120 | tf_op jit(solution)/shard_map/ppermute | solution.py:147
  8.9 0.7 and_select_fusion
  9.5 0.1 select_reduce_fusion
  9.6 0.9 %select_reduce_fusion.1 = f32[4]{0:T(128)S(1)} fusion(f32[8]{0:T(128)} %param.11, s32[4]{0:T(128)} %param.10), kind=kLoop, calls=%fused_computation.21 | loop fusion | flops 92 | bytes 64 | tf_op jit(solution)/shard_map/reduce_sum | solution.py:155
  10.5 0.1 pad.3.clone
  10.6 0.0 copy-done
  10.6 1.7 %fusion.3 = bf16[4,128,128]{1,2,0:T(8,128)(2,1)S(1)} fusion(bf16[128,1024,1]{0,1,2:T(8,128)(2,1)} %constant.51, f32[4,128]{1,0:T(4,128)} %param.9, f32[4]{0:T(128)S(1)} %select_reduce_fusion.1, bf16[128,4,128]{2,1,0:T(4,128)(2,1)S(1)} %bitcast.26), kind=kOutput, calls=%fused_computation.4 | convolution fusion | flops 270139392 | bytes 526352 | tf_op jit(solution)/shard_map/csn,kn->kcs/dot_general | solution.py:159
  12.3 0.1 pad_maximum_fusion
  12.3 0.8 %copy.29 = bf16[64,3,4,128]{3,2,1,0:T(4,128)(2,1)} copy(bf16[64,3,4,128]{3,0,2,1:T(8,128)(2,1)S(1)} %bitcast.29) | data formatting | bytes 393216 | tf_op jit(solution)/shard_map/reshape | solution.py:167
  13.2 14.6 %all-to-all-start = ((bf16[64,3,4,128]{3,2,1,0:T(4,128)(2,1)}), bf16[64,3,4,128]{3,2,1,0:T(4,128)(2,1)S(1)}, u32[]{:S(2)}, u32[]{:S(2)}) async-start(bf16[64,3,4,128]{3,2,1,0:T(4,128)(2,1)} %copy.29), calls=%async_computation | async-start | bytes 393216 | tf_op jit(solution)/shard_map/all_to_all | solution.py:168
  27.8 0.0 collective-permute-done.3
  27.8 0.0 collective-permute-done.2
  27.8 0.1 concatenate.11
  27.9 11.8 %all-to-all-done = bf16[64,3,4,128]{3,2,1,0:T(4,128)(2,1)S(1)} async-done(((bf16[64,3,4,128]{3,2,1,0:T(4,128)(2,1)}), bf16[64,3,4,128]{3,2,1,0:T(4,128)(2,1)S(1)}, u32[]{:S(2)}, u32[]{:S(2)}) %all-to-all-start) | async-done | bytes 196640 | tf_op jit(solution)/shard_map/all_to_all | solution.py:168
  39.8 3.2 %collective-permute-start = (bf16[12,128]{1,0:T(8,128)(2,1)S(1)}, bf16[12,128]{1,0:T(8,128)(2,1)S(1)}, u32[]{:S(2)}, u32[]{:S(2)}) collective-permute-start(bf16[12,128]{1,0:T(8,128)(2,1)S(1)} %reshape_squeeze.6), channel_id=1, source_target_pairs={{0,1},{1,2},{2,3},{3,4},{4,5},{5,6},{6,7},{8,9},{9,10},{10,11},{11... | collective-permute-start | bytes 9224 | tf_op jit(solution)/shard_map/ppermute | solution.py:179
  43.0 2.1 %collective-permute-start.1 = (bf16[12,128]{1,0:T(8,128)(2,1)S(1)}, bf16[12,128]{1,0:T(8,128)(2,1)S(1)}, u32[]{:S(2)}, u32[]{:S(2)}) collective-permute-start(bf16[12,128]{1,0:T(8,128)(2,1)S(1)} %reshape_squeeze.7), channel_id=1, source_target_pairs={{1,0},{2,1},{3,2},{4,3},{5,4},{6,5},{7,6},{9,8},{10,9},{11,10},{12... | collective-permute-start | bytes 9224 | tf_op jit(solution)/shard_map/ppermute | solution.py:180
  45.1 2.4 %sweeps.1.q_ref = bf16[8,256,256]{2,1,0:T(8,128)(2,1)S(1)} custom-call(f32[8,1152]{1,0:T(8,128)S(1)} %slice.30.adm_ref, s32[3,1152]{1,0:T(4,128)S(1)} %slice_convert_fusion.off_ref), custom_call_target="tpu_custom_call" | custom-call | flops 536870912 | bytes 1048576 | tf_op jit(solution)/shard_map/sweeps/pallas_call | solution.py:171
  47.5 0.0 collective-permute-done.low_ref
  47.5 1.1 %collective-permute-done.1.high_ref = bf16[12,128]{1,0:T(8,128)(2,1)S(1)} collective-permute-done((bf16[12,128]{1,0:T(8,128)(2,1)S(1)}, bf16[12,128]{1,0:T(8,128)(2,1)S(1)}, u32[]{:S(2)}, u32[]{:S(2)}) %collective-permute-start.1) | collective-permute-done | bytes 3104 | tf_op jit(solution)/shard_map/ppermute | solution.py:180
  48.6 1.6 %network.1 = (bf16[2,1,1024,128]{3,2,1,0:T(8,128)(2,1)}, bf16[512,128]{1,0:T(8,128)(2,1)S(1)}) custom-call(bf16[768,128]{1,0:T(8,128)(2,1)S(1)} %bitcast.27, bf16[12,128]{1,0:T(8,128)(2,1)S(1)} %collective-permute-done.low_ref, bf16[12,128]{1,0:T(8,128)(2,1)S(1)} %collective-permute-done.1.high_ref, bf16[8,256,256]{2,1,0:T(8,128)(2,1)S(1)} %sweeps.1.q_ref), custom_call_target="tpu_custom_call" | custom-call | flops 268435456 | bytes 1048576 | tf_op jit(solution)/shard_map/network/pallas_call | solution.py:181
  50.2 16.8 %all_to_all.10 = bf16[64,8,128]{2,1,0:T(8,128)(2,1)S(1)} all-to-all(bf16[64,8,128]{2,1,0:T(8,128)(2,1)S(1)} %bitcast.28), channel_id=1, replica_groups=mesh['harm'=64,'bus'=8] {'harm'}, dimensions={0} | all-to-all | bytes 262144 | tf_op jit(solution)/shard_map/all_to_all | solution.py:197
  67.0 0.8 %copy.31 = bf16[2,64,4,128]{3,2,1,0:T(4,128)(2,1)} copy(bf16[2,64,4,128]{3,1,0,2:T(8,128)(2,1)S(1)} %bitcast.30) | data formatting | bytes 262144
  (12 shorter events, 0.1 us)
Async XLA Ops:
  0.6 9.9 %copy-start = (bf16[2,64,4,128]{3,2,1,0:T(4,128)(2,1)S(1)}, bf16[2,64,4,128]{3,2,1,0:T(4,128)(2,1)}, u32[]{:S(2)}) copy-start(bf16[2,64,4,128]{3,2,1,0:T(4,128)(2,1)} %param.8) | copy-start | bytes 393220
  2.3 25.4 %collective-permute-start.3 = (f32[11,16]{1,0:T(8,128)S(1)}, f32[11,16]{1,0:T(8,128)S(1)}, u32[]{:S(2)}, u32[]{:S(2)}) collective-permute-start(f32[11,16]{1,0:T(8,128)S(1)} %get-tuple-element.16), channel_id=1, source_target_pairs={{1,0},{2,1},{3,2},{4,3},{5,4},{6,5},{7,6},{9,8},{10,9},{11,10},{12... | collective-permute-start | bytes 2120 | tf_op jit(solution)/shard_map/ppermute | solution.py:148
  4.4 23.4 %collective-permute-start.2 = (f32[11,16]{1,0:T(8,128)S(1)}, f32[11,16]{1,0:T(8,128)S(1)}, u32[]{:S(2)}, u32[]{:S(2)}) collective-permute-start(f32[11,16]{1,0:T(8,128)S(1)} %get-tuple-element.17), channel_id=1, source_target_pairs={{0,1},{1,2},{2,3},{3,4},{4,5},{5,6},{6,7},{8,9},{9,10},{10,11},{11... | collective-permute-start | bytes 2120 | tf_op jit(solution)/shard_map/ppermute | solution.py:147
  13.2 26.6 %all-to-all-start = ((bf16[64,3,4,128]{3,2,1,0:T(4,128)(2,1)}), bf16[64,3,4,128]{3,2,1,0:T(4,128)(2,1)S(1)}, u32[]{:S(2)}, u32[]{:S(2)}) async-start(bf16[64,3,4,128]{3,2,1,0:T(4,128)(2,1)} %copy.29), calls=%async_computation | async-start | bytes 393216 | tf_op jit(solution)/shard_map/all_to_all | solution.py:168
  39.8 7.7 %collective-permute-start = (bf16[12,128]{1,0:T(8,128)(2,1)S(1)}, bf16[12,128]{1,0:T(8,128)(2,1)S(1)}, u32[]{:S(2)}, u32[]{:S(2)}) collective-permute-start(bf16[12,128]{1,0:T(8,128)(2,1)S(1)} %reshape_squeeze.6), channel_id=1, source_target_pairs={{0,1},{1,2},{2,3},{3,4},{4,5},{5,6},{6,7},{8,9},{9,10},{10,11},{11... | collective-permute-start | bytes 9224 | tf_op jit(solution)/shard_map/ppermute | solution.py:179
  43.0 5.6 %collective-permute-start.1 = (bf16[12,128]{1,0:T(8,128)(2,1)S(1)}, bf16[12,128]{1,0:T(8,128)(2,1)S(1)}, u32[]{:S(2)}, u32[]{:S(2)}) collective-permute-start(bf16[12,128]{1,0:T(8,128)(2,1)S(1)} %reshape_squeeze.7), channel_id=1, source_target_pairs={{1,0},{2,1},{3,2},{4,3},{5,4},{6,5},{7,6},{9,8},{10,9},{11,10},{12... | collective-permute-start | bytes 9224 | tf_op jit(solution)/shard_map/ppermute | solution.py:180

commit v2 on v1

v2 whole, which is shorter than its diff:
```python
import math

import jax
import jax.numpy as jnp
import numpy as np
from jax import lax
from jax.experimental import pallas as pl
from jax.experimental.pallas import tpu as pltpu
from jax.sharding import PartitionSpec as P

H = 64
NT = 1024
REACH = 8
LINKS = 3
SUB = 16
CONV = 4
EDGE = 2 * REACH
TILE = 128
WIN = 256
ROWS = 12
COEF = 8
MARK = 11
HALF = 32
F32 = jnp.float32
BF16 = jnp.bfloat16
I32 = jnp.int32


def make_basis():
    turn = np.arange(1, H + 1)[:, None] * np.arange(NT)[None, :] % NT
    angle = turn * (2.0 * math.pi / NT)
    return np.concatenate([np.cos(angle), -np.sin(angle)], axis=0).astype(BF16)


def iota(shape, dim):
    return lax.broadcasted_iota(I32, shape, dim)


def product(ar, ai, br, bi):
    return ar * br - ai * bi, ar * bi + ai * br


def prepare_kernel(adm_ref, off_ref, coef_ref, first_ref, last_ref):
    inv_r, inv_i = adm_ref[0, 0], adm_ref[1, 0]
    steps = [product(inv_r, inv_i, adm_ref[0, k], adm_ref[1, k]) for k in range(1, 1 + LINKS)]
    blank = jnp.zeros((5, inv_r.shape[1]), F32)
    coefs = jnp.concatenate(
        [inv_r] + [s[0] for s in steps] + [inv_i] + [s[1] for s in steps] + [off_ref[...].astype(F32), blank], axis=0
    )
    coef_ref[...] = coefs
    first_ref[...] = coefs[:, :128]
    last_ref[...] = coefs[:, coefs.shape[1] - 128 :]


def convert_kernel(type_ref, steep_ref, bus_ref, harm_ref, volt_ref, power_ref, turned_ref, basis_ref, out_ref, volts):
    volts[...] = volt_ref[...].astype(F32)
    kinds = 2 * H
    volt = jnp.concatenate(
        [volts[pl.ds(c, kinds, stride=CONV), :] for c in range(CONV)], axis=1
    ).astype(BF16)
    steep = jnp.concatenate([jnp.full((1, 128), steep_ref[type_ref[c]], F32) for c in range(CONV)], axis=1)
    power = jnp.concatenate([power_ref[c : c + 1, :] for c in range(CONV)], axis=1)
    spectra = jnp.zeros((kinds, CONV * 128), F32)
    step = 256
    for n in range(0, NT, step):
        wave = jnp.dot(turned_ref[n : n + step, :], volt, preferred_element_type=F32)
        current = (power * jnp.tanh(steep * wave)).astype(BF16)
        spectra += jnp.dot(basis_ref[:, n : n + step], current, preferred_element_type=F32)
    spectra = spectra * NT ** (-0.5)
    for c in range(CONV):
        for p in range(2):
            out_ref[pl.ds(2 * c + p, H, stride=ROWS), :] = spectra[p * H : p * H + H, c * 128 : c * 128 + 128]
    lane = iota((H, 128), 1)
    column = lax.rem(harm_ref[0], HALF)
    mark = jnp.zeros((H, 128), F32)
    for c in range(CONV):
        mark += jnp.where(lane == c * HALF + column, lax.rem(bus_ref[c], SUB).astype(F32), 0.0)
    out_ref[pl.ds(MARK, H, stride=ROWS), :] = mark


def pack_kernel(rows_ref, coef_ref, low_ref, high_ref, out_ref, ext_ref, rows, groups):
    rows[...] = rows_ref[...]
    whole = jnp.concatenate([low_ref[...], coef_ref[...], high_ref[...]], axis=1)
    width = whole.shape[1]
    ext = pltpu.roll(whole, width - (128 - EDGE), 1)[:, : width - 128]
    ext_ref[...] = ext
    k, j = iota((8, 128), 0), iota((8, 128), 1) // SUB
    for v in range(ext.shape[1] // 128):
        x = ext[:8, v * 128 : v * 128 + 128]
        for s in (1, 2, 4):
            later = pltpu.roll(pltpu.roll(x, s, 0), 128 - SUB * s, 1)
            sooner = pltpu.roll(pltpu.roll(x, 8 - s, 0), SUB * s, 1)
            bk, bj = (k // s) % 2, (j // s) % 2
            x = jnp.where(bk == bj, x, jnp.where(bk == 1, later, sooner))
        groups[v * 8 : v * 8 + 8, :] = x
    for q in range(3):
        rows[pl.ds(COEF + q, H, stride=ROWS), :] = groups[q : q + H, :]
    out_ref[...] = rows[...].astype(BF16)


def sweeps_kernel(ext_ref, q_ref):
    rows = iota((WIN, WIN), 0)
    lanes = iota((1, WIN), 1)
    same = iota((TILE, WIN), 0) + EDGE == iota((TILE, WIN), 1)
    for b in range(q_ref.shape[0]):
        win = slice(b * TILE, b * TILE + WIN)
        turned_r = jnp.zeros((WIN, WIN), F32)
        turned_i = jnp.zeros((WIN, WIN), F32)
        for k in range(LINKS):
            here = rows == lanes + ext_ref[8 + k : 9 + k, win].astype(I32)
            turned_r += jnp.where(here, ext_ref[1 + k : 2 + k, win], 0.0)
            turned_i += jnp.where(here, ext_ref[5 + k : 6 + k, win], 0.0)
        step_r, step_i = turned_r.T, turned_i.T
        mid_r, mid_i = step_r[EDGE : EDGE + TILE], step_i[EDGE : EDGE + TILE]
        twice = jnp.dot(
            jnp.concatenate([mid_r, mid_i], axis=0).astype(BF16),
            jnp.concatenate([step_r, step_i], axis=1).astype(BF16),
            preferred_element_type=F32,
        )
        all_r = twice[:TILE, :WIN] - twice[TILE:, WIN:] + mid_r + jnp.where(same, 1.0, 0.0)
        all_i = twice[:TILE, WIN:] + twice[TILE:, :WIN] + mid_i
        q_r, q_i = product(all_r, all_i, ext_ref[0:1, win], ext_ref[4:5, win])
        q_ref[b, :TILE, :] = q_r.astype(BF16)
        q_ref[b, TILE:, :] = q_i.astype(BF16)


def network_kernel(got_ref, low_ref, high_ref, q_ref, volt_ref, rows, inject):
    rows[...] = got_ref[...].astype(F32)

    def part(p):
        return jnp.concatenate(
            [
                rows[pl.ds(h * HALF * ROWS + 2 * c + p, HALF, stride=ROWS), :]
                for h in range(2)
                for c in range(CONV)
            ],
            axis=0,
        )

    spectra = jnp.concatenate([part(0), part(1)], axis=1).astype(BF16)
    convs = H * CONV
    at = [
        jnp.sum(rows[pl.ds(h * HALF * ROWS + MARK, HALF, stride=ROWS), :], axis=0, keepdims=True)
        for h in range(2)
    ]
    at = jnp.concatenate(at, axis=1).astype(I32)
    lane = iota((1, convs), 1)
    source = lane // (CONV * HALF) * HALF + lane % HALF
    target = source * SUB + at
    buses = H * SUB
    owner = jnp.where(iota((buses, convs), 0) == target, 1.0, 0.0).astype(BF16)
    inject[EDGE : EDGE + buses, :] = jnp.dot(owner, spectra, preferred_element_type=F32).astype(BF16)
    for ref, lane0, row0 in ((low_ref, HALF - 1, 0), (high_ref, 0, EDGE + buses)):
        edge = ref[...].astype(F32)
        total_r = jnp.zeros((SUB, 128), F32)
        total_i = jnp.zeros((SUB, 128), F32)
        for c in range(CONV):
            at = c * HALF + lane0
            bus = jnp.broadcast_to(edge[MARK : MARK + 1, at : at + 1], (SUB, 128)).astype(I32)
            here = iota((SUB, 128), 0) == bus
            total_r += jnp.where(here, edge[2 * c : 2 * c + 1, :], 0.0)
            total_i += jnp.where(here, edge[2 * c + 1 : 2 * c + 2, :], 0.0)
        inject[row0 : row0 + EDGE, :] = jnp.concatenate([total_r, total_i], axis=1).astype(BF16)
    tail = 2 * EDGE + buses
    inject[tail:, :] = jnp.zeros((inject.shape[0] - tail, 256), BF16)
    for b in range(q_ref.shape[0]):
        acc = jnp.dot(q_ref[b], inject[b * TILE : b * TILE + WIN, :], preferred_element_type=F32)
        volt_ref[0, 0, b * TILE : b * TILE + TILE, :] = (acc[:TILE, :128] - acc[TILE:, 128:]).astype(BF16)
        volt_ref[1, 0, b * TILE : b * TILE + TILE, :] = (acc[:TILE, 128:] + acc[TILE:, :128]).astype(BF16)


def swapped(x):
    return pltpu.roll(x, 64, 1)


def packed_product(a, b, real):
    turned = swapped(b)
    return a * jnp.where(real, b, turned) + swapped(a) * jnp.where(real, -turned, b)


def near_kernel(bus_ref, harm_ref, got_ref, mine_ref, prev_ref, next_ref, ext_ref, out_ref, coefs, rows, out):
    harm = harm_ref[0]
    coefs[...] = got_ref[...].astype(F32)
    size = mine_ref.shape[0]
    for q, ref in enumerate((prev_ref, mine_ref, next_ref)):
        rows[q * size : q * size + size, :] = ref[...].astype(F32)

    shape = (8, 128)
    lane = iota(shape, 1)
    real = lane < 64
    spot = lane % 64
    conv, path = spot // 16, spot % 16
    base = pl.multiple_of(harm * SUB // 128 * 128, 128)
    offs = ext_ref[8:16, pl.ds(base, 256)]
    offs = pltpu.roll(offs, 256 - lax.rem(harm * SUB, 128), 1)[:, :128].astype(I32)
    offs = [jnp.broadcast_to(offs[k : k + 1, :], shape) for k in range(LINKS)]

    def hop(bus, line):
        total = bus
        for k in range(LINKS):
            total += jnp.where(line == k + 1, jnp.take_along_axis(offs[k], bus, axis=1), 0)
        return total

    def place(bus, line, used):
        at = bus // SUB * 128 + line * SUB + bus % SUB + jnp.where(real, 0, 64)
        return jnp.where(used, at, -1)[:1]

    bus0 = jnp.full(shape, SUB, I32)
    for c in range(CONV):
        bus0 += jnp.where(conv == c, lax.rem(bus_ref[c], SUB), 0)
    two = path >= 1 + LINKS
    line1 = jnp.where(two, 1 + (path - 1 - LINKS) // LINKS, path)
    line2 = jnp.where(two, 1 + (path - 1 - LINKS) % LINKS, 0)
    valid = path < 1 + LINKS + LINKS * LINKS
    line1 = jnp.where(valid, line1, 0)
    line2 = jnp.where(valid, line2, 0)
    bus1 = hop(bus0, line1)
    bus2 = hop(bus1, line2)
    places = jnp.concatenate(
        [place(bus0, line1, valid & (path >= 1)), place(bus1, line2, valid & two), place(bus2, 0, valid)], axis=1
    )
    pick = jnp.where(iota((3 * 128, 3 * 128), 0) == places, 1.0, 0.0).astype(BF16)
    window = jnp.concatenate(
        [coefs[pl.ds(COEF + q, H, stride=ROWS), :] for q in range(3)], axis=1
    ).astype(BF16)
    found = jnp.dot(window, pick, preferred_element_type=F32)
    real, path = real[:1], path[:1]
    first = found[:, :128] + jnp.where(real & (path == 0), 1.0, 0.0)
    second = found[:, 128:256] + jnp.where(real & (path <= LINKS), 1.0, 0.0)
    weight = packed_product(packed_product(first, second, real), found[:, 256:], real)

    many = (128, 128)
    row = iota(many, 0)
    other = row % 64 % (3 * CONV)
    bus_of = jnp.zeros(many, I32)
    for q in range(3):
        marks = rows[q * size + MARK : q * size + MARK + 1, :]
        column = lax.rem(harm + q - 1 + HALF, HALF)
        for c in range(CONV):
            bus = jnp.sum(jnp.where(iota((1, 128), 1) == c * HALF + column, marks, 0.0), axis=1, keepdims=True)
            bus = jnp.broadcast_to(bus.astype(I32), many) + q * SUB
            bus_of = jnp.where(other == q * CONV + c, bus, bus_of)
    wide = iota(many, 1)
    match = (row // 64 == wide // 64) & (row % 64 // (3 * CONV) == wide % 64 // 16) & (bus_of == bus2[:1])
    match = jnp.where(match, 1.0, 0.0).astype(BF16)
    high = weight.astype(BF16)
    rest = (weight - high.astype(F32)).astype(BF16)
    dims = (((1,), (1,)), ((), ()))
    table = lax.dot_general(high, match, dims, preferred_element_type=F32)
    table += lax.dot_general(rest, match, dims, preferred_element_type=F32)

    total = [[jnp.zeros((H, 128), F32) for _ in range(2)] for _ in range(CONV)]
    for q in range(3):
        for o in range(CONV):
            spec_r = rows[pl.ds(q * size + 2 * o, H, stride=ROWS), :]
            spec_i = rows[pl.ds(q * size + 2 * o + 1, H, stride=ROWS), :]
            for c in range(CONV):
                at = c * 3 * CONV + q * CONV + o
                add_r, add_i = product(table[:, at : at + 1], table[:, 64 + at : 65 + at], spec_r, spec_i)
                total[c][0] += add_r
                total[c][1] += add_i
    for c in range(CONV):
        for p in range(2):
            out[pl.ds(p * H * CONV + c, H, stride=CONV), :] = total[c][p]
    out_ref[...] = out[...].astype(BF16)


SMEM = pl.BlockSpec(memory_space=pltpu.SMEM)
VMEM = pl.BlockSpec(memory_space=pltpu.VMEM)


def call(kernel, name, out_shape, in_specs, scratch=(), cost=(0, 0, 0)):
    flops, moved, hard = cost
    return pl.pallas_call(
        kernel,
        out_shape=out_shape,
        in_specs=in_specs,
        out_specs=jax.tree.map(lambda _: VMEM, out_shape),
        scratch_shapes=list(scratch),
        compiler_params=pltpu.CompilerParams(vmem_limit_bytes=40 * 2**20),
        cost_estimate=pl.CostEstimate(flops=flops, bytes_accessed=moved, transcendentals=hard),
        name=name,
    )


def local(conv_volt, conv_power, conv_type, type_steep, conv_bus, admittance, link_offset):
    harm_count = lax.axis_size("harm")
    bus_count = lax.axis_size("bus")
    block = admittance.shape[3]
    snapshots = conv_volt.shape[3]
    tiles = block // TILE
    size = harm_count * ROWS
    up = [(i, i + 1) for i in range(bus_count - 1)]
    down = [(i + 1, i) for i in range(bus_count - 1)]
    along = harm_count * bus_count
    harm = lax.axis_index("harm").astype(I32).reshape(1)
    S = jax.ShapeDtypeStruct

    coef, first, last = call(
        prepare_kernel,
        "prepare",
        (S((16, block), F32), S((16, 128), F32), S((16, 128), F32)),
        [VMEM] * 2,
    )(admittance.reshape(2, 4, 1, block), link_offset)
    low = lax.ppermute(last, "bus", up)
    high = lax.ppermute(first, "bus", down)

    basis = make_basis()
    rows = call(
        convert_kernel,
        "convert",
        S((size, 128), F32),
        [SMEM] * 4 + [VMEM] * 4,
        [pltpu.VMEM((2 * H * CONV, 128), F32)],
        (2 * 2 * 128 * 1024 * 512, 2**20, 2**19),
    )(
        conv_type,
        type_steep,
        conv_bus,
        harm,
        conv_volt.reshape(2 * H * CONV, snapshots),
        conv_power,
        jnp.asarray(np.ascontiguousarray(basis.T)),
        jnp.asarray(basis),
    )
    payload, ext = call(
        pack_kernel,
        "pack",
        (S((size, 128), BF16), S((16, block + 128), F32)),
        [VMEM] * 4,
        [pltpu.VMEM((size, 128), F32), pltpu.VMEM((block // SUB + 8, 128), F32)],
    )(rows, coef, low, high)

    four = (harm_count, ROWS // 4, 4, snapshots)
    got = lax.all_to_all(payload.reshape(four), "harm", split_axis=0, concat_axis=0, tiled=True)

    q = call(
        sweeps_kernel,
        "sweeps",
        S((tiles, 2 * TILE, WIN), BF16),
        [VMEM],
        cost=(2 * tiles * 256 * 256 * 512, 2**20, 0),
    )(ext)
    sideways = [[(i, i + 1) for i in range(along - 1)], [(i + 1, i) for i in range(along - 1)]]
    prev = turn(payload, sideways[0], harm_count)
    following = turn(payload, sideways[1], harm_count)

    low_rows = lax.ppermute(got[harm_count - 1].reshape(ROWS, snapshots), "bus", up)
    high_rows = lax.ppermute(got[0].reshape(ROWS, snapshots), "bus", down)
    got = got.reshape(size, snapshots)
    near = call(
        near_kernel,
        "near",
        S((2 * H * CONV, snapshots), BF16),
        [SMEM] * 2 + [VMEM] * 5,
        [
            pltpu.VMEM((size, 128), F32),
            pltpu.VMEM((3 * size, 128), F32),
            pltpu.VMEM((2 * H * CONV, 128), F32),
        ],
        (2 * 10**7, 2**20, 0),
    )(conv_bus, harm, got, payload, prev, following, ext)
    bus_volt = call(
        network_kernel,
        "network",
        S((2, 1, block, snapshots), BF16),
        [VMEM] * 4,
        [pltpu.VMEM((size, 128), F32), pltpu.VMEM((block + WIN - TILE, 256), BF16)],
        (2 * tiles * 256 * 256 * 256, 2**20, 0),
    )(got, low_rows, high_rows, q)
    return (bus_volt, near.reshape(2, H, CONV, snapshots))


def turn(array, pairs, harm_count):
    bus_count = lax.axis_size("bus")
    number = lambda r: r % harm_count * bus_count + r // harm_count
    return lax.ppermute(array, ("harm", "bus"), [(number(s), number(d)) for s, d in pairs])


def solution(mesh):
    in_specs = (
        P(None, None, ("bus", "harm"), None),
        P(("bus", "harm"), None),
        P(("bus", "harm")),
        P(),
        P(("bus", "harm")),
        P(None, None, "harm", "bus"),
        P(None, "bus"),
    )
    out_specs = (P(None, "harm", "bus", None), P(None, None, ("bus", "harm"), None))
    return jax.shard_map(local, mesh=mesh, in_specs=in_specs, out_specs=out_specs, check_vma=False)
```

time: 68.2 us -> 56.2 us (0.82)
  the two profiles are of different devices: /device:TPU:25 before, /device:TPU:32 now
where the time goes in v2:
time: 56.2 us; the launch traced here: 55.6 us
  starting transfers between devices  36.1 us (64%)
  Pallas kernels  10.1 us (18%)
  local copies, waits for them, and re-layouts  4.98 us (9%)
  waiting for transfers between devices  3.71 us (7%)
  between operations  0.79 us (1%)
    all_to_all x1, starting transfers between devices, local(): lax.all_to_all(payload.reshape(four), 'harm', split_axis=0, concat_axis=0...  13.8 us
    ppermute x2, starting transfers between devices, turn(): lax.ppermute(array, ('harm', 'bus'), [(number(s), number(d)) for s, d in...  8.23 us
    ppermute x1, starting transfers between devices, local(): high_rows = lax.ppermute(got[0].reshape(ROWS, snapshots), 'bus', down)  5.13 us
    unnamed x18, local copies, waits for them, and re-layouts  4.94 us
    ppermute x1, starting transfers between devices, local(): high = lax.ppermute(first, 'bus', down)  4.47 us
    all_to_all x1, waiting for transfers between devices, local(): lax.all_to_all(payload.reshape(four), 'harm', split_axis=0, concat_axis=0...  3.7 us
    pallas_call x1, Pallas kernels, local(): call(near_kernel, 'near', S((2 * H * CONV, snapshots), BF16), [SMEM] * 2...  3.54 us
    ppermute x1, starting transfers between devices, local(): low = lax.ppermute(last, 'bus', up)  2.59 us
  transfers between devices with their start and end apart: 7, of which 1 were waited for; matrix products, arithmetic and copies ran while one was open for 0% of the time, Pallas kernels for 13%

profile of v2, /device:TPU:32, one launch (start us, length us, event | category | flops | bytes accessed | tf_op | source)
XLA Modules:
  0.0 55.6 jit_solution(3105152126647792155)
XLA Ops:
  0.6 0.0 copy-start.3
  0.6 0.7 %copy-done.3 = f32[2,4,1,1024]{3,2,1,0:T(1,128)S(1)} copy-done((f32[2,4,1,1024]{3,2,1,0:T(1,128)S(1)}, f32[2,4,1,1024]{3,2,1,0:T(1,128)}, u32[]{:S(2)}) %copy-start.3) | copy-done | bytes 32792
  1.4 0.0 copy-start.4
  1.4 0.7 %copy-done.4 = s32[3,1024]{1,0:T(4,128)S(1)} copy-done((s32[3,1024]{1,0:T(4,128)S(1)}, s32[3,1024]{1,0:T(4,128)}, u32[]{:S(2)}) %copy-start.4) | copy-done | bytes 12312
  2.1 2.6 %collective-permute-start = (f32[16,128]{1,0:T(8,128)S(1)}, f32[16,128]{1,0:T(8,128)S(1)}, u32[]{:S(2)}, u32[]{:S(2)}) collective-permute-start(f32[16,128]{1,0:T(8,128)S(1)} %get-tuple-element.8), channel_id=1, source_target_pairs={{0,1},{1,2},{2,3},{3,4},{4,5},{5,6},{6,7},{8,9},{9,10},{10,11},{11... | collective-permute-start | bytes 24584 | tf_op jit(solution)/shard_map/ppermute | solution.py:305
  4.7 4.5 %collective-permute-start.1 = (f32[16,128]{1,0:T(8,128)S(1)}, f32[16,128]{1,0:T(8,128)S(1)}, u32[]{:S(2)}, u32[]{:S(2)}) collective-permute-start(f32[16,128]{1,0:T(8,128)S(1)} %get-tuple-element.9), channel_id=1, source_target_pairs={{1,0},{2,1},{3,2},{4,3},{5,4},{6,5},{7,6},{9,8},{10,9},{11,10},{12... | collective-permute-start | bytes 24584 | tf_op jit(solution)/shard_map/ppermute | solution.py:306
  9.2 0.0 copy-start.5
  9.2 0.0 copy-start.6
  9.2 0.0 copy-start.7
  9.2 0.0 copy-start.8
  9.3 0.6 %copy-done.5 = f32[4,128]{1,0:T(4,128)S(1)} copy-done((f32[4,128]{1,0:T(4,128)S(1)}, f32[4,128]{1,0:T(4,128)}, u32[]{:S(2)}) %copy-start.5) | copy-done | bytes 2072
  9.9 0.0 copy-done.6
  9.9 0.0 copy-done.7
  9.9 0.0 copy-done.8
  9.9 0.0 copy-start
  9.9 0.9 %copy-done = bf16[128,1024]{1,0:T(8,128)(2,1)S(1)} copy-done((bf16[128,1024]{1,0:T(8,128)(2,1)S(1)}, bf16[128,1024]{1,0:T(8,128)(2,1)}, u32[]{:S(2)}) %copy-start) | copy-done | bytes 262168
  10.9 0.0 copy-start.1
  10.9 0.9 %copy-done.1 = bf16[1024,128]{1,0:T(8,128)(2,1)S(1)} copy-done((bf16[1024,128]{1,0:T(8,128)(2,1)S(1)}, bf16[1024,128]{1,0:T(8,128)(2,1)}, u32[]{:S(2)}) %copy-start.1) | copy-done | bytes 262168
  11.8 0.0 copy-start.2
  11.8 0.9 %copy-done.2 = bf16[2,64,4,128]{3,2,1,0:T(4,128)(2,1)S(1)} copy-done((bf16[2,64,4,128]{3,2,1,0:T(4,128)(2,1)S(1)}, bf16[2,64,4,128]{3,2,1,0:T(4,128)(2,1)}, u32[]{:S(2)}) %copy-start.2) | copy-done | bytes 131096
  12.7 1.5 %convert.1.rows_ref = f32[768,128]{1,0:T(8,128)S(1)} custom-call(s32[4]{0:T(128)S(1)} %copy-done.7, f32[8]{0:T(128)S(1)} %copy-done.8, s32[4]{0:T(128)S(1)} %copy-done.6, s32[1]{0:T(128)} %bitcast.harm_ref, bf16[512,128]{1,0:T(8,128)(2,1)S(1)} %bitcast.7, f32[4,128]{1,0:T(4,128)S(1)} %copy-done.5, bf16[1024,128]{1,0:T(8,128)(2,1)S(1)} %copy-done.1, ...), custom_call_target="tpu_custom_call" | custom-call | flops 268435456 | bytes 1048576 | tf_op jit(solution)/shard_map/convert/pallas_call | solution.py:309
  14.3 0.0 collective-permute-done.low_ref
  14.3 0.0 collective-permute-done.1.high_ref
  14.3 1.0 %pack.1 = (bf16[768,128]{1,0:T(8,128)(2,1)}, f32[16,1152]{1,0:T(8,128)S(1)}) custom-call(f32[768,128]{1,0:T(8,128)S(1)} %convert.1.rows_ref, f32[16,1024]{1,0:T(8,128)S(1)} %get-tuple-element.7.coef_ref, f32[16,128]{1,0:T(8,128)S(1)} %collective-permute-done.low_ref, f32[16,128]{1,0:T(8,128)S(1)} %collective-permute-done.1.high_ref), custom_call_target="tpu_custom_call" | custom-call | tf_op jit(solution)/shard_map/pack/pallas_call | solution.py:326
  15.3 13.8 %all-to-all-start = ((bf16[64,3,4,128]{3,2,1,0:T(4,128)(2,1)}), bf16[64,3,4,128]{3,2,1,0:T(4,128)(2,1)S(1)}, u32[]{:S(2)}, u32[]{:S(2)}) async-start(bf16[64,3,4,128]{3,2,1,0:T(4,128)(2,1)} %bitcast.2), calls=%async_computation | async-start | bytes 393216 | tf_op jit(solution)/shard_map/all_to_all | solution.py:335
  29.1 6.3 %collective-permute-start.5 = (bf16[768,128]{1,0:T(8,128)(2,1)}, bf16[768,128]{1,0:T(8,128)(2,1)S(1)}, u32[]{:S(2)}, u32[]{:S(2)}) collective-permute-start(bf16[768,128]{1,0:T(8,128)(2,1)} %get-tuple-element.10.mine_ref), channel_id=1, source_target_pairs={{8,0},{16,8},{24,16},{32,24},{40,32},{48,40},{56,48},{64,56},{72,6... | collective-permute-start | bytes 589832 | tf_op jit(solution)/shard_map/ppermute | solution.py:377
  35.4 1.9 %collective-permute-start.4 = (bf16[768,128]{1,0:T(8,128)(2,1)}, bf16[768,128]{1,0:T(8,128)(2,1)S(1)}, u32[]{:S(2)}, u32[]{:S(2)}) collective-permute-start(bf16[768,128]{1,0:T(8,128)(2,1)} %get-tuple-element.10.mine_ref), channel_id=1, source_target_pairs={{0,8},{8,16},{16,24},{24,32},{32,40},{40,48},{48,56},{56,64},{64,7... | collective-permute-start | bytes 589832 | tf_op jit(solution)/shard_map/ppermute | solution.py:377
  37.3 3.7 %all-to-all-done = bf16[64,3,4,128]{3,2,1,0:T(4,128)(2,1)S(1)} async-done(((bf16[64,3,4,128]{3,2,1,0:T(4,128)(2,1)}), bf16[64,3,4,128]{3,2,1,0:T(4,128)(2,1)S(1)}, u32[]{:S(2)}, u32[]{:S(2)}) %all-to-all-start) | async-done | bytes 196640 | tf_op jit(solution)/shard_map/all_to_all | solution.py:335
  41.1 1.9 %collective-permute-start.2 = (bf16[12,128]{1,0:T(8,128)(2,1)S(1)}, bf16[12,128]{1,0:T(8,128)(2,1)S(1)}, u32[]{:S(2)}, u32[]{:S(2)}) collective-permute-start(bf16[12,128]{1,0:T(8,128)(2,1)S(1)} %reshape_squeeze.6), channel_id=1, source_target_pairs={{0,1},{1,2},{2,3},{3,4},{4,5},{5,6},{6,7},{8,9},{9,10},{10,11},{11... | collective-permute-start | bytes 9224 | tf_op jit(solution)/shard_map/ppermute | solution.py:348
  43.0 5.1 %collective-permute-start.3 = (bf16[12,128]{1,0:T(8,128)(2,1)S(1)}, bf16[12,128]{1,0:T(8,128)(2,1)S(1)}, u32[]{:S(2)}, u32[]{:S(2)}) collective-permute-start(bf16[12,128]{1,0:T(8,128)(2,1)S(1)} %reshape_squeeze.7), channel_id=1, source_target_pairs={{1,0},{2,1},{3,2},{4,3},{5,4},{6,5},{7,6},{9,8},{10,9},{11,10},{12... | collective-permute-start | bytes 9224 | tf_op jit(solution)/shard_map/ppermute | solution.py:349
  48.1 2.4 %sweeps.1.q_ref = bf16[8,256,256]{2,1,0:T(8,128)(2,1)S(1)} custom-call(f32[16,1152]{1,0:T(8,128)S(1)} %get-tuple-element.11.ext_ref), custom_call_target="tpu_custom_call" | custom-call | flops 536870912 | bytes 1048576 | tf_op jit(solution)/shard_map/sweeps/pallas_call | solution.py:337
  50.5 0.0 collective-permute-done.5.next_ref
  50.5 0.0 collective-permute-done.4.prev_ref
  50.5 3.5 %near.1 = bf16[512,128]{1,0:T(8,128)(2,1)} custom-call(s32[4]{0:T(128)S(1)} %copy-done.6, s32[1]{0:T(128)} %bitcast.harm_ref, bf16[768,128]{1,0:T(8,128)(2,1)S(1)} %bitcast.5, bf16[768,128]{1,0:T(8,128)(2,1)} %get-tuple-element.10.mine_ref, bf16[768,128]{1,0:T(8,128)(2,1)S(1)} %collective-permute-done.4.prev_ref, ...), custom_call_target="tpu_custom_call" | custom-call | flops 20000000 | bytes 1048576 | tf_op jit(solution)/shard_map/near/pallas_call | solution.py:351
  54.0 0.0 collective-permute-done.2.low_ref
  54.0 0.0 collective-permute-done.3.high_ref
  54.0 1.6 %network.1 = bf16[2,1,1024,128]{3,2,1,0:T(8,128)(2,1)} custom-call(bf16[768,128]{1,0:T(8,128)(2,1)S(1)} %bitcast.6, bf16[12,128]{1,0:T(8,128)(2,1)S(1)} %collective-permute-done.2.low_ref, bf16[12,128]{1,0:T(8,128)(2,1)S(1)} %collective-permute-done.3.high_ref, bf16[8,256,256]{2,1,0:T(8,128)(2,1)S(1)} %sweeps.1.q_ref), custom_call_target="tpu_custom_call" | custom-call | flops 268435456 | bytes 1048576 | tf_op jit(solution)/shard_map/network/pallas_call | solution.py:363
  (4 shorter events, 0.1 us)
Async XLA Ops:
  0.6 0.8 %copy-start.3 = (f32[2,4,1,1024]{3,2,1,0:T(1,128)S(1)}, f32[2,4,1,1024]{3,2,1,0:T(1,128)}, u32[]{:S(2)}) copy-start(f32[2,4,1,1024]{3,2,1,0:T(1,128)} %adm_ref.1) | copy-start | bytes 98308
  1.4 0.7 %copy-start.4 = (s32[3,1024]{1,0:T(4,128)S(1)}, s32[3,1024]{1,0:T(4,128)}, u32[]{:S(2)}) copy-start(s32[3,1024]{1,0:T(4,128)} %off_ref.1) | copy-start | bytes 36868
  2.1 12.1 %collective-permute-start = (f32[16,128]{1,0:T(8,128)S(1)}, f32[16,128]{1,0:T(8,128)S(1)}, u32[]{:S(2)}, u32[]{:S(2)}) collective-permute-start(f32[16,128]{1,0:T(8,128)S(1)} %get-tuple-element.8), channel_id=1, source_target_pairs={{0,1},{1,2},{2,3},{3,4},{4,5},{5,6},{6,7},{8,9},{9,10},{10,11},{11... | collective-permute-start | bytes 24584 | tf_op jit(solution)/shard_map/ppermute | solution.py:305
  4.7 9.6 %collective-permute-start.1 = (f32[16,128]{1,0:T(8,128)S(1)}, f32[16,128]{1,0:T(8,128)S(1)}, u32[]{:S(2)}, u32[]{:S(2)}) collective-permute-start(f32[16,128]{1,0:T(8,128)S(1)} %get-tuple-element.9), channel_id=1, source_target_pairs={{1,0},{2,1},{3,2},{4,3},{5,4},{6,5},{7,6},{9,8},{10,9},{11,10},{12... | collective-permute-start | bytes 24584 | tf_op jit(solution)/shard_map/ppermute | solution.py:306
  9.2 0.7 %copy-start.5 = (f32[4,128]{1,0:T(4,128)S(1)}, f32[4,128]{1,0:T(4,128)}, u32[]{:S(2)}) copy-start(f32[4,128]{1,0:T(4,128)} %power_ref.1) | copy-start | bytes 6148
  9.2 0.7 %copy-start.6 = (s32[4]{0:T(128)S(1)}, s32[4]{0:T(128)}, u32[]{:S(2)}) copy-start(s32[4]{0:T(128)} %bus_ref.3) | copy-start | bytes 52
  9.2 0.7 %copy-start.7 = (s32[4]{0:T(128)S(1)}, s32[4]{0:T(128)}, u32[]{:S(2)}) copy-start(s32[4]{0:T(128)} %type_ref.1) | copy-start | bytes 52
  9.2 0.7 %copy-start.8 = (f32[8]{0:T(128)S(1)}, f32[8]{0:T(128)}, u32[]{:S(2)}) copy-start(f32[8]{0:T(128)} %steep_ref.1) | copy-start | bytes 100
  9.9 0.9 %copy-start = (bf16[128,1024]{1,0:T(8,128)(2,1)S(1)}, bf16[128,1024]{1,0:T(8,128)(2,1)}, u32[]{:S(2)}) copy-start(bf16[128,1024]{1,0:T(8,128)(2,1)} %constant.11.clone.basis_ref) | copy-start | bytes 786436
  10.9 0.9 %copy-start.1 = (bf16[1024,128]{1,0:T(8,128)(2,1)S(1)}, bf16[1024,128]{1,0:T(8,128)(2,1)}, u32[]{:S(2)}) copy-start(bf16[1024,128]{1,0:T(8,128)(2,1)} %constant.10.clone.turned_ref) | copy-start | bytes 786436
  11.8 0.9 %copy-start.2 = (bf16[2,64,4,128]{3,2,1,0:T(4,128)(2,1)S(1)}, bf16[2,64,4,128]{3,2,1,0:T(4,128)(2,1)}, u32[]{:S(2)}) copy-start(bf16[2,64,4,128]{3,2,1,0:T(4,128)(2,1)} %param.9) | copy-start | bytes 393220
  15.3 25.7 %all-to-all-start = ((bf16[64,3,4,128]{3,2,1,0:T(4,128)(2,1)}), bf16[64,3,4,128]{3,2,1,0:T(4,128)(2,1)S(1)}, u32[]{:S(2)}, u32[]{:S(2)}) async-start(bf16[64,3,4,128]{3,2,1,0:T(4,128)(2,1)} %bitcast.2), calls=%async_computation | async-start | bytes 393216 | tf_op jit(solution)/shard_map/all_to_all | solution.py:335
  29.1 21.4 %collective-permute-start.5 = (bf16[768,128]{1,0:T(8,128)(2,1)}, bf16[768,128]{1,0:T(8,128)(2,1)S(1)}, u32[]{:S(2)}, u32[]{:S(2)}) collective-permute-start(bf16[768,128]{1,0:T(8,128)(2,1)} %get-tuple-element.10.mine_ref), channel_id=1, source_target_pairs={{8,0},{16,8},{24,16},{32,24},{40,32},{48,40},{56,48},{64,56},{72,6... | collective-permute-start | bytes 589832 | tf_op jit(solution)/shard_map/ppermute | solution.py:377
  35.4 15.1 %collective-permute-start.4 = (bf16[768,128]{1,0:T(8,128)(2,1)}, bf16[768,128]{1,0:T(8,128)(2,1)S(1)}, u32[]{:S(2)}, u32[]{:S(2)}) collective-permute-start(bf16[768,128]{1,0:T(8,128)(2,1)} %get-tuple-element.10.mine_ref), channel_id=1, source_target_pairs={{0,8},{8,16},{16,24},{24,32},{32,40},{40,48},{48,56},{56,64},{64,7... | collective-permute-start | bytes 589832 | tf_op jit(solution)/shard_map/ppermute | solution.py:377
  41.1 13.0 %collective-permute-start.2 = (bf16[12,128]{1,0:T(8,128)(2,1)S(1)}, bf16[12,128]{1,0:T(8,128)(2,1)S(1)}, u32[]{:S(2)}, u32[]{:S(2)}) collective-permute-start(bf16[12,128]{1,0:T(8,128)(2,1)S(1)} %reshape_squeeze.6), channel_id=1, source_target_pairs={{0,1},{1,2},{2,3},{3,4},{4,5},{5,6},{6,7},{8,9},{9,10},{10,11},{11... | collective-permute-start | bytes 9224 | tf_op jit(solution)/shard_map/ppermute | solution.py:348
  43.0 11.1 %collective-permute-start.3 = (bf16[12,128]{1,0:T(8,128)(2,1)S(1)}, bf16[12,128]{1,0:T(8,128)(2,1)S(1)}, u32[]{:S(2)}, u32[]{:S(2)}) collective-permute-start(bf16[12,128]{1,0:T(8,128)(2,1)S(1)} %reshape_squeeze.7), channel_id=1, source_target_pairs={{1,0},{2,1},{3,2},{4,3},{5,4},{6,5},{7,6},{9,8},{10,9},{11,10},{12... | collective-permute-start | bytes 9224 | tf_op jit(solution)/shard_map/ppermute | solution.py:349

commit v3 on v2

v3 whole, which is shorter than its diff:
```python
import math

import jax
import jax.numpy as jnp
import numpy as np
from jax import lax
from jax.experimental import pallas as pl
from jax.experimental.pallas import tpu as pltpu
from jax.sharding import PartitionSpec as P

H = 64
NT = 1024
REACH = 8
LINKS = 3
SUB = 16
CONV = 4
EDGE = 2 * REACH
TILE = 128
WIN = 256
ROWS = 12
COEF = 8
MARK = 11
EXTRA = 11
HALF = 32
F32 = jnp.float32
BF16 = jnp.bfloat16
I32 = jnp.int32


def make_basis():
    turn = np.arange(1, H + 1)[:, None] * np.arange(NT)[None, :] % NT
    angle = turn * (2.0 * math.pi / NT)
    return np.concatenate([np.cos(angle), -np.sin(angle)], axis=0).astype(BF16)


def iota(shape, dim):
    return lax.broadcasted_iota(I32, shape, dim)


def product(ar, ai, br, bi):
    return ar * br - ai * bi, ar * bi + ai * br


def grouped(x):
    k, j = iota((8, 128), 0), iota((8, 128), 1) // SUB
    for s in (1, 2, 4):
        later = pltpu.roll(pltpu.roll(x, s, 0), 128 - SUB * s, 1)
        sooner = pltpu.roll(pltpu.roll(x, 8 - s, 0), SUB * s, 1)
        bk, bj = (k // s) % 2, (j // s) % 2
        x = jnp.where(bk == bj, x, jnp.where(bk == 1, later, sooner))
    return x


def even(axis):
    return lax.rem(lax.axis_index(axis), 2) == 0


def prepare_kernel(
    adm_hbm, off_hbm, type_hbm, steep_hbm, bus_hbm, power_hbm, volt_hbm, turned_hbm, basis_hbm,
    coef_ref, a_ref, b_ref, aux_ref, group_ref, volt_ref, turned_ref, basis_ref,
    adm, off, kind, steep, bus, power, sems,
):
    pairs = [
        (adm_hbm, adm), (off_hbm, off), (type_hbm, kind), (steep_hbm, steep), (bus_hbm, bus), (power_hbm, power),
        (volt_hbm, volt_ref), (turned_hbm, turned_ref), (basis_hbm, basis_ref),
    ]
    copies = [pltpu.make_async_copy(src, dst, sems.at[i]) for i, (src, dst) in enumerate(pairs)]
    for copy in copies:
        copy.start()
    for copy in copies[:2]:
        copy.wait()
    inv_r, inv_i = adm[0, 0], adm[1, 0]
    steps = [product(inv_r, inv_i, adm[0, k], adm[1, k]) for k in range(1, 1 + LINKS)]
    blank = jnp.zeros((5, inv_r.shape[1]), F32)
    coefs = jnp.concatenate(
        [inv_r] + [s[0] for s in steps] + [inv_i] + [s[1] for s in steps] + [off[...].astype(F32), blank], axis=0
    )
    coef_ref[...] = coefs
    tiles = coefs.shape[1] // 128
    for v in range(tiles):
        group_ref[v * 8 : v * 8 + 8, :] = grouped(coefs[:8, v * 128 : v * 128 + 128])
    row = iota((16, 128), 0)

    def edge(v, at):
        group = jnp.broadcast_to(group_ref[at : at + 1, :], (16, 128))
        return jnp.where(row == EXTRA, group, coefs[:, v * 128 : v * 128 + 128])

    first, last = edge(0, 0), edge(tiles - 1, tiles * 8 - 1)
    is_even = even("bus")
    a_ref[...] = jnp.where(is_even, last, first)
    b_ref[...] = jnp.where(is_even, first, last)

    for copy in copies[2:6]:
        copy.wait()
    for c in range(CONV):
        lanes = slice(c * 128, c * 128 + 128)
        aux_ref[0:1, lanes] = jnp.full((1, 128), steep[kind[c]], F32)
        aux_ref[1:2, lanes] = power[c : c + 1, :]
    lane = iota((1, 128), 1)
    column = lax.rem(lax.axis_index("harm"), HALF)
    mark = jnp.zeros((1, 128), F32)
    start = jnp.full((1, 128), SUB, F32)
    for c in range(CONV):
        number = lax.rem(bus[c], SUB).astype(F32)
        mark += jnp.where(lane == c * HALF + column, number, 0.0)
        start += jnp.where(lane % 64 // 16 == c, number, 0.0)
    aux_ref[2:3, :128] = mark
    aux_ref[3:4, :128] = start
    for copy in copies[6:]:
        copy.wait()


def convert_kernel(volt_ref, turned_ref, basis_ref, aux_ref, group_ref, out_ref, volts, rows):
    volts[...] = volt_ref[...].astype(F32)
    kinds = 2 * H
    volt = jnp.concatenate(
        [volts[pl.ds(c, kinds, stride=CONV), :] for c in range(CONV)], axis=1
    ).astype(BF16)
    steep, power = aux_ref[0:1, :], aux_ref[1:2, :]
    spectra = jnp.zeros((kinds, CONV * 128), F32)
    step = 256
    for n in range(0, NT, step):
        wave = jnp.dot(turned_ref[n : n + step, :], volt, preferred_element_type=F32)
        current = (power * jnp.tanh(steep * wave)).astype(BF16)
        spectra += jnp.dot(basis_ref[:, n : n + step], current, preferred_element_type=F32)
    spectra = spectra * NT ** (-0.5)
    for c in range(CONV):
        for p in range(2):
            rows[pl.ds(2 * c + p, H, stride=ROWS), :] = spectra[p * H : p * H + H, c * 128 : c * 128 + 128]
    rows[pl.ds(COEF, H, stride=ROWS), :] = pltpu.roll(group_ref[...], 1, 0)
    rows[pl.ds(COEF + 1, H, stride=ROWS), :] = group_ref[...]
    rows[pl.ds(COEF + 2, H, stride=ROWS), :] = pltpu.roll(group_ref[...], H - 1, 0)
    rows[pl.ds(MARK, H, stride=ROWS), :] = jnp.broadcast_to(aux_ref[2:3, :128], (H, 128))
    out_ref[...] = rows[...].astype(BF16)


def low_high(a, b):
    is_even = even("bus")
    return jnp.where(is_even, b, a), jnp.where(is_even, a, b)


def patch_kernel(rows_ref, a_ref, b_ref, out_ref):
    low, high = low_high(a_ref[EXTRA : EXTRA + 1, :], b_ref[EXTRA : EXTRA + 1, :])
    size = rows_ref.shape[0]
    out_ref[16 : size - 16, :] = rows_ref[16 : size - 16, :]
    row = iota((16, 128), 0)
    out_ref[:16, :] = jnp.where(row == COEF, low, rows_ref[:16, :].astype(F32)).astype(BF16)
    at = 16 - ROWS + COEF + 2
    out_ref[size - 16 :, :] = jnp.where(row == at, high, rows_ref[size - 16 :, :].astype(F32)).astype(BF16)


def sweeps_kernel(coef_ref, a_ref, b_ref, q_ref, ext_ref):
    low, high = low_high(a_ref[...], b_ref[...])
    whole = jnp.concatenate([low, coef_ref[...], high], axis=1)
    width = whole.shape[1]
    ext_ref[...] = pltpu.roll(whole, width - (128 - EDGE), 1)[:, : width - 128]
    rows = iota((WIN, WIN), 0)
    lanes = iota((1, WIN), 1)
    same = iota((TILE, WIN), 0) + EDGE == iota((TILE, WIN), 1)
    for b in range(q_ref.shape[0]):
        win = slice(b * TILE, b * TILE + WIN)
        turned_r = jnp.zeros((WIN, WIN), F32)
        turned_i = jnp.zeros((WIN, WIN), F32)
        for k in range(LINKS):
            here = rows == lanes + ext_ref[8 + k : 9 + k, win].astype(I32)
            turned_r += jnp.where(here, ext_ref[1 + k : 2 + k, win], 0.0)
            turned_i += jnp.where(here, ext_ref[5 + k : 6 + k, win], 0.0)
        step_r, step_i = turned_r.T, turned_i.T
        mid_r, mid_i = step_r[EDGE : EDGE + TILE], step_i[EDGE : EDGE + TILE]
        twice = jnp.dot(
            jnp.concatenate([mid_r, mid_i], axis=0).astype(BF16),
            jnp.concatenate([step_r, step_i], axis=1).astype(BF16),
            preferred_element_type=F32,
        )
        all_r = twice[:TILE, :WIN] - twice[TILE:, WIN:] + mid_r + jnp.where(same, 1.0, 0.0)
        all_i = twice[:TILE, WIN:] + twice[TILE:, :WIN] + mid_i
        q_r, q_i = product(all_r, all_i, ext_ref[0:1, win], ext_ref[4:5, win])
        q_ref[b, :TILE, :] = q_r.astype(BF16)
        q_ref[b, TILE:, :] = q_i.astype(BF16)


def network_kernel(got_ref, a_ref, b_ref, q_ref, volt_ref, rows, inject):
    rows[...] = got_ref[...].astype(F32)
    low, high = low_high(a_ref[...].astype(F32), b_ref[...].astype(F32))

    def part(p):
        return jnp.concatenate(
            [
                rows[pl.ds(h * HALF * ROWS + 2 * c + p, HALF, stride=ROWS), :]
                for h in range(2)
                for c in range(CONV)
            ],
            axis=0,
        )

    spectra = jnp.concatenate([part(0), part(1)], axis=1).astype(BF16)
    convs = H * CONV
    at = [
        jnp.sum(rows[pl.ds(h * HALF * ROWS + MARK, HALF, stride=ROWS), :], axis=0, keepdims=True)
        for h in range(2)
    ]
    at = jnp.concatenate(at, axis=1).astype(I32)
    lane = iota((1, convs), 1)
    source = lane // (CONV * HALF) * HALF + lane % HALF
    target = source * SUB + at
    buses = H * SUB
    owner = jnp.where(iota((buses, convs), 0) == target, 1.0, 0.0).astype(BF16)
    inject[EDGE : EDGE + buses, :] = jnp.dot(owner, spectra, preferred_element_type=F32).astype(BF16)
    for edge, lane0, row0 in ((low, HALF - 1, 0), (high, 0, EDGE + buses)):
        total_r = jnp.zeros((SUB, 128), F32)
        total_i = jnp.zeros((SUB, 128), F32)
        for c in range(CONV):
            at = c * HALF + lane0
            bus = jnp.broadcast_to(edge[MARK : MARK + 1, at : at + 1], (SUB, 128)).astype(I32)
            here = iota((SUB, 128), 0) == bus
            total_r += jnp.where(here, edge[2 * c : 2 * c + 1, :], 0.0)
            total_i += jnp.where(here, edge[2 * c + 1 : 2 * c + 2, :], 0.0)
        inject[row0 : row0 + EDGE, :] = jnp.concatenate([total_r, total_i], axis=1).astype(BF16)
    tail = 2 * EDGE + buses
    inject[tail:, :] = jnp.zeros((inject.shape[0] - tail, 256), BF16)
    for b in range(q_ref.shape[0]):
        acc = jnp.dot(q_ref[b], inject[b * TILE : b * TILE + WIN, :], preferred_element_type=F32)
        volt_ref[0, 0, b * TILE : b * TILE + TILE, :] = (acc[:TILE, :128] - acc[TILE:, 128:]).astype(BF16)
        volt_ref[1, 0, b * TILE : b * TILE + TILE, :] = (acc[:TILE, 128:] + acc[TILE:, :128]).astype(BF16)


def swapped(x):
    return pltpu.roll(x, 64, 1)


def packed_product(a, b, real):
    turned = swapped(b)
    return a * jnp.where(real, b, turned) + swapped(a) * jnp.where(real, -turned, b)


def aim_kernel(aux_ref, mine_ref, a_ref, b_ref, ext_ref, pick_ref, match_ref, spec_ref, rows):
    harm = lax.axis_index("harm")
    is_even = even("harm")
    size = mine_ref.shape[0]
    got_a, got_b = a_ref[...].astype(F32), b_ref[...].astype(F32)
    rows[:size, :] = jnp.where(is_even, got_b, got_a)
    rows[size : 2 * size, :] = mine_ref[...].astype(F32)
    rows[2 * size :, :] = jnp.where(is_even, got_a, got_b)

    shape = (8, 128)
    lane = iota(shape, 1)
    real = lane < 64
    spot = lane % 64
    path = spot % 16
    base = pl.multiple_of(harm * SUB // 128 * 128, 128)
    offs = ext_ref[8:16, pl.ds(base, 256)]
    offs = pltpu.roll(offs, 256 - lax.rem(harm * SUB, 128), 1)[:, :128].astype(I32)
    offs = [jnp.broadcast_to(offs[k : k + 1, :], shape) for k in range(LINKS)]

    def hop(bus, line):
        total = bus
        for k in range(LINKS):
            total += jnp.where(line == k + 1, jnp.take_along_axis(offs[k], bus, axis=1), 0)
        return total

    def place(bus, line, used):
        at = bus // SUB * 128 + line * SUB + bus % SUB + jnp.where(real, 0, 64)
        return jnp.where(used, at, -1)[:1]

    bus0 = jnp.broadcast_to(aux_ref[3:4, :128], shape).astype(I32)
    two = path >= 1 + LINKS
    line1 = jnp.where(two, 1 + (path - 1 - LINKS) // LINKS, path)
    line2 = jnp.where(two, 1 + (path - 1 - LINKS) % LINKS, 0)
    valid = path < 1 + LINKS + LINKS * LINKS
    line1 = jnp.where(valid, line1, 0)
    line2 = jnp.where(valid, line2, 0)
    bus1 = hop(bus0, line1)
    bus2 = hop(bus1, line2)
    places = jnp.concatenate(
        [place(bus0, line1, valid & (path >= 1)), place(bus1, line2, valid & two), place(bus2, 0, valid)], axis=1
    )
    pick_ref[...] = jnp.where(iota((3 * 128, 3 * 128), 0) == places, 1.0, 0.0).astype(BF16)
    many = (128, 128)
    row = iota(many, 0)
    other = row % 64 % (3 * CONV)
    bus_of = jnp.zeros(many, I32)
    for q in range(3):
        marks = rows[q * size + MARK : q * size + MARK + 1, :]
        column = lax.rem(harm + q - 1 + HALF, HALF)
        for c in range(CONV):
            bus = jnp.sum(jnp.where(iota((1, 128), 1) == c * HALF + column, marks, 0.0), axis=1, keepdims=True)
            bus = jnp.broadcast_to(bus.astype(I32), many) + q * SUB
            bus_of = jnp.where(other == q * CONV + c, bus, bus_of)
    wide = iota(many, 1)
    match = (row // 64 == wide // 64) & (row % 64 // (3 * CONV) == wide % 64 // 16) & (bus_of == bus2[:1])
    match_ref[...] = jnp.where(match, 1.0, 0.0).astype(BF16)
    for q in range(3):
        for o in range(2 * CONV):
            at = (q * 2 * CONV + o) * H
            spec_ref[at : at + H, :] = rows[pl.ds(q * size + o, H, stride=ROWS), :]


def near_kernel(got_ref, pick_ref, match_ref, spec_ref, out_ref, coefs, out):
    coefs[...] = got_ref[...].astype(F32)
    window = jnp.concatenate(
        [coefs[pl.ds(COEF + q, H, stride=ROWS), :] for q in range(3)], axis=1
    ).astype(BF16)
    found = jnp.dot(window, pick_ref[...], preferred_element_type=F32)
    lane = iota((1, 128), 1)
    real, path = lane < 64, lane % 16
    first = found[:, :128] + jnp.where(real & (path == 0), 1.0, 0.0)
    second = found[:, 128:256] + jnp.where(real & (path <= LINKS), 1.0, 0.0)
    weight = packed_product(packed_product(first, second, real), found[:, 256:], real)
    high = weight.astype(BF16)
    rest = (weight - high.astype(F32)).astype(BF16)
    dims = (((1,), (1,)), ((), ()))
    table = lax.dot_general(high, match_ref[...], dims, preferred_element_type=F32)
    table += lax.dot_general(rest, match_ref[...], dims, preferred_element_type=F32)

    total = [[jnp.zeros((H, 128), F32) for _ in range(2)] for _ in range(CONV)]
    for q in range(3):
        for o in range(CONV):
            at = (q * CONV + o) * 2 * H
            spec_r, spec_i = spec_ref[at : at + H, :], spec_ref[at + H : at + 2 * H, :]
            for c in range(CONV):
                at = c * 3 * CONV + q * CONV + o
                add_r, add_i = product(table[:, at : at + 1], table[:, 64 + at : 65 + at], spec_r, spec_i)
                total[c][0] += add_r
                total[c][1] += add_i
    for c in range(CONV):
        for p in range(2):
            out[pl.ds(p * H * CONV + c, H, stride=CONV), :] = total[c][p]
    out_ref[...] = out[...].astype(BF16)


VMEM = pl.BlockSpec(memory_space=pltpu.VMEM)
HBM = pl.BlockSpec(memory_space=pltpu.HBM)


def call(kernel, name, out_shape, in_specs, scratch=(), cost=(0, 0, 0)):
    flops, moved, hard = cost
    return pl.pallas_call(
        kernel,
        out_shape=out_shape,
        in_specs=in_specs,
        out_specs=jax.tree.map(lambda _: VMEM, out_shape),
        scratch_shapes=list(scratch),
        compiler_params=pltpu.CompilerParams(vmem_limit_bytes=40 * 2**20),
        cost_estimate=pl.CostEstimate(flops=flops, bytes_accessed=moved, transcendentals=hard),
        name=name,
    )


def swaps(count):
    rounds = []
    for start in (0, 1):
        firsts = range(start, count - 1, 2)
        rounds.append([(i, i + 1) for i in firsts] + [(i + 1, i) for i in firsts])
    return rounds


def local(conv_volt, conv_power, conv_type, type_steep, conv_bus, admittance, link_offset):
    harm_count = lax.axis_size("harm")
    bus_count = lax.axis_size("bus")
    block = admittance.shape[3]
    snapshots = conv_volt.shape[3]
    tiles = block // TILE
    size = harm_count * ROWS
    kinds = 2 * H
    S = jax.ShapeDtypeStruct
    over_bus = swaps(bus_count)
    number = lambda r: r % harm_count * bus_count + r // harm_count
    over_ranges = [[(number(s), number(d)) for s, d in pairs] for pairs in swaps(harm_count * bus_count)]

    basis = make_basis()
    coef, edge_a, edge_b, aux, group, volt, turned, basis = call(
        prepare_kernel,
        "prepare",
        (
            S((16, block), F32),
            S((16, 128), F32),
            S((16, 128), F32),
            S((8, CONV * 128), F32),
            S((harm_count, 128), F32),
            S((kinds * CONV, snapshots), BF16),
            S((NT, kinds), BF16),
            S((kinds, NT), BF16),
        ),
        [HBM] * 9,
        [
            pltpu.VMEM((2, 4, 1, block), F32),
            pltpu.VMEM((LINKS, block), I32),
            pltpu.SMEM((CONV,), I32),
            pltpu.SMEM(type_steep.shape, F32),
            pltpu.SMEM((CONV,), I32),
            pltpu.VMEM((CONV, snapshots), F32),
            pltpu.SemaphoreType.DMA((9,)),
        ],
    )(
        *(
            pltpu.with_memory_space_constraint(array, pltpu.HBM)
            for array in (
                admittance,
                link_offset,
                conv_type,
                type_steep,
                conv_bus,
                conv_power,
                conv_volt.reshape(kinds * CONV, snapshots),
                jnp.asarray(np.ascontiguousarray(basis.T)),
                jnp.asarray(basis),
            )
        )
    )
    edge_a = lax.ppermute(edge_a, "bus", over_bus[0])
    edge_b = lax.ppermute(edge_b, "bus", over_bus[1])

    payload = call(
        convert_kernel,
        "convert",
        S((size, 128), BF16),
        [VMEM] * 5,
        [pltpu.VMEM((kinds * CONV, 128), F32), pltpu.VMEM((size, 128), F32)],
        (2 * 2 * 128 * 1024 * 512, 2**20, 2**19),
    )(volt, turned, basis, aux, group)
    payload = call(patch_kernel, "patch", S((size, 128), BF16), [VMEM] * 3)(payload, edge_a, edge_b)

    four = (harm_count, ROWS // 4, 4, snapshots)
    got = lax.all_to_all(payload.reshape(four), "harm", split_axis=0, concat_axis=0, tiled=True)

    q, ext = call(
        sweeps_kernel,
        "sweeps",
        (S((tiles, 2 * TILE, WIN), BF16), S((16, block + 128), F32)),
        [VMEM] * 3,
        cost=(2 * tiles * 256 * 256 * 512, 2**20, 0),
    )(coef, edge_a, edge_b)
    beside_a = lax.ppermute(payload, ("harm", "bus"), over_ranges[0])
    beside_b = lax.ppermute(payload, ("harm", "bus"), over_ranges[1])
    pick, match, spec = call(
        aim_kernel,
        "aim",
        (S((3 * 128, 3 * 128), BF16), S((128, 128), BF16), S((3 * 2 * CONV * H, 128), F32)),
        [VMEM] * 5,
        [pltpu.VMEM((3 * size, 128), F32)],
        (10**6, 2**20, 0),
    )(aux, payload, beside_a, beside_b, ext)
    got, q, pick, match, spec = lax.optimization_barrier((got, q, pick, match, spec))

    is_even = even("bus")
    outer = harm_count - 1
    rows_a = lax.dynamic_index_in_dim(got, jnp.where(is_even, outer, 0), 0, keepdims=False)
    rows_b = lax.dynamic_index_in_dim(got, jnp.where(is_even, 0, outer), 0, keepdims=False)
    rows_a = lax.ppermute(rows_a.reshape(ROWS, snapshots), "bus", over_bus[0])
    rows_b = lax.ppermute(rows_b.reshape(ROWS, snapshots), "bus", over_bus[1])
    got = got.reshape(size, snapshots)
    near = call(
        near_kernel,
        "near",
        S((kinds * CONV, snapshots), BF16),
        [VMEM] * 4,
        [pltpu.VMEM((size, 128), F32), pltpu.VMEM((kinds * CONV, 128), F32)],
        (2 * 10**7, 2**20, 0),
    )(got, pick, match, spec)
    bus_volt = call(
        network_kernel,
        "network",
        S((2, 1, block, snapshots), BF16),
        [VMEM] * 4,
        [pltpu.VMEM((size, 128), F32), pltpu.VMEM((block + WIN - TILE, 256), BF16)],
        (2 * tiles * 256 * 256 * 256, 2**20, 0),
    )(got, rows_a, rows_b, q)
    return (bus_volt, near.reshape(2, H, CONV, snapshots))


def solution(mesh):
    in_specs = (
        P(None, None, ("bus", "harm"), None),
        P(("bus", "harm"), None),
        P(("bus", "harm")),
        P(),
        P(("bus", "harm")),
        P(None, None, "harm", "bus"),
        P(None, "bus"),
    )
    out_specs = (P(None, "harm", "bus", None), P(None, None, ("bus", "harm"), None))
    return jax.shard_map(local, mesh=mesh, in_specs=in_specs, out_specs=out_specs, check_vma=False)
```

time: 56.2 us -> 52.8 us (0.940)
  the two profiles are of different devices: /device:TPU:32 before, /device:TPU:24 now
where the time goes in v3:
time: 52.8 us; the launch traced here: 52.5 us
  starting transfers between devices  37.8 us (72%)
  Pallas kernels  10.8 us (20%)
  waiting for transfers between devices  3.01 us (6%)
  between operations  0.76 us (1%)
    all_to_all x1, starting transfers between devices, local(): lax.all_to_all(payload.reshape(four), 'harm', split_axis=0, concat_axis=0...  13.8 us
    ppermute x1, starting transfers between devices, local(): beside_b = lax.ppermute(payload, ('harm', 'bus'), over_ranges[1])  6.97 us
    ppermute x1, starting transfers between devices, local(): rows_b = lax.ppermute(rows_b.reshape(ROWS, snapshots), 'bus', over_bus[1])  5.58 us
    ppermute x1, starting transfers between devices, local(): edge_b = lax.ppermute(edge_b, 'bus', over_bus[1])  4.92 us
    pallas_call x1, Pallas kernels, local(): call(sweeps_kernel, 'sweeps', (S((tiles, 2 * TILE, WIN), BF16), S((16, bl...  2.44 us
    pallas_call x1, Pallas kernels, local(): call(near_kernel, 'near', S((kinds * CONV, snapshots), BF16), [VMEM] * 4,...  2.36 us
    ppermute x1, starting transfers between devices, local(): edge_a = lax.ppermute(edge_a, 'bus', over_bus[0])  2.36 us
    ppermute x1, starting transfers between devices, local(): rows_a = lax.ppermute(rows_a.reshape(ROWS, snapshots), 'bus', over_bus[0])  2.27 us
  transfers between devices with their start and end apart: 7, of which 2 were waited for; matrix products, arithmetic and copies ran while one was open for 0% of the time, Pallas kernels for 14%

profile of v3, /device:TPU:24, one launch (start us, length us, event | category | flops | bytes accessed | tf_op | source)
XLA Modules:
  0.0 52.5 jit_solution(3634493389694659012)
XLA Ops:
  0.6 1.2 %prepare.1 = (f32[16,1024]{1,0:T(8,128)S(1)}, f32[16,128]{1,0:T(8,128)S(1)}, f32[16,128]{1,0:T(8,128)S(1)}, f32[8,512]{1,0:T(8,128)S(1)}, f32[64,128]{1,0:T(8,12...) custom-call(f32[2,4,1,1024]{3,2,1,0:T(1,128)} %adm_hbm.1, ...), custom_call_target="tpu_custom_call" | custom-call | tf_op jit(solution)/shard_map/prepare/pallas_call | solution.py:371
  1.9 2.4 %collective-permute-start = (f32[16,128]{1,0:T(8,128)S(1)}, f32[16,128]{1,0:T(8,128)S(1)}, u32[]{:S(2)}, u32[]{:S(2)}) collective-permute-start(f32[16,128]{1,0:T(8,128)S(1)} %get-tuple-element.25), channel_id=1, source_target_pairs={{0,1},{2,3},{4,5},{6,7},{1,0},{3,2},{5,4},{7,6},{8,9},{10,11},{12,... | collective-permute-start | bytes 24584 | tf_op jit(solution)/shard_map/ppermute | solution.py:410
  4.2 4.9 %collective-permute-start.1 = (f32[16,128]{1,0:T(8,128)S(1)}, f32[16,128]{1,0:T(8,128)S(1)}, u32[]{:S(2)}, u32[]{:S(2)}) collective-permute-start(f32[16,128]{1,0:T(8,128)S(1)} %get-tuple-element.26), channel_id=1, source_target_pairs={{1,2},{3,4},{5,6},{2,1},{4,3},{6,5},{9,10},{11,12},{13,14},{10,9},... | collective-permute-start | bytes 24584 | tf_op jit(solution)/shard_map/ppermute | solution.py:411
  9.2 1.0 %convert.1.rows_ref = bf16[768,128]{1,0:T(8,128)(2,1)S(1)} custom-call(bf16[512,128]{1,0:T(8,128)(2,1)S(1)} %get-tuple-element.20.volt_ref, bf16[1024,128]{1,0:T(8,128)(2,1)S(1)} %get-tuple-element.21.turned_ref, bf16[128,1024]{1,0:T(8,128)(2,1)S(1)} %get-tuple-element.22.basis_ref, f32[8,512]{1,0:T(8,128)S(1)} %get-tuple-element.23.aux_ref, ...), custom_call_target="tpu_custom_call" | custom-call | flops 268435456 | bytes 1048576 | tf_op jit(solution)/shard_map/convert/pallas_call | solution.py:413
  10.2 0.0 collective-permute-done.a_ref
  10.2 0.8 %collective-permute-done.1.b_ref = f32[16,128]{1,0:T(8,128)S(1)} collective-permute-done((f32[16,128]{1,0:T(8,128)S(1)}, f32[16,128]{1,0:T(8,128)S(1)}, u32[]{:S(2)}, u32[]{:S(2)}) %collective-permute-start.1) | collective-permute-done | bytes 8224 | tf_op jit(solution)/shard_map/ppermute | solution.py:411
  11.0 0.7 %patch.1.mine_ref = bf16[768,128]{1,0:T(8,128)(2,1)} custom-call(bf16[768,128]{1,0:T(8,128)(2,1)S(1)} %convert.1.rows_ref, f32[16,128]{1,0:T(8,128)S(1)} %collective-permute-done.a_ref, f32[16,128]{1,0:T(8,128)S(1)} %collective-permute-done.1.b_ref), custom_call_target="tpu_custom_call" | custom-call | tf_op jit(solution)/shard_map/patch/pallas_call | solution.py:421
  11.7 13.8 %all-to-all-start = ((bf16[64,3,4,128]{3,2,1,0:T(4,128)(2,1)}), bf16[64,3,4,128]{3,2,1,0:T(4,128)(2,1)S(1)}, u32[]{:S(2)}, u32[]{:S(2)}) async-start(bf16[64,3,4,128]{3,2,1,0:T(4,128)(2,1)} %bitcast.1), calls=%async_computation | async-start | bytes 393216 | tf_op jit(solution)/shard_map/all_to_all | solution.py:424
  25.5 2.0 %collective-permute-start.2 = (bf16[768,128]{1,0:T(8,128)(2,1)}, bf16[768,128]{1,0:T(8,128)(2,1)S(1)}, u32[]{:S(2)}, u32[]{:S(2)}) collective-permute-start(bf16[768,128]{1,0:T(8,128)(2,1)} %patch.1.mine_ref), channel_id=1, source_target_pairs={{0,8},{16,24},{32,40},{48,56},{64,72},{80,88},{96,104},{112,120},{... | collective-permute-start | bytes 589832 | tf_op jit(solution)/shard_map/ppermute | solution.py:433
  27.5 7.0 %collective-permute-start.3 = (bf16[768,128]{1,0:T(8,128)(2,1)}, bf16[768,128]{1,0:T(8,128)(2,1)S(1)}, u32[]{:S(2)}, u32[]{:S(2)}) collective-permute-start(bf16[768,128]{1,0:T(8,128)(2,1)} %patch.1.mine_ref), channel_id=1, source_target_pairs={{8,16},{24,32},{40,48},{56,64},{72,80},{88,96},{104,112},{120,128}... | collective-permute-start | bytes 589832 | tf_op jit(solution)/shard_map/ppermute | solution.py:434
  34.4 2.4 %sweeps.1 = (bf16[8,256,256]{2,1,0:T(8,128)(2,1)S(1)}, f32[16,1152]{1,0:T(8,128)S(1)}) custom-call(f32[16,1024]{1,0:T(8,128)S(1)} %get-tuple-element.27.coef_ref, f32[16,128]{1,0:T(8,128)S(1)} %collective-permute-done.a_ref, f32[16,128]{1,0:T(8,128)S(1)} %collective-permute-done.1.b_ref), custom_call_target="tpu_custom_call" | custom-call | flops 536870912 | bytes 1048576 | tf_op jit(solution)/shard_map/sweeps/pallas_call | solution.py:426
  36.9 0.0 collective-permute-done.2.a_ref
  36.9 2.2 %collective-permute-done.3.b_ref = bf16[768,128]{1,0:T(8,128)(2,1)S(1)} collective-permute-done((bf16[768,128]{1,0:T(8,128)(2,1)}, bf16[768,128]{1,0:T(8,128)(2,1)S(1)}, u32[]{:S(2)}, u32[]{:S(2)}) %collective-permute-start.3) | collective-permute-done | bytes 196640 | tf_op jit(solution)/shard_map/ppermute | solution.py:434
  39.1 1.4 %aim.1 = (bf16[384,384]{1,0:T(8,128)(2,1)S(1)}, bf16[128,128]{1,0:T(8,128)(2,1)S(1)}, f32[1536,128]{1,0:T(8,128)S(1)}) custom-call(f32[8,512]{1,0:T(8,128)S(1)} %get-tuple-element.23.aux_ref, bf16[768,128]{1,0:T(8,128)(2,1)} %patch.1.mine_ref, bf16[768,128]{1,0:T(8,128)(2,1)S(1)} %collective-permute-done.2.a_ref, ...), custom_call_target="tpu_custom_call" | custom-call | flops 1000000 | bytes 1048576 | tf_op jit(solution)/shard_map/aim/pallas_call | solution.py:435
  40.5 0.0 all-to-all-done
  40.6 2.3 %collective-permute-start.4 = (bf16[12,128]{1,0:T(8,128)(2,1)S(1)}, bf16[12,128]{1,0:T(8,128)(2,1)S(1)}, u32[]{:S(2)}, u32[]{:S(2)}) collective-permute-start(bf16[12,128]{1,0:T(8,128)(2,1)S(1)} %reshape.27), channel_id=1, source_target_pairs={{0,1},{2,3},{4,5},{6,7},{1,0},{3,2},{5,4},{7,6},{8,9},{10,11},{12,... | collective-permute-start | bytes 9224 | tf_op jit(solution)/shard_map/ppermute | solution.py:449
  42.9 5.6 %collective-permute-start.5 = (bf16[12,128]{1,0:T(8,128)(2,1)S(1)}, bf16[12,128]{1,0:T(8,128)(2,1)S(1)}, u32[]{:S(2)}, u32[]{:S(2)}) collective-permute-start(bf16[12,128]{1,0:T(8,128)(2,1)S(1)} %reshape.28), channel_id=1, source_target_pairs={{1,2},{3,4},{5,6},{2,1},{4,3},{6,5},{9,10},{11,12},{13,14},{10,9},... | collective-permute-start | bytes 9224 | tf_op jit(solution)/shard_map/ppermute | solution.py:450
  48.5 2.4 %near.1 = bf16[512,128]{1,0:T(8,128)(2,1)} custom-call(bf16[768,128]{1,0:T(8,128)(2,1)S(1)} %bitcast.4, bf16[384,384]{1,0:T(8,128)(2,1)S(1)} %get-tuple-element.35.pick_ref, bf16[128,128]{1,0:T(8,128)(2,1)S(1)} %get-tuple-element.36.match_ref, f32[1536,128]{1,0:T(8,128)S(1)} %get-tuple-element.37.spec_ref), custom_call_target="tpu_custom_call" | custom-call | flops 20000000 | bytes 1048576 | tf_op jit(solution)/shard_map/near/pallas_call | solution.py:452
  50.8 0.0 collective-permute-done.4.a_ref
  50.8 0.0 collective-permute-done.5.b_ref
  50.8 1.6 %network.1 = bf16[2,1,1024,128]{3,2,1,0:T(8,128)(2,1)} custom-call(bf16[768,128]{1,0:T(8,128)(2,1)S(1)} %bitcast.5, bf16[12,128]{1,0:T(8,128)(2,1)S(1)} %collective-permute-done.4.a_ref, bf16[12,128]{1,0:T(8,128)(2,1)S(1)} %collective-permute-done.5.b_ref, bf16[8,256,256]{2,1,0:T(8,128)(2,1)S(1)} %get-tuple-element.34.q_ref), custom_call_target="tpu_custom_call" | custom-call | flops 268435456 | bytes 1048576 | tf_op jit(solution)/shard_map/network/pallas_call | solution.py:460
  (3 shorter events, 0.1 us)
Async XLA Ops:
  1.9 8.3 %collective-permute-start = (f32[16,128]{1,0:T(8,128)S(1)}, f32[16,128]{1,0:T(8,128)S(1)}, u32[]{:S(2)}, u32[]{:S(2)}) collective-permute-start(f32[16,128]{1,0:T(8,128)S(1)} %get-tuple-element.25), channel_id=1, source_target_pairs={{0,1},{2,3},{4,5},{6,7},{1,0},{3,2},{5,4},{7,6},{8,9},{10,11},{12,... | collective-permute-start | bytes 24584 | tf_op jit(solution)/shard_map/ppermute | solution.py:410
  4.2 6.8 %collective-permute-start.1 = (f32[16,128]{1,0:T(8,128)S(1)}, f32[16,128]{1,0:T(8,128)S(1)}, u32[]{:S(2)}, u32[]{:S(2)}) collective-permute-start(f32[16,128]{1,0:T(8,128)S(1)} %get-tuple-element.26), channel_id=1, source_target_pairs={{1,2},{3,4},{5,6},{2,1},{4,3},{6,5},{9,10},{11,12},{13,14},{10,9},... | collective-permute-start | bytes 24584 | tf_op jit(solution)/shard_map/ppermute | solution.py:411
  11.7 28.9 %all-to-all-start = ((bf16[64,3,4,128]{3,2,1,0:T(4,128)(2,1)}), bf16[64,3,4,128]{3,2,1,0:T(4,128)(2,1)S(1)}, u32[]{:S(2)}, u32[]{:S(2)}) async-start(bf16[64,3,4,128]{3,2,1,0:T(4,128)(2,1)} %bitcast.1), calls=%async_computation | async-start | bytes 393216 | tf_op jit(solution)/shard_map/all_to_all | solution.py:424
  25.5 11.4 %collective-permute-start.2 = (bf16[768,128]{1,0:T(8,128)(2,1)}, bf16[768,128]{1,0:T(8,128)(2,1)S(1)}, u32[]{:S(2)}, u32[]{:S(2)}) collective-permute-start(bf16[768,128]{1,0:T(8,128)(2,1)} %patch.1.mine_ref), channel_id=1, source_target_pairs={{0,8},{16,24},{32,40},{48,56},{64,72},{80,88},{96,104},{112,120},{... | collective-permute-start | bytes 589832 | tf_op jit(solution)/shard_map/ppermute | solution.py:433
  27.5 11.6 %collective-permute-start.3 = (bf16[768,128]{1,0:T(8,128)(2,1)}, bf16[768,128]{1,0:T(8,128)(2,1)S(1)}, u32[]{:S(2)}, u32[]{:S(2)}) collective-permute-start(bf16[768,128]{1,0:T(8,128)(2,1)} %patch.1.mine_ref), channel_id=1, source_target_pairs={{8,16},{24,32},{40,48},{56,64},{72,80},{88,96},{104,112},{120,128}... | collective-permute-start | bytes 589832 | tf_op jit(solution)/shard_map/ppermute | solution.py:434
  40.6 10.2 %collective-permute-start.4 = (bf16[12,128]{1,0:T(8,128)(2,1)S(1)}, bf16[12,128]{1,0:T(8,128)(2,1)S(1)}, u32[]{:S(2)}, u32[]{:S(2)}) collective-permute-start(bf16[12,128]{1,0:T(8,128)(2,1)S(1)} %reshape.27), channel_id=1, source_target_pairs={{0,1},{2,3},{4,5},{6,7},{1,0},{3,2},{5,4},{7,6},{8,9},{10,11},{12,... | collective-permute-start | bytes 9224 | tf_op jit(solution)/shard_map/ppermute | solution.py:449
  42.9 8.0 %collective-permute-start.5 = (bf16[12,128]{1,0:T(8,128)(2,1)S(1)}, bf16[12,128]{1,0:T(8,128)(2,1)S(1)}, u32[]{:S(2)}, u32[]{:S(2)}) collective-permute-start(bf16[12,128]{1,0:T(8,128)(2,1)S(1)} %reshape.28), channel_id=1, source_target_pairs={{1,2},{3,4},{5,6},{2,1},{4,3},{6,5},{9,10},{11,12},{13,14},{10,9},... | collective-permute-start | bytes 9224 | tf_op jit(solution)/shard_map/ppermute | solution.py:450

commit v4 on v3

v4 whole, which is shorter than its diff:
```python
import math

import jax
import jax.numpy as jnp
import numpy as np
from jax import lax
from jax.experimental import pallas as pl
from jax.experimental.pallas import tpu as pltpu
from jax.sharding import PartitionSpec as P

H = 64
NT = 1024
REACH = 8
LINKS = 3
SUB = 16
CONV = 4
EDGE = 2 * REACH
TILE = 128
WIN = 256
ROWS = 12
COEF = 8
PAIR = 9
SPAN = 10
MARK = 11
HALF = 32
F32 = jnp.float32
BF16 = jnp.bfloat16
I32 = jnp.int32


def make_basis():
    turn = np.arange(1, H + 1)[:, None] * np.arange(NT)[None, :] % NT
    angle = turn * (2.0 * math.pi / NT)
    return np.concatenate([np.cos(angle), -np.sin(angle)], axis=0).astype(BF16)


def iota(shape, dim):
    return lax.broadcasted_iota(I32, shape, dim)


def product(ar, ai, br, bi):
    return ar * br - ai * bi, ar * bi + ai * br


def grouped(x):
    k, j = iota((8, 128), 0), iota((8, 128), 1) // SUB
    for s in (1, 2, 4):
        later = pltpu.roll(pltpu.roll(x, s, 0), 128 - SUB * s, 1)
        sooner = pltpu.roll(pltpu.roll(x, 8 - s, 0), SUB * s, 1)
        bk, bj = (k // s) % 2, (j // s) % 2
        x = jnp.where(bk == bj, x, jnp.where(bk == 1, later, sooner))
    return x


def even(axis):
    return lax.rem(lax.axis_index(axis), 2) == 0


def prepare_kernel(
    adm_hbm, off_hbm, type_hbm, steep_hbm, bus_hbm, power_hbm, volt_hbm, turned_hbm, basis_hbm,
    coef_ref, a_ref, b_ref, aux_ref, group_ref, volt_ref, turned_ref, basis_ref,
    adm, off, kind, steep, bus, power, spans, sems,
):
    pairs = [
        (adm_hbm, adm), (off_hbm, off), (type_hbm, kind), (steep_hbm, steep), (bus_hbm, bus), (power_hbm, power),
        (volt_hbm, volt_ref), (turned_hbm, turned_ref), (basis_hbm, basis_ref),
    ]
    copies = [pltpu.make_async_copy(src, dst, sems.at[i]) for i, (src, dst) in enumerate(pairs)]
    for copy in copies:
        copy.start()
    for copy in copies[:2]:
        copy.wait()
    inv_r, inv_i = adm[0, 0], adm[1, 0]
    steps = [product(inv_r, inv_i, adm[0, k], adm[1, k]) for k in range(1, 1 + LINKS)]
    blank = jnp.zeros((5, inv_r.shape[1]), F32)
    coefs = jnp.concatenate(
        [inv_r] + [s[0] for s in steps] + [inv_i] + [s[1] for s in steps] + [off[...].astype(F32), blank], axis=0
    )
    coef_ref[...] = coefs
    tiles = coefs.shape[1] // 128
    for v in range(tiles):
        group_ref[v * 8 : v * 8 + 8, :] = grouped(coefs[:8, v * 128 : v * 128 + 128])
        spans[v * 8 : v * 8 + 8, :] = grouped(coefs[8:, v * 128 : v * 128 + 128])
    first, last = coefs[:, :128], coefs[:, tiles * 128 - 128 :]
    is_even = even("bus")
    a_ref[...] = jnp.where(is_even, last, first)
    b_ref[...] = jnp.where(is_even, first, last)

    for copy in copies[2:6]:
        copy.wait()
    for c in range(CONV):
        lanes = slice(c * 128, c * 128 + 128)
        aux_ref[0:1, lanes] = jnp.full((1, 128), steep[kind[c]], F32)
        aux_ref[1:2, lanes] = power[c : c + 1, :]
    lane = iota((1, 128), 1)
    harm = lax.axis_index("harm")
    column = lax.rem(harm, HALF)
    mark = jnp.zeros((1, 128), F32)
    start = jnp.full((1, 128), SUB, F32)
    for c in range(CONV):
        number = lax.rem(bus[c], SUB).astype(F32)
        mark += jnp.where(lane == c * HALF + column, number, 0.0)
        start += jnp.where(lane % 64 // 16 == c, number, 0.0)
    aux_ref[2:3, :128] = mark
    aux_ref[3:4, :128] = start
    aux_ref[4:5, :128] = spans[pl.ds(harm, 1), :]
    aux_ref[5:6, :128] = spans[pl.ds(harm + jnp.where(even("harm"), 1, -1), 1), :]
    for copy in copies[6:]:
        copy.wait()


def convert_kernel(volt_ref, turned_ref, basis_ref, aux_ref, group_ref, out_ref, volts, rows):
    volts[...] = volt_ref[...].astype(F32)
    kinds = 2 * H
    volt = jnp.concatenate(
        [volts[pl.ds(c, kinds, stride=CONV), :] for c in range(CONV)], axis=1
    ).astype(BF16)
    steep, power = aux_ref[0:1, :], aux_ref[1:2, :]
    spectra = jnp.zeros((kinds, CONV * 128), F32)
    step = 256
    for n in range(0, NT, step):
        wave = jnp.dot(turned_ref[n : n + step, :], volt, preferred_element_type=F32)
        current = (power * jnp.tanh(steep * wave)).astype(BF16)
        spectra += jnp.dot(basis_ref[:, n : n + step], current, preferred_element_type=F32)
    spectra = spectra * NT ** (-0.5)
    for c in range(CONV):
        for p in range(2):
            rows[pl.ds(2 * c + p, H, stride=ROWS), :] = spectra[p * H : p * H + H, c * 128 : c * 128 + 128]
    group = group_ref[...]
    pair = jnp.where(iota((H, 128), 0) % 2 == 0, pltpu.roll(group, H - 1, 0), pltpu.roll(group, 1, 0))
    rows[pl.ds(COEF, H, stride=ROWS), :] = group
    rows[pl.ds(PAIR, H, stride=ROWS), :] = pair
    rows[pl.ds(SPAN, H, stride=ROWS), :] = jnp.broadcast_to(aux_ref[4:5, :128], (H, 128))
    rows[pl.ds(MARK, H, stride=ROWS), :] = jnp.broadcast_to(aux_ref[2:3, :128], (H, 128))
    out_ref[...] = rows[...].astype(BF16)


def low_high(a, b):
    is_even = even("bus")
    return jnp.where(is_even, b, a), jnp.where(is_even, a, b)


def sweeps_matrix(coefs):
    coefs = pltpu.roll(coefs, 3 * TILE - (TILE - EDGE), 1)[:, :WIN]
    rows = iota((WIN, WIN), 0)
    lanes = iota((1, WIN), 1)
    turned_r = jnp.zeros((WIN, WIN), F32)
    turned_i = jnp.zeros((WIN, WIN), F32)
    for k in range(LINKS):
        here = rows == lanes + coefs[8 + k : 9 + k].astype(I32)
        turned_r += jnp.where(here, coefs[1 + k : 2 + k], 0.0)
        turned_i += jnp.where(here, coefs[5 + k : 6 + k], 0.0)
    step_r, step_i = turned_r.T, turned_i.T
    mid_r, mid_i = step_r[EDGE : EDGE + TILE], step_i[EDGE : EDGE + TILE]
    twice = jnp.dot(
        jnp.concatenate([mid_r, mid_i], axis=0).astype(BF16),
        jnp.concatenate([step_r, step_i], axis=1).astype(BF16),
        preferred_element_type=F32,
    )
    same = iota((TILE, WIN), 0) + EDGE == iota((TILE, WIN), 1)
    all_r = twice[:TILE, :WIN] - twice[TILE:, WIN:] + mid_r + jnp.where(same, 1.0, 0.0)
    all_i = twice[:TILE, WIN:] + twice[TILE:, :WIN] + mid_i
    q_r, q_i = product(all_r, all_i, coefs[0:1], coefs[4:5])
    return jnp.concatenate([q_r, q_i], axis=0).astype(BF16)


def sweeps_kernel(coef_ref, q_ref):
    for b in range(q_ref.shape[0]):
        q_ref[b] = sweeps_matrix(coef_ref[:, b * TILE : (b + 3) * TILE])


def mix_kernel(got_ref, mine_ref, a_ref, b_ref, range_ref, out_a_ref, out_b_ref):
    shape = got_ref.shape
    got = got_ref[...].astype(F32)
    here = iota(shape, 0) % ROWS == COEF
    range_ref[...] = jnp.where(here, got, mine_ref[...].astype(F32)).astype(BF16)
    first, last = got[:16], got[shape[0] - 16 :]
    last = pltpu.roll(last, ROWS, 0)
    is_even = even("bus")
    out_a_ref[:16, :] = jnp.where(is_even, last, first)
    out_b_ref[:16, :] = jnp.where(is_even, first, last)
    out_a_ref[16:, :] = a_ref[...]
    out_b_ref[16:, :] = b_ref[...]


def network_kernel(got_ref, a_ref, b_ref, q_ref, coef_ref, volt_ref, rows, inject):
    rows[...] = got_ref[...].astype(F32)
    is_even = even("bus")
    low = jnp.where(is_even, b_ref[...], a_ref[...])
    high = jnp.where(is_even, a_ref[...], b_ref[...])

    def part(p):
        return jnp.concatenate(
            [
                rows[pl.ds(h * HALF * ROWS + 2 * c + p, HALF, stride=ROWS), :]
                for h in range(2)
                for c in range(CONV)
            ],
            axis=0,
        )

    spectra = jnp.concatenate([part(0), part(1)], axis=1).astype(BF16)
    convs = H * CONV
    at = [
        jnp.sum(rows[pl.ds(h * HALF * ROWS + MARK, HALF, stride=ROWS), :], axis=0, keepdims=True)
        for h in range(2)
    ]
    at = jnp.concatenate(at, axis=1).astype(I32)
    lane = iota((1, convs), 1)
    source = lane // (CONV * HALF) * HALF + lane % HALF
    target = source * SUB + at
    buses = H * SUB
    owner = jnp.where(iota((buses, convs), 0) == target, 1.0, 0.0).astype(BF16)
    inject[EDGE : EDGE + buses, :] = jnp.dot(owner, spectra, preferred_element_type=F32).astype(BF16)
    for edge, lane0, row0 in ((low, HALF - 1, 0), (high, 0, EDGE + buses)):
        total_r = jnp.zeros((SUB, 128), F32)
        total_i = jnp.zeros((SUB, 128), F32)
        for c in range(CONV):
            at = c * HALF + lane0
            bus = jnp.broadcast_to(edge[MARK : MARK + 1, at : at + 1], (SUB, 128)).astype(I32)
            here = iota((SUB, 128), 0) == bus
            total_r += jnp.where(here, edge[2 * c : 2 * c + 1, :], 0.0)
            total_i += jnp.where(here, edge[2 * c + 1 : 2 * c + 2, :], 0.0)
        inject[row0 : row0 + EDGE, :] = jnp.concatenate([total_r, total_i], axis=1).astype(BF16)
    tail = 2 * EDGE + buses
    inject[tail:, :] = jnp.zeros((inject.shape[0] - tail, 256), BF16)
    tiles = buses // TILE
    for b in range(tiles):
        if b == 0:
            matrix = sweeps_matrix(jnp.concatenate([low[16:], coef_ref[:, : 2 * TILE]], axis=1))
        elif b == tiles - 1:
            matrix = sweeps_matrix(jnp.concatenate([coef_ref[:, buses - 2 * TILE :], high[16:]], axis=1))
        else:
            matrix = q_ref[b - 1]
        acc = jnp.dot(matrix, inject[b * TILE : b * TILE + WIN, :], preferred_element_type=F32)
        volt_ref[0, 0, b * TILE : b * TILE + TILE, :] = (acc[:TILE, :128] - acc[TILE:, 128:]).astype(BF16)
        volt_ref[1, 0, b * TILE : b * TILE + TILE, :] = (acc[:TILE, 128:] + acc[TILE:, :128]).astype(BF16)


def swapped(x):
    return pltpu.roll(x, 64, 1)


def packed_product(a, b, real):
    turned = swapped(b)
    return a * jnp.where(real, b, turned) + swapped(a) * jnp.where(real, -turned, b)


def lift_kernel(mine_ref, a_ref, spec_ref, mark_ref, rows):
    size = mine_ref.shape[0]
    rows[:size, :] = mine_ref[...].astype(F32)
    rows[size:, :] = a_ref[...].astype(F32)
    for q in range(2):
        for o in range(2 * CONV):
            at = (q * 2 * CONV + o) * H
            spec_ref[at : at + H, :] = rows[pl.ds(q * size + o, H, stride=ROWS), :]
        mark_ref[q : q + 1, :] = rows[q * size + MARK : q * size + MARK + 1, :]


def near_kernel(aux_ref, got_ref, spec_ref, mark_ref, b_ref, out_ref, coefs, rows, out):
    coefs[...] = got_ref[...].astype(F32)
    rows[...] = b_ref[...].astype(F32)
    harm = lax.axis_index("harm")
    is_even = even("harm")
    a_at = jnp.where(is_even, 2, 0)
    b_at = 2 - a_at

    shape = (8, 128)
    lane = iota(shape, 1)
    real = lane < 64
    path = lane % 16
    spans = [aux_ref[4:5, :128], aux_ref[5:6, :128], rows[SPAN : SPAN + 1, :]]
    spans = [jnp.broadcast_to(x, shape).astype(I32) for x in spans]

    def place(bus, line):
        at = bus // SUB
        slot = jnp.where(at == 1, 0, jnp.where(at == a_at, 1, 2))
        return slot, line * SUB + bus % SUB

    def hop(bus, line):
        slot, at = place(bus, jnp.maximum(line - 1, 0))
        found = [jnp.take_along_axis(x, at, axis=1) for x in spans]
        far = jnp.where(slot == 0, found[0], jnp.where(slot == 1, found[1], found[2]))
        return bus + jnp.where(line == 0, 0, far)

    def coef_at(bus, line, used):
        slot, at = place(bus, line)
        return jnp.where(used, slot * 128 + at + jnp.where(real, 0, 64), -1)[:1]

    bus0 = jnp.broadcast_to(aux_ref[3:4, :128], shape).astype(I32)
    valid = path < 1 + LINKS + LINKS * LINKS
    two = (path >= 1 + LINKS) & valid
    line1 = jnp.where(two, 1 + (path - 1 - LINKS) // LINKS, jnp.where(valid, path, 0))
    line2 = jnp.where(two, 1 + (path - 1 - LINKS) % LINKS, 0)
    bus1 = hop(bus0, line1)
    bus2 = hop(bus1, line2)
    places = [coef_at(bus0, line1, valid & (path >= 1)), coef_at(bus1, line2, two), coef_at(bus2, 0, valid)]
    pick = jnp.where(iota((3 * 128, 3 * 128), 0) == jnp.concatenate(places, axis=1), 1.0, 0.0).astype(BF16)
    window = jnp.concatenate(
        [
            coefs[pl.ds(COEF, H, stride=ROWS), :],
            coefs[pl.ds(PAIR, H, stride=ROWS), :],
            rows[pl.ds(COEF, H, stride=ROWS), :],
        ],
        axis=1,
    ).astype(BF16)
    found = jnp.dot(window, pick, preferred_element_type=F32)
    real, path = real[:1], path[:1]
    first = found[:, :128] + jnp.where(real & (path == 0), 1.0, 0.0)
    second = found[:, 128:256] + jnp.where(real & (path <= LINKS), 1.0, 0.0)
    weight = packed_product(packed_product(first, second, real), found[:, 256:], real)

    many = (128, 128)
    row = iota(many, 0)
    other = row % 64 % (3 * CONV)
    bus_of = jnp.zeros(many, I32)
    marks = [mark_ref[0:1, :], mark_ref[1:2, :], rows[MARK : MARK + 1, :]]
    beside = jnp.where(is_even, 1, -1)
    for q, (at, column) in enumerate(((1, harm), (a_at, harm + beside), (b_at, harm - beside))):
        column = lax.rem(column + HALF, HALF)
        for c in range(CONV):
            bus = jnp.sum(jnp.where(iota((1, 128), 1) == c * HALF + column, marks[q], 0.0), axis=1, keepdims=True)
            bus = jnp.broadcast_to(bus.astype(I32), many) + at * SUB
            bus_of = jnp.where(other == q * CONV + c, bus, bus_of)
    wide = iota(many, 1)
    match = (row // 64 == wide // 64) & (row % 64 // (3 * CONV) == wide % 64 // 16) & (bus_of == bus2[:1])
    match = jnp.where(match, 1.0, 0.0).astype(BF16)
    high = weight.astype(BF16)
    rest = (weight - high.astype(F32)).astype(BF16)
    dims = (((1,), (1,)), ((), ()))
    table = lax.dot_general(high, match, dims, preferred_element_type=F32)
    table += lax.dot_general(rest, match, dims, preferred_element_type=F32)

    total = [[jnp.zeros((H, 128), F32) for _ in range(2)] for _ in range(CONV)]
    for q in range(3):
        for o in range(CONV):
            if q < 2:
                at = (q * CONV + o) * 2 * H
                spec_r, spec_i = spec_ref[at : at + H, :], spec_ref[at + H : at + 2 * H, :]
            else:
                spec_r, spec_i = (rows[pl.ds(2 * o + p, H, stride=ROWS), :] for p in range(2))
            for c in range(CONV):
                at = c * 3 * CONV + q * CONV + o
                add_r, add_i = product(table[:, at : at + 1], table[:, 64 + at : 65 + at], spec_r, spec_i)
                total[c][0] += add_r
                total[c][1] += add_i
    for c in range(CONV):
        for p in range(2):
            out[pl.ds(p * H * CONV + c, H, stride=CONV), :] = total[c][p]
    out_ref[...] = out[...].astype(BF16)


VMEM = pl.BlockSpec(memory_space=pltpu.VMEM)
HBM = pl.BlockSpec(memory_space=pltpu.HBM)


def call(kernel, name, out_shape, in_specs, scratch=(), cost=(0, 0, 0)):
    flops, moved, hard = cost
    return pl.pallas_call(
        kernel,
        out_shape=out_shape,
        in_specs=in_specs,
        out_specs=jax.tree.map(lambda _: VMEM, out_shape),
        scratch_shapes=list(scratch),
        compiler_params=pltpu.CompilerParams(vmem_limit_bytes=40 * 2**20),
        cost_estimate=pl.CostEstimate(flops=flops, bytes_accessed=moved, transcendentals=hard),
        name=name,
    )


def swaps(count):
    rounds = []
    for start in (0, 1):
        firsts = range(start, count - 1, 2)
        rounds.append([(i, i + 1) for i in firsts] + [(i + 1, i) for i in firsts])
    return rounds


def local(conv_volt, conv_power, conv_type, type_steep, conv_bus, admittance, link_offset):
    harm_count = lax.axis_size("harm")
    bus_count = lax.axis_size("bus")
    block = admittance.shape[3]
    snapshots = conv_volt.shape[3]
    tiles = block // TILE
    size = harm_count * ROWS
    kinds = 2 * H
    S = jax.ShapeDtypeStruct
    over_bus = swaps(bus_count)
    number = lambda r: r % harm_count * bus_count + r // harm_count
    over_ranges = [[(number(s), number(d)) for s, d in pairs] for pairs in swaps(harm_count * bus_count)]

    basis = make_basis()
    coef, edge_a, edge_b, aux, group, volt, turned, basis = call(
        prepare_kernel,
        "prepare",
        (
            S((16, block), F32),
            S((16, 128), F32),
            S((16, 128), F32),
            S((8, CONV * 128), F32),
            S((harm_count, 128), F32),
            S((kinds * CONV, snapshots), BF16),
            S((NT, kinds), BF16),
            S((kinds, NT), BF16),
        ),
        [HBM] * 9,
        [
            pltpu.VMEM((2, 4, 1, block), F32),
            pltpu.VMEM((LINKS, block), I32),
            pltpu.SMEM((CONV,), I32),
            pltpu.SMEM(type_steep.shape, F32),
            pltpu.SMEM((CONV,), I32),
            pltpu.VMEM((CONV, snapshots), F32),
            pltpu.VMEM((harm_count, 128), F32),
            pltpu.SemaphoreType.DMA((9,)),
        ],
    )(
        *(
            pltpu.with_memory_space_constraint(array, pltpu.HBM)
            for array in (
                admittance,
                link_offset,
                conv_type,
                type_steep,
                conv_bus,
                conv_power,
                conv_volt.reshape(kinds * CONV, snapshots),
                jnp.asarray(np.ascontiguousarray(basis.T)),
                jnp.asarray(basis),
            )
        )
    )
    payload = call(
        convert_kernel,
        "convert",
        S((size, 128), BF16),
        [VMEM] * 5,
        [pltpu.VMEM((kinds * CONV, 128), F32), pltpu.VMEM((size, 128), F32)],
        (2 * 2 * 128 * 1024 * 512, 2**20, 2**19),
    )(volt, turned, basis, aux, group)

    four = (harm_count, ROWS // 4, 4, snapshots)
    got = lax.all_to_all(payload.reshape(four), "harm", split_axis=0, concat_axis=0, tiled=True)

    beside_a = lax.ppermute(payload, ("harm", "bus"), over_ranges[0])
    q = call(
        sweeps_kernel,
        "sweeps",
        S((tiles - 2, 2 * TILE, WIN), BF16),
        [VMEM],
        cost=(2 * tiles * 256 * 256 * 512, 2**20, 0),
    )(coef)
    spec, mark = call(
        lift_kernel,
        "lift",
        (S((2 * 2 * CONV * H, 128), F32), S((8, 128), F32)),
        [VMEM] * 2,
        [pltpu.VMEM((2 * size, 128), F32)],
        (10**6, 2**20, 0),
    )(payload, beside_a)
    got, q, spec, mark = lax.optimization_barrier((got, q, spec, mark))

    got = got.reshape(size, snapshots)
    beside_b, halo_a, halo_b = call(
        mix_kernel, "mix", (S((size, 128), BF16), S((32, 128), F32), S((32, 128), F32)), [VMEM] * 4
    )(got, payload, edge_a, edge_b)
    beside_b = lax.ppermute(beside_b, ("harm", "bus"), over_ranges[1])
    halo_a = lax.ppermute(halo_a, "bus", over_bus[0])
    halo_b = lax.ppermute(halo_b, "bus", over_bus[1])
    near = call(
        near_kernel,
        "near",
        S((kinds * CONV, snapshots), BF16),
        [VMEM] * 5,
        [pltpu.VMEM((size, 128), F32), pltpu.VMEM((size, 128), F32), pltpu.VMEM((kinds * CONV, 128), F32)],
        (2 * 10**7, 2**20, 0),
    )(aux, got, spec, mark, beside_b)
    bus_volt = call(
        network_kernel,
        "network",
        S((2, 1, block, snapshots), BF16),
        [VMEM] * 5,
        [pltpu.VMEM((size, 128), F32), pltpu.VMEM((block + WIN - TILE, 256), BF16)],
        (2 * tiles * 256 * 256 * 256, 2**20, 0),
    )(got, halo_a, halo_b, q, coef)
    return (bus_volt, near.reshape(2, H, CONV, snapshots))


def solution(mesh):
    in_specs = (
        P(None, None, ("bus", "harm"), None),
        P(("bus", "harm"), None),
        P(("bus", "harm")),
        P(),
        P(("bus", "harm")),
        P(None, None, "harm", "bus"),
        P(None, "bus"),
    )
    out_specs = (P(None, "harm", "bus", None), P(None, None, ("bus", "harm"), None))
    return jax.shard_map(local, mesh=mesh, in_specs=in_specs, out_specs=out_specs, check_vma=False)
```

time: 52.8 us -> 49 us (0.928)
  the two profiles are of different devices: /device:TPU:24 before, /device:TPU:32 now
where the time goes in v4:
time: 49 us; the launch traced here: 48.7 us
  starting transfers between devices  24.3 us (50%)
  waiting for transfers between devices  12 us (24%)
  Pallas kernels  11.7 us (24%)
  between operations  0.7 us (1%)
    all_to_all x1, starting transfers between devices, local(): lax.all_to_all(payload.reshape(four), 'harm', split_axis=0, concat_axis=0...  13.8 us
    all_to_all x1, waiting for transfers between devices, local(): lax.all_to_all(payload.reshape(four), 'harm', split_axis=0, concat_axis=0...  7.1 us
    ppermute x1, waiting for transfers between devices, local(): halo_b = lax.ppermute(halo_b, 'bus', over_bus[1])  4.7 us
    ppermute x1, starting transfers between devices, local(): halo_a = lax.ppermute(halo_a, 'bus', over_bus[0])  3.48 us
    ppermute x1, starting transfers between devices, local(): beside_b = lax.ppermute(beside_b, ('harm', 'bus'), over_ranges[1])  3.16 us
    pallas_call x1, Pallas kernels, local(): call(near_kernel, 'near', S((kinds * CONV, snapshots), BF16), [VMEM] * 5,...  2.6 us
    pallas_call x1, Pallas kernels, local(): call(network_kernel, 'network', S((2, 1, block, snapshots), BF16), [VMEM]...  2.18 us
    ppermute x1, starting transfers between devices, local(): beside_a = lax.ppermute(payload, ('harm', 'bus'), over_ranges[0])  1.96 us
  transfers between devices with their start and end apart: 5, of which 3 were waited for; matrix products, arithmetic and copies ran while one was open for 0% of the time, Pallas kernels for 10%

profile of v4, /device:TPU:32, one launch (start us, length us, event | category | flops | bytes accessed | tf_op | source)
XLA Modules:
  0.0 48.7 jit_solution(6108673633078866487)
XLA Ops:
  0.6 1.2 %prepare.1 = (f32[16,1024]{1,0:T(8,128)S(1)}, f32[16,128]{1,0:T(8,128)S(1)}, f32[16,128]{1,0:T(8,128)S(1)}, f32[8,512]{1,0:T(8,128)S(1)}, f32[64,128]{1,0:T(8,12...) custom-call(f32[2,4,1,1024]{3,2,1,0:T(1,128)} %adm_hbm.1, ...), custom_call_target="tpu_custom_call" | custom-call | tf_op jit(solution)/shard_map/prepare/pallas_call | solution.py:393
  1.9 1.7 %convert.1.mine_ref = bf16[768,128]{1,0:T(8,128)(2,1)} custom-call(bf16[512,128]{1,0:T(8,128)(2,1)S(1)} %get-tuple-element.19.volt_ref, bf16[1024,128]{1,0:T(8,128)(2,1)S(1)} %get-tuple-element.20.turned_ref, bf16[128,1024]{1,0:T(8,128)(2,1)S(1)} %get-tuple-element.21.basis_ref, f32[8,512]{1,0:T(8,128)S(1)} %get-tuple-element.22.aux_ref, ...), custom_call_target="tpu_custom_call" | custom-call | flops 268435456 | bytes 1048576 | tf_op jit(solution)/shard_map/convert/pallas_call | solution.py:433
  3.6 13.8 %all-to-all-start = ((bf16[64,3,4,128]{3,2,1,0:T(4,128)(2,1)}), bf16[64,3,4,128]{3,2,1,0:T(4,128)(2,1)S(1)}, u32[]{:S(2)}, u32[]{:S(2)}) async-start(bf16[64,3,4,128]{3,2,1,0:T(4,128)(2,1)} %bitcast.1), calls=%async_computation | async-start | bytes 393216 | tf_op jit(solution)/shard_map/all_to_all | solution.py:443
  17.4 2.0 %collective-permute-start = (bf16[768,128]{1,0:T(8,128)(2,1)}, bf16[768,128]{1,0:T(8,128)(2,1)S(1)}, u32[]{:S(2)}, u32[]{:S(2)}) collective-permute-start(bf16[768,128]{1,0:T(8,128)(2,1)} %convert.1.mine_ref), channel_id=1, source_target_pairs={{0,8},{16,24},{32,40},{48,56},{64,72},{80,88},{96,104},{112,120},{... | collective-permute-start | bytes 589832 | tf_op jit(solution)/shard_map/ppermute | solution.py:445
  19.3 1.8 %sweeps.1.q_ref = bf16[6,256,256]{2,1,0:T(8,128)(2,1)S(1)} custom-call(f32[16,1024]{1,0:T(8,128)S(1)} %get-tuple-element.24.coef_ref), custom_call_target="tpu_custom_call" | custom-call | flops 536870912 | bytes 1048576 | tf_op jit(solution)/shard_map/sweeps/pallas_call | solution.py:446
  21.2 0.0 collective-permute-done.a_ref
  21.2 1.0 %lift.1 = (f32[1024,128]{1,0:T(8,128)S(1)}, f32[8,128]{1,0:T(8,128)S(1)}) custom-call(bf16[768,128]{1,0:T(8,128)(2,1)} %convert.1.mine_ref, bf16[768,128]{1,0:T(8,128)(2,1)S(1)} %collective-permute-done.a_ref), custom_call_target="tpu_custom_call" | custom-call | flops 1000000 | bytes 1048576 | tf_op jit(solution)/shard_map/lift/pallas_call | solution.py:453
  22.2 7.1 %all-to-all-done = bf16[64,3,4,128]{3,2,1,0:T(4,128)(2,1)S(1)} async-done(((bf16[64,3,4,128]{3,2,1,0:T(4,128)(2,1)}), bf16[64,3,4,128]{3,2,1,0:T(4,128)(2,1)S(1)}, u32[]{:S(2)}, u32[]{:S(2)}) %all-to-all-start) | async-done | bytes 196640 | tf_op jit(solution)/shard_map/all_to_all | solution.py:443
  29.3 1.1 %mix.1 = (bf16[768,128]{1,0:T(8,128)(2,1)S(1)}, f32[32,128]{1,0:T(8,128)S(1)}, f32[32,128]{1,0:T(8,128)S(1)}) custom-call(bf16[768,128]{1,0:T(8,128)(2,1)S(1)} %bitcast.4, bf16[768,128]{1,0:T(8,128)(2,1)} %convert.1.mine_ref, f32[16,128]{1,0:T(8,128)S(1)} %get-tuple-element.28.a_ref, f32[16,128]{1,0:T(8,128)S(1)} %get-tuple-element.29.b_ref), custom_call_target="tpu_custom_call" | custom-call | tf_op jit(solution)/shard_map/mix/pallas_call | solution.py:464
  30.4 3.2 %collective-permute-start.3 = (bf16[768,128]{1,0:T(8,128)(2,1)S(1)}, bf16[768,128]{1,0:T(8,128)(2,1)S(1)}, u32[]{:S(2)}, u32[]{:S(2)}) collective-permute-start(bf16[768,128]{1,0:T(8,128)(2,1)S(1)} %get-tuple-element.35), channel_id=1, source_target_pairs={{8,16},{24,32},{40,48},{56,64},{72,80},{88,96},{104,112},{120,128}... | collective-permute-start | bytes 589832 | tf_op jit(solution)/shard_map/ppermute | solution.py:467
  33.6 3.5 %collective-permute-start.1 = (f32[32,128]{1,0:T(8,128)S(1)}, f32[32,128]{1,0:T(8,128)S(1)}, u32[]{:S(2)}, u32[]{:S(2)}) collective-permute-start(f32[32,128]{1,0:T(8,128)S(1)} %get-tuple-element.30), channel_id=1, source_target_pairs={{0,1},{2,3},{4,5},{6,7},{1,0},{3,2},{5,4},{7,6},{8,9},{10,11},{12,... | collective-permute-start | bytes 49160 | tf_op jit(solution)/shard_map/ppermute | solution.py:468
  37.1 1.9 %collective-permute-start.2 = (f32[32,128]{1,0:T(8,128)S(1)}, f32[32,128]{1,0:T(8,128)S(1)}, u32[]{:S(2)}, u32[]{:S(2)}) collective-permute-start(f32[32,128]{1,0:T(8,128)S(1)} %get-tuple-element.31), channel_id=1, source_target_pairs={{1,2},{3,4},{5,6},{2,1},{4,3},{6,5},{9,10},{11,12},{13,14},{10,9},... | collective-permute-start | bytes 49160 | tf_op jit(solution)/shard_map/ppermute | solution.py:469
  39.0 0.2 collective-permute-done.1.a_ref
  39.2 4.7 %collective-permute-done.2.b_ref = f32[32,128]{1,0:T(8,128)S(1)} collective-permute-done((f32[32,128]{1,0:T(8,128)S(1)}, f32[32,128]{1,0:T(8,128)S(1)}, u32[]{:S(2)}, u32[]{:S(2)}) %collective-permute-start.2) | collective-permute-done | bytes 16416 | tf_op jit(solution)/shard_map/ppermute | solution.py:469
  43.9 2.2 %network.1 = bf16[2,1,1024,128]{3,2,1,0:T(8,128)(2,1)} custom-call(bf16[768,128]{1,0:T(8,128)(2,1)S(1)} %bitcast.5, f32[32,128]{1,0:T(8,128)S(1)} %collective-permute-done.1.a_ref, f32[32,128]{1,0:T(8,128)S(1)} %collective-permute-done.2.b_ref, bf16[6,256,256]{2,1,0:T(8,128)(2,1)S(1)} %sweeps.1.q_ref, f32[16,1024]{1,0:T(8,128)S(1)} %get-tuple-element.24.coef_ref), custom_call_target="tpu_custom_call" | custom-call | flops 268435456 | bytes 1048576 | tf_op jit(solution)/shard_map/network/pallas_call | solution.py:478
  46.1 0.0 collective-permute-done.3.b_ref
  46.1 2.6 %near.1 = bf16[512,128]{1,0:T(8,128)(2,1)} custom-call(f32[8,512]{1,0:T(8,128)S(1)} %get-tuple-element.22.aux_ref, bf16[768,128]{1,0:T(8,128)(2,1)S(1)} %bitcast.6, f32[1024,128]{1,0:T(8,128)S(1)} %get-tuple-element.33.spec_ref, f32[8,128]{1,0:T(8,128)S(1)} %get-tuple-element.34.mark_ref, bf16[768,128]{1,0:T(8,128)(2,1)S(1)} %collective-permute-done.3.b_ref), custom_call_target="tpu_custom_call" | custom-call | flops 20000000 | bytes 1048576 | tf_op jit(solution)/shard_map/near/pallas_call | solution.py:470
Async XLA Ops:
  3.6 25.7 %all-to-all-start = ((bf16[64,3,4,128]{3,2,1,0:T(4,128)(2,1)}), bf16[64,3,4,128]{3,2,1,0:T(4,128)(2,1)S(1)}, u32[]{:S(2)}, u32[]{:S(2)}) async-start(bf16[64,3,4,128]{3,2,1,0:T(4,128)(2,1)} %bitcast.1), calls=%async_computation | async-start | bytes 393216 | tf_op jit(solution)/shard_map/all_to_all | solution.py:443
  17.4 3.8 %collective-permute-start = (bf16[768,128]{1,0:T(8,128)(2,1)}, bf16[768,128]{1,0:T(8,128)(2,1)S(1)}, u32[]{:S(2)}, u32[]{:S(2)}) collective-permute-start(bf16[768,128]{1,0:T(8,128)(2,1)} %convert.1.mine_ref), channel_id=1, source_target_pairs={{0,8},{16,24},{32,40},{48,56},{64,72},{80,88},{96,104},{112,120},{... | collective-permute-start | bytes 589832 | tf_op jit(solution)/shard_map/ppermute | solution.py:445
  30.4 15.7 %collective-permute-start.3 = (bf16[768,128]{1,0:T(8,128)(2,1)S(1)}, bf16[768,128]{1,0:T(8,128)(2,1)S(1)}, u32[]{:S(2)}, u32[]{:S(2)}) collective-permute-start(bf16[768,128]{1,0:T(8,128)(2,1)S(1)} %get-tuple-element.35), channel_id=1, source_target_pairs={{8,16},{24,32},{40,48},{56,64},{72,80},{88,96},{104,112},{120,128}... | collective-permute-start | bytes 589832 | tf_op jit(solution)/shard_map/ppermute | solution.py:467
  33.6 5.6 %collective-permute-start.1 = (f32[32,128]{1,0:T(8,128)S(1)}, f32[32,128]{1,0:T(8,128)S(1)}, u32[]{:S(2)}, u32[]{:S(2)}) collective-permute-start(f32[32,128]{1,0:T(8,128)S(1)} %get-tuple-element.30), channel_id=1, source_target_pairs={{0,1},{2,3},{4,5},{6,7},{1,0},{3,2},{5,4},{7,6},{8,9},{10,11},{12,... | collective-permute-start | bytes 49160 | tf_op jit(solution)/shard_map/ppermute | solution.py:468
  37.1 6.8 %collective-permute-start.2 = (f32[32,128]{1,0:T(8,128)S(1)}, f32[32,128]{1,0:T(8,128)S(1)}, u32[]{:S(2)}, u32[]{:S(2)}) collective-permute-start(f32[32,128]{1,0:T(8,128)S(1)} %get-tuple-element.31), channel_id=1, source_target_pairs={{1,2},{3,4},{5,6},{2,1},{4,3},{6,5},{9,10},{11,12},{13,14},{10,9},... | collective-permute-start | bytes 49160 | tf_op jit(solution)/shard_map/ppermute | solution.py:469

commit v5 on v4

v5 whole, which is shorter than its diff:
```python
import math

import jax
import jax.numpy as jnp
import numpy as np
from jax import lax
from jax.experimental import pallas as pl
from jax.experimental.pallas import tpu as pltpu
from jax.sharding import PartitionSpec as P

H = 64
NT = 1024
REACH = 8
LINKS = 3
SUB = 16
CONV = 4
EDGE = 2 * REACH
TILE = 128
WIN = 256
ROWS = 12
COEF = 8
PAIR = 9
SPAN = 10
MARK = 11
LIFT = 8 * H
HALF = 32
F32 = jnp.float32
BF16 = jnp.bfloat16
I32 = jnp.int32


def make_basis():
    turn = np.arange(1, H + 1)[:, None] * np.arange(NT)[None, :] % NT
    angle = turn * (2.0 * math.pi / NT)
    return np.concatenate([np.cos(angle), -np.sin(angle)], axis=0).astype(BF16)


def iota(shape, dim):
    return lax.broadcasted_iota(I32, shape, dim)


def product(ar, ai, br, bi):
    return ar * br - ai * bi, ar * bi + ai * br


def grouped(x):
    k, j = iota((8, 128), 0), iota((8, 128), 1) // SUB
    for s in (1, 2, 4):
        later = pltpu.roll(pltpu.roll(x, s, 0), 128 - SUB * s, 1)
        sooner = pltpu.roll(pltpu.roll(x, 8 - s, 0), SUB * s, 1)
        bk, bj = (k // s) % 2, (j // s) % 2
        x = jnp.where(bk == bj, x, jnp.where(bk == 1, later, sooner))
    return x


def even(axis):
    return lax.rem(lax.axis_index(axis), 2) == 0


def begin_kernel(
    adm_hbm, off_hbm, type_hbm, steep_hbm, bus_hbm, power_hbm, volt_hbm, turned_hbm, basis_hbm,
    coef_ref, a_ref, b_ref, aux_ref, out_ref, lift_ref,
    adm, off, kind, steep, bus, power, volt_in, turned, basis, volts, groups, spans, rows, sems,
):
    pairs = [
        (adm_hbm, adm), (off_hbm, off), (type_hbm, kind), (steep_hbm, steep), (bus_hbm, bus), (power_hbm, power),
        (volt_hbm, volt_in), (turned_hbm, turned), (basis_hbm, basis),
    ]
    copies = [pltpu.make_async_copy(src, dst, sems.at[i]) for i, (src, dst) in enumerate(pairs)]
    for copy in copies:
        copy.start()
    for copy in copies[:2]:
        copy.wait()
    inv_r, inv_i = adm[0, 0], adm[1, 0]
    steps = [product(inv_r, inv_i, adm[0, k], adm[1, k]) for k in range(1, 1 + LINKS)]
    blank = jnp.zeros((5, inv_r.shape[1]), F32)
    coefs = jnp.concatenate(
        [inv_r] + [s[0] for s in steps] + [inv_i] + [s[1] for s in steps] + [off[...].astype(F32), blank], axis=0
    )
    coef_ref[...] = coefs
    tiles = coefs.shape[1] // 128
    for v in range(tiles):
        groups[v * 8 : v * 8 + 8, :] = grouped(coefs[:8, v * 128 : v * 128 + 128])
        spans[v * 8 : v * 8 + 8, :] = grouped(coefs[8:, v * 128 : v * 128 + 128])
    first, last = coefs[:, :128], coefs[:, tiles * 128 - 128 :]
    is_even = even("bus")
    a_ref[...] = jnp.where(is_even, last, first)
    b_ref[...] = jnp.where(is_even, first, last)
    harm = lax.axis_index("harm")
    span = spans[pl.ds(harm, 1), :]
    aux_ref[1:2, :] = span
    aux_ref[2:3, :] = spans[pl.ds(harm + jnp.where(even("harm"), 1, -1), 1), :]
    group = groups[...]
    pair = jnp.where(iota((H, 128), 0) % 2 == 0, pltpu.roll(group, H - 1, 0), pltpu.roll(group, 1, 0))
    rows[pl.ds(COEF, H, stride=ROWS), :] = group
    rows[pl.ds(PAIR, H, stride=ROWS), :] = pair
    rows[pl.ds(SPAN, H, stride=ROWS), :] = jnp.broadcast_to(span, (H, 128))

    for copy in copies[2:]:
        copy.wait()
    lane = iota((1, 128), 1)
    column = lax.rem(harm, HALF)
    mark = jnp.zeros((1, 128), F32)
    start = jnp.full((1, 128), SUB, F32)
    for c in range(CONV):
        number = lax.rem(bus[c], SUB).astype(F32)
        mark += jnp.where(lane == c * HALF + column, number, 0.0)
        start += jnp.where(lane % 64 // 16 == c, number, 0.0)
    aux_ref[0:1, :] = start
    rows[pl.ds(MARK, H, stride=ROWS), :] = jnp.broadcast_to(mark, (H, 128))

    volts[...] = volt_in[...].astype(F32)
    kinds = 2 * H
    volt = jnp.concatenate(
        [volts[pl.ds(c, kinds, stride=CONV), :] for c in range(CONV)], axis=1
    ).astype(BF16)
    sharp = jnp.concatenate([jnp.full((1, 128), steep[kind[c]], F32) for c in range(CONV)], axis=1)
    strong = jnp.concatenate([power[c : c + 1, :] for c in range(CONV)], axis=1)
    spectra = jnp.zeros((kinds, CONV * 128), F32)
    step = 256
    for n in range(0, NT, step):
        wave = jnp.dot(turned[n : n + step, :], volt, preferred_element_type=F32)
        current = (strong * jnp.tanh(sharp * wave)).astype(BF16)
        spectra += jnp.dot(basis[:, n : n + step], current, preferred_element_type=F32)
    spectra = spectra * NT ** (-0.5)
    for c in range(CONV):
        for p in range(2):
            piece = spectra[p * H : p * H + H, c * 128 : c * 128 + 128]
            at = (2 * c + p) * H
            rows[pl.ds(2 * c + p, H, stride=ROWS), :] = piece
            lift_ref[at : at + H, :] = piece.astype(BF16)
    row = iota((16, 128), 0)
    notes = jnp.where(row == 0, span, jnp.where(row == 1, mark, 0.0))
    lift_ref[LIFT:, :] = notes.astype(BF16)
    out_ref[...] = rows[...].astype(BF16)


def sweeps_matrix(coefs):
    coefs = pltpu.roll(coefs, 3 * TILE - (TILE - EDGE), 1)[:, :WIN]
    rows = iota((WIN, WIN), 0)
    lanes = iota((1, WIN), 1)
    turned_r = jnp.zeros((WIN, WIN), F32)
    turned_i = jnp.zeros((WIN, WIN), F32)
    for k in range(LINKS):
        here = rows == lanes + coefs[8 + k : 9 + k].astype(I32)
        turned_r += jnp.where(here, coefs[1 + k : 2 + k], 0.0)
        turned_i += jnp.where(here, coefs[5 + k : 6 + k], 0.0)
    step_r, step_i = turned_r.T, turned_i.T
    mid_r, mid_i = step_r[EDGE : EDGE + TILE], step_i[EDGE : EDGE + TILE]
    twice = jnp.dot(
        jnp.concatenate([mid_r, mid_i], axis=0).astype(BF16),
        jnp.concatenate([step_r, step_i], axis=1).astype(BF16),
        preferred_element_type=F32,
    )
    same = iota((TILE, WIN), 0) + EDGE == iota((TILE, WIN), 1)
    all_r = twice[:TILE, :WIN] - twice[TILE:, WIN:] + mid_r + jnp.where(same, 1.0, 0.0)
    all_i = twice[:TILE, WIN:] + twice[TILE:, :WIN] + mid_i
    q_r, q_i = product(all_r, all_i, coefs[0:1], coefs[4:5])
    return jnp.concatenate([q_r, q_i], axis=0).astype(BF16)


def sweeps_kernel(coef_ref, q_ref):
    for b in range(q_ref.shape[0]):
        q_ref[b] = sweeps_matrix(coef_ref[:, b * TILE : (b + 3) * TILE])


def mix_kernel(got_ref, lift_ref, a_ref, b_ref, rows_ref, range_ref, out_a_ref, out_b_ref):
    size = got_ref.shape[0]
    rows_ref[...] = got_ref[...].astype(F32)
    range_ref[: LIFT + 16, :] = lift_ref[...]
    range_ref[LIFT + 16 :, :] = rows_ref[pl.ds(COEF, H, stride=ROWS), :].astype(BF16)
    first, last = rows_ref[:16, :], pltpu.roll(rows_ref[size - 16 :, :], ROWS, 0)
    is_even = even("bus")
    out_a_ref[:16, :] = jnp.where(is_even, last, first)
    out_b_ref[:16, :] = jnp.where(is_even, first, last)
    out_a_ref[16:, :] = a_ref[...]
    out_b_ref[16:, :] = b_ref[...]


def volt_of(matrix, inject):
    acc = jnp.dot(matrix, inject, preferred_element_type=F32)
    return (acc[:TILE, :128] - acc[TILE:, 128:]).astype(BF16), (acc[:TILE, 128:] + acc[TILE:, :128]).astype(BF16)


def inner_network(rows, q_ref, inject, volt, volt_hbm, sems):
    def part(p):
        return jnp.concatenate(
            [
                rows[pl.ds(h * HALF * ROWS + 2 * c + p, HALF, stride=ROWS), :]
                for h in range(2)
                for c in range(CONV)
            ],
            axis=0,
        )

    spectra = jnp.concatenate([part(0), part(1)], axis=1).astype(BF16)
    convs = H * CONV
    at = [
        jnp.sum(rows[pl.ds(h * HALF * ROWS + MARK, HALF, stride=ROWS), :], axis=0, keepdims=True)
        for h in range(2)
    ]
    at = jnp.concatenate(at, axis=1).astype(I32)
    lane = iota((1, convs), 1)
    source = lane // (CONV * HALF) * HALF + lane % HALF
    target = source * SUB + at
    buses = H * SUB
    owner = jnp.where(iota((buses, convs), 0) == target, 1.0, 0.0).astype(BF16)
    inject[...] = jnp.dot(owner, spectra, preferred_element_type=F32).astype(BF16)
    for b in range(1, buses // TILE - 1):
        window = inject[b * TILE - EDGE : b * TILE - EDGE + WIN, :]
        volt[0, 0, b * TILE : b * TILE + TILE, :], volt[1, 0, b * TILE : b * TILE + TILE, :] = volt_of(
            q_ref[b - 1], window
        )
    inner = pl.ds(TILE, buses - 2 * TILE)
    copies = [pltpu.make_async_copy(volt.at[p, 0, inner], volt_hbm.at[p, 0, inner], sems.at[p]) for p in range(2)]
    for copy in copies:
        copy.start()
    return copies


def edge_kernel(a_ref, b_ref, inject_ref, coef_ref, done_hbm, volt_hbm, volt, sems):
    del done_hbm
    is_even = even("bus")
    low = jnp.where(is_even, b_ref[...], a_ref[...])
    high = jnp.where(is_even, a_ref[...], b_ref[...])
    buses = inject_ref.shape[0]

    def injected(edge, lane0):
        total_r = jnp.zeros((SUB, 128), F32)
        total_i = jnp.zeros((SUB, 128), F32)
        for c in range(CONV):
            at = c * HALF + lane0
            bus = jnp.broadcast_to(edge[MARK : MARK + 1, at : at + 1], (SUB, 128)).astype(I32)
            here = iota((SUB, 128), 0) == bus
            total_r += jnp.where(here, edge[2 * c : 2 * c + 1, :], 0.0)
            total_i += jnp.where(here, edge[2 * c + 1 : 2 * c + 2, :], 0.0)
        return jnp.concatenate([total_r, total_i], axis=1).astype(BF16)

    rest = WIN - TILE - 2 * EDGE
    windows = [
        jnp.concatenate([injected(low, HALF - 1), inject_ref[: WIN - EDGE, :]], axis=0),
        jnp.concatenate(
            [inject_ref[buses - TILE - EDGE :, :], injected(high, 0), jnp.zeros((rest, 256), BF16)], axis=0
        ),
    ]
    coefs = [
        jnp.concatenate([low[16:], coef_ref[:, : 2 * TILE]], axis=1),
        jnp.concatenate([coef_ref[:, buses - 2 * TILE :], high[16:]], axis=1),
    ]
    copies = []
    for e in range(2):
        volt[e, 0], volt[e, 1] = volt_of(sweeps_matrix(coefs[e]), windows[e])
        for p in range(2):
            place = volt_hbm.at[p, 0, pl.ds(e * (buses - TILE), TILE)]
            copies.append(pltpu.make_async_copy(volt.at[e, p], place, sems.at[2 * e + p]))
            copies[-1].start()
    for copy in copies:
        copy.wait()


def swapped(x):
    return pltpu.roll(x, 64, 1)


def packed_product(a, b, real):
    turned = swapped(b)
    return a * jnp.where(real, b, turned) + swapped(a) * jnp.where(real, -turned, b)


def solve_kernel(
    aux_ref, rows, mine_ref, a_ref, b_ref, q_ref, inject_ref, near_hbm, volt_hbm, near, volt, out, sems
):
    copies = inner_network(rows, q_ref, inject_ref, volt, volt_hbm, sems)
    near_converters(aux_ref, rows, (mine_ref, a_ref, b_ref), out)
    near[...] = out[...].astype(BF16)
    copies.append(pltpu.make_async_copy(near, near_hbm, sems.at[2]))
    copies[-1].start()
    for copy in copies:
        copy.wait()


def near_converters(aux_ref, rows, lifts, out):
    harm = lax.axis_index("harm")
    is_even = even("harm")
    a_at = jnp.where(is_even, 2, 0)
    b_at = 2 - a_at

    shape = (8, 128)
    lane = iota(shape, 1)
    real = lane < 64
    path = lane % 16
    notes = [ref[LIFT : LIFT + 16, :].astype(F32) for ref in lifts]
    spans = [aux_ref[1:2, :], aux_ref[2:3, :], notes[2][:1]]
    spans = [jnp.broadcast_to(x, shape).astype(I32) for x in spans]

    def place(bus, line):
        at = bus // SUB
        slot = jnp.where(at == 1, 0, jnp.where(at == a_at, 1, 2))
        return slot, line * SUB + bus % SUB

    def hop(bus, line):
        slot, at = place(bus, jnp.maximum(line - 1, 0))
        found = [jnp.take_along_axis(x, at, axis=1) for x in spans]
        far = jnp.where(slot == 0, found[0], jnp.where(slot == 1, found[1], found[2]))
        return bus + jnp.where(line == 0, 0, far)

    def coef_at(bus, line, used):
        slot, at = place(bus, line)
        return jnp.where(used, slot * 128 + at + jnp.where(real, 0, 64), -1)[:1]

    bus0 = jnp.broadcast_to(aux_ref[0:1, :], shape).astype(I32)
    valid = path < 1 + LINKS + LINKS * LINKS
    two = (path >= 1 + LINKS) & valid
    line1 = jnp.where(two, 1 + (path - 1 - LINKS) // LINKS, jnp.where(valid, path, 0))
    line2 = jnp.where(two, 1 + (path - 1 - LINKS) % LINKS, 0)
    bus1 = hop(bus0, line1)
    bus2 = hop(bus1, line2)
    places = [coef_at(bus0, line1, valid & (path >= 1)), coef_at(bus1, line2, two), coef_at(bus2, 0, valid)]
    pick = jnp.where(iota((3 * 128, 3 * 128), 0) == jnp.concatenate(places, axis=1), 1.0, 0.0).astype(BF16)
    window = jnp.concatenate(
        [
            rows[pl.ds(COEF, H, stride=ROWS), :].astype(BF16),
            rows[pl.ds(PAIR, H, stride=ROWS), :].astype(BF16),
            lifts[2][LIFT + 16 :, :],
        ],
        axis=1,
    )
    found = jnp.dot(window, pick, preferred_element_type=F32)
    real, path = real[:1], path[:1]
    first = found[:, :128] + jnp.where(real & (path == 0), 1.0, 0.0)
    second = found[:, 128:256] + jnp.where(real & (path <= LINKS), 1.0, 0.0)
    weight = packed_product(packed_product(first, second, real), found[:, 256:], real)

    many = (128, 128)
    row = iota(many, 0)
    other = row % 64 % (3 * CONV)
    bus_of = jnp.zeros(many, I32)
    marks = [x[1:2] for x in notes]
    beside = jnp.where(is_even, 1, -1)
    for q, (at, column) in enumerate(((1, harm), (a_at, harm + beside), (b_at, harm - beside))):
        column = lax.rem(column + HALF, HALF)
        for c in range(CONV):
            bus = jnp.sum(jnp.where(iota((1, 128), 1) == c * HALF + column, marks[q], 0.0), axis=1, keepdims=True)
            bus = jnp.broadcast_to(bus.astype(I32), many) + at * SUB
            bus_of = jnp.where(other == q * CONV + c, bus, bus_of)
    wide = iota(many, 1)
    match = (row // 64 == wide // 64) & (row % 64 // (3 * CONV) == wide % 64 // 16) & (bus_of == bus2[:1])
    match = jnp.where(match, 1.0, 0.0).astype(BF16)
    high = weight.astype(BF16)
    rest = (weight - high.astype(F32)).astype(BF16)
    dims = (((1,), (1,)), ((), ()))
    table = lax.dot_general(high, match, dims, preferred_element_type=F32)
    table += lax.dot_general(rest, match, dims, preferred_element_type=F32)

    total = [[jnp.zeros((H, 128), F32) for _ in range(2)] for _ in range(CONV)]
    for q in range(3):
        for o in range(CONV):
            spec_r, spec_i = (lifts[q][(2 * o + p) * H : (2 * o + p + 1) * H, :].astype(F32) for p in range(2))
            for c in range(CONV):
                at = c * 3 * CONV + q * CONV + o
                add_r, add_i = product(table[:, at : at + 1], table[:, 64 + at : 65 + at], spec_r, spec_i)
                total[c][0] += add_r
                total[c][1] += add_i
    for c in range(CONV):
        for p in range(2):
            out[pl.ds(p * H * CONV + c, H, stride=CONV), :] = total[c][p]


VMEM = pl.BlockSpec(memory_space=pltpu.VMEM)
HBM = pl.BlockSpec(memory_space=pltpu.HBM)


def call(kernel, name, out_shape, in_specs, scratch=(), cost=(0, 0, 0), out_specs=None, aliases=None):
    flops, moved, hard = cost
    return pl.pallas_call(
        kernel,
        out_shape=out_shape,
        in_specs=in_specs,
        out_specs=out_specs or jax.tree.map(lambda _: VMEM, out_shape),
        input_output_aliases=aliases or {},
        scratch_shapes=list(scratch),
        compiler_params=pltpu.CompilerParams(vmem_limit_bytes=40 * 2**20),
        cost_estimate=pl.CostEstimate(flops=flops, bytes_accessed=moved, transcendentals=hard),
        name=name,
    )


def swaps(count):
    rounds = []
    for start in (0, 1):
        firsts = range(start, count - 1, 2)
        rounds.append([(i, i + 1) for i in firsts] + [(i + 1, i) for i in firsts])
    return rounds


def local(conv_volt, conv_power, conv_type, type_steep, conv_bus, admittance, link_offset):
    harm_count = lax.axis_size("harm")
    bus_count = lax.axis_size("bus")
    block = admittance.shape[3]
    snapshots = conv_volt.shape[3]
    tiles = block // TILE
    size = harm_count * ROWS
    kinds = 2 * H
    S = jax.ShapeDtypeStruct
    over_bus = swaps(bus_count)
    number = lambda r: r % harm_count * bus_count + r // harm_count
    over_ranges = [[(number(s), number(d)) for s, d in pairs] for pairs in swaps(harm_count * bus_count)]

    basis = make_basis()
    coef, edge_a, edge_b, aux, payload, lift = call(
        begin_kernel,
        "begin",
        (
            S((16, block), F32),
            S((16, 128), F32),
            S((16, 128), F32),
            S((8, 128), F32),
            S((size, 128), BF16),
            S((LIFT + 16, 128), BF16),
        ),
        [HBM] * 9,
        [
            pltpu.VMEM((2, 4, 1, block), F32),
            pltpu.VMEM((LINKS, block), I32),
            pltpu.SMEM((CONV,), I32),
            pltpu.SMEM(type_steep.shape, F32),
            pltpu.SMEM((CONV,), I32),
            pltpu.VMEM((CONV, snapshots), F32),
            pltpu.VMEM((kinds * CONV, snapshots), BF16),
            pltpu.VMEM((NT, kinds), BF16),
            pltpu.VMEM((kinds, NT), BF16),
            pltpu.VMEM((kinds * CONV, snapshots), F32),
            pltpu.VMEM((harm_count, 128), F32),
            pltpu.VMEM((harm_count, 128), F32),
            pltpu.VMEM((size, 128), F32),
            pltpu.SemaphoreType.DMA((9,)),
        ],
        (2 * 2 * 128 * 1024 * 512, 2**20, 2**19),
    )(
        *(
            pltpu.with_memory_space_constraint(array, pltpu.HBM)
            for array in (
                admittance,
                link_offset,
                conv_type,
                type_steep,
                conv_bus,
                conv_power,
                conv_volt.reshape(kinds * CONV, snapshots),
                jnp.asarray(np.ascontiguousarray(basis.T)),
                jnp.asarray(basis),
            )
        )
    )

    four = (harm_count, ROWS // 4, 4, snapshots)
    got = lax.all_to_all(payload.reshape(four), "harm", split_axis=0, concat_axis=0, tiled=True)

    beside_a = lax.ppermute(lift, ("harm", "bus"), over_ranges[0])
    q = call(
        sweeps_kernel,
        "sweeps",
        S((tiles - 2, 2 * TILE, WIN), BF16),
        [VMEM],
        cost=(2 * tiles * 256 * 256 * 512, 2**20, 0),
    )(coef)
    got, q, beside_a = lax.optimization_barrier((got, q, beside_a))

    rows, beside_b, halo_a, halo_b = call(
        mix_kernel,
        "mix",
        (S((size, 128), F32), S((LIFT + 16 + H, 128), BF16), S((32, 128), F32), S((32, 128), F32)),
        [VMEM] * 4,
    )(got.reshape(size, snapshots), lift, edge_a, edge_b)
    beside_b = lax.ppermute(beside_b, ("harm", "bus"), over_ranges[1])
    halo_a = lax.ppermute(halo_a, "bus", over_bus[0])
    halo_b = lax.ppermute(halo_b, "bus", over_bus[1])
    out_volt = S((2, 1, block, snapshots), BF16)
    inject, near, bus_volt = call(
        solve_kernel,
        "solve",
        (S((block, 256), BF16), S((kinds * CONV, snapshots), BF16), out_volt),
        [VMEM] * 6,
        [
            pltpu.VMEM((kinds * CONV, snapshots), BF16),
            pltpu.VMEM((2, 1, block, snapshots), BF16),
            pltpu.VMEM((kinds * CONV, 128), F32),
            pltpu.SemaphoreType.DMA((3,)),
        ],
        (2 * tiles * 256 * 256 * 256, 2**20, 0),
        (VMEM, HBM, HBM),
    )(aux, rows, lift, beside_a, beside_b, q)
    halo_a, halo_b, near = lax.optimization_barrier((halo_a, halo_b, near))
    bus_volt = call(
        edge_kernel,
        "edge",
        out_volt,
        [VMEM] * 4 + [HBM],
        [pltpu.VMEM((2, 2, TILE, snapshots), BF16), pltpu.SemaphoreType.DMA((4,))],
        (4 * 256 * 256 * 512, 2**20, 0),
        HBM,
        {4: 0},
    )(halo_a, halo_b, inject, coef, bus_volt)
    return (bus_volt, near.reshape(2, H, CONV, snapshots))


def solution(mesh):
    in_specs = (
        P(None, None, ("bus", "harm"), None),
        P(("bus", "harm"), None),
        P(("bus", "harm")),
        P(),
        P(("bus", "harm")),
        P(None, None, "harm", "bus"),
        P(None, "bus"),
    )
    out_specs = (P(None, "harm", "bus", None), P(None, None, ("bus", "harm"), None))
    return jax.shard_map(local, mesh=mesh, in_specs=in_specs, out_specs=out_specs, check_vma=False)
```

time: 49 us -> 46.3 us (0.945)
  Pallas kernels: 11.7 us -> 9.5 us
  waiting for transfers between devices: 12 us -> 11.5 us
    ppermute x1, waiting for transfers between devices: 4.7 us -> 0.01 us  [local(): halo_b = lax.ppermute(halo_b, 'bus', over_bus[1])]
    ppermute x1, waiting for transfers between devices: 0.01 us -> 3.35 us  [local(): beside_b = lax.ppermute(beside_b, ('harm', 'bus'), over_ranges[1])]
    pallas_call x6 -> x4, Pallas kernels: 9.86 us -> 7.68 us  [the longest x1 2.95 us: local(): call(solve_kernel, 'solve', (S((block, 256), BF16), S((kinds * CONV, snap...]
    all_to_all x1, waiting for transfers between devices: 7.1 us -> 8.13 us  [local(): lax.all_to_all(payload.reshape(four), 'harm', split_axis=0, concat_axis=0...]
  transfers between devices with their start and end apart: 5 -> 5, of which waited for: 3 -> 2; matrix products, arithmetic and copies ran while one was open for 0% -> 0% of each run, Pallas kernels for 10% -> 10%
where the time goes in v5:
time: 46.3 us; the launch traced here: 46 us
  starting transfers between devices  24.3 us (52%)
  waiting for transfers between devices  11.5 us (25%)
  Pallas kernels  9.5 us (21%)
  between operations  0.72 us (2%)
    all_to_all x1, starting transfers between devices, local(): lax.all_to_all(payload.reshape(four), 'harm', split_axis=0, concat_axis=0...  13.8 us
    all_to_all x1, waiting for transfers between devices, local(): lax.all_to_all(payload.reshape(four), 'harm', split_axis=0, concat_axis=0...  8.13 us
    ppermute x1, starting transfers between devices, local(): halo_a = lax.ppermute(halo_a, 'bus', over_bus[0])  3.49 us
    ppermute x1, waiting for transfers between devices, local(): beside_b = lax.ppermute(beside_b, ('harm', 'bus'), over_ranges[1])  3.35 us
    ppermute x1, starting transfers between devices, local(): beside_b = lax.ppermute(beside_b, ('harm', 'bus'), over_ranges[1])  3.15 us
    pallas_call x1, Pallas kernels, local(): call(solve_kernel, 'solve', (S((block, 256), BF16), S((kinds * CONV, snap...  2.95 us
    pallas_call x1, Pallas kernels, local(): call(begin_kernel, 'begin', (S((16, block), F32), S((16, 128), F32), S((1...  2.92 us
    ppermute x1, starting transfers between devices, local(): beside_a = lax.ppermute(lift, ('harm', 'bus'), over_ranges[0])  1.96 us
  transfers between devices with their start and end apart: 5, of which 2 were waited for; matrix products, arithmetic and copies ran while one was open for 0% of the time, Pallas kernels for 10%

profile of v5, /device:TPU:32, one launch (start us, length us, event | category | flops | bytes accessed | tf_op | source)
XLA Modules:
  0.0 46.0 jit_solution(8956591286051462017)
XLA Ops:
  0.6 2.9 %begin.1 = (f32[16,1024]{1,0:T(8,128)S(1)}, f32[16,128]{1,0:T(8,128)S(1)}, f32[16,128]{1,0:T(8,128)S(1)}, f32[8,128]{1,0:T(8,128)S(1)}, bf16[768,128]{1,0:T(8,128)(2,1)}, /*index=5*/bf16[528,128]{1,0:T(8,128)(2,1)S(1)}) custom-call(f32[2,4,1,1024]{3,2,1,0:T(1,128)} %adm_hbm.1, s32[3,1024]{1,0:T(4,128)} %off_hbm.1, s32[4]{0:T(128)} %type_hbm.1, f32[8]{0:T(128)} %steep_hbm.1, ...), custom_call_target="tpu_custom_call" | custom-call | flops 268435456 | bytes 1048576 | tf_op jit(solution)/shard_map/begin/pallas_call | solution.py:410
  3.6 13.8 %all-to-all-start = ((bf16[64,3,4,128]{3,2,1,0:T(4,128)(2,1)}), bf16[64,3,4,128]{3,2,1,0:T(4,128)(2,1)S(1)}, u32[]{:S(2)}, u32[]{:S(2)}) async-start(bf16[64,3,4,128]{3,2,1,0:T(4,128)(2,1)} %bitcast.1), calls=%async_computation | async-start | bytes 393216 | tf_op jit(solution)/shard_map/all_to_all | solution.py:457
  17.4 2.0 %collective-permute-start = (bf16[528,128]{1,0:T(8,128)(2,1)S(1)}, bf16[528,128]{1,0:T(8,128)(2,1)S(1)}, u32[]{:S(2)}, u32[]{:S(2)}) collective-permute-start(bf16[528,128]{1,0:T(8,128)(2,1)S(1)} %get-tuple-element.23.lift_ref.mine_ref), channel_id=1, source_target_pairs={{0,8},{16,24},{32,40},{48,56},{64,72},{80,88},{96,104},{112,120},{... | collective-permute-start | bytes 405512 | tf_op jit(solution)/shard_map/ppermute | solution.py:459
  19.3 1.8 %sweeps.1.q_ref = bf16[6,256,256]{2,1,0:T(8,128)(2,1)S(1)} custom-call(f32[16,1024]{1,0:T(8,128)S(1)} %get-tuple-element.22.coef_ref), custom_call_target="tpu_custom_call" | custom-call | flops 536870912 | bytes 1048576 | tf_op jit(solution)/shard_map/sweeps/pallas_call | solution.py:460
  21.2 0.0 collective-permute-done.a_ref
  21.2 8.1 %all-to-all-done = bf16[64,3,4,128]{3,2,1,0:T(4,128)(2,1)S(1)} async-done(((bf16[64,3,4,128]{3,2,1,0:T(4,128)(2,1)}), bf16[64,3,4,128]{3,2,1,0:T(4,128)(2,1)S(1)}, u32[]{:S(2)}, u32[]{:S(2)}) %all-to-all-start) | async-done | bytes 196640 | tf_op jit(solution)/shard_map/all_to_all | solution.py:457
  29.3 3.1 %collective-permute-start.3 = (bf16[592,128]{1,0:T(8,128)(2,1)S(1)}, bf16[592,128]{1,0:T(8,128)(2,1)S(1)}, u32[]{:S(2)}, u32[]{:S(2)}) collective-permute-start(bf16[592,128]{1,0:T(8,128)(2,1)S(1)} %get-tuple-element.32), channel_id=1, source_target_pairs={{8,16},{24,32},{40,48},{56,64},{72,80},{88,96},{104,112},{120,128}... | collective-permute-start | bytes 454664 | tf_op jit(solution)/shard_map/ppermute | solution.py:475
  32.5 3.5 %collective-permute-start.1 = (f32[32,128]{1,0:T(8,128)S(1)}, f32[32,128]{1,0:T(8,128)S(1)}, u32[]{:S(2)}, u32[]{:S(2)}) collective-permute-start(f32[32,128]{1,0:T(8,128)S(1)} %get-tuple-element.27), channel_id=1, source_target_pairs={{0,1},{2,3},{4,5},{6,7},{1,0},{3,2},{5,4},{7,6},{8,9},{10,11},{12,... | collective-permute-start | bytes 49160 | tf_op jit(solution)/shard_map/ppermute | solution.py:476
  36.0 1.9 %collective-permute-start.2 = (f32[32,128]{1,0:T(8,128)S(1)}, f32[32,128]{1,0:T(8,128)S(1)}, u32[]{:S(2)}, u32[]{:S(2)}) collective-permute-start(f32[32,128]{1,0:T(8,128)S(1)} %get-tuple-element.28), channel_id=1, source_target_pairs={{1,2},{3,4},{5,6},{2,1},{4,3},{6,5},{9,10},{11,12},{13,14},{10,9},... | collective-permute-start | bytes 49160 | tf_op jit(solution)/shard_map/ppermute | solution.py:477
  37.9 3.4 %collective-permute-done.3.b_ref = bf16[592,128]{1,0:T(8,128)(2,1)S(1)} collective-permute-done((bf16[592,128]{1,0:T(8,128)(2,1)S(1)}, bf16[592,128]{1,0:T(8,128)(2,1)S(1)}, u32[]{:S(2)}, u32[]{:S(2)}) %collective-permute-start.3) | collective-permute-done | bytes 151584 | tf_op jit(solution)/shard_map/ppermute | solution.py:475
  41.3 2.9 %solve.1 = (bf16[1024,256]{1,0:T(8,128)(2,1)S(1)}, bf16[512,128]{1,0:T(8,128)(2,1)}, bf16[2,1,1024,128]{3,2,1,0:T(8,128)(2,1)}) custom-call(f32[8,128]{1,0:T(8,128)S(1)} %get-tuple-element.29.aux_ref, f32[768,128]{1,0:T(8,128)S(1)} %get-tuple-element.30.rows, bf16[528,128]{1,0:T(8,128)(2,1)S(1)} %get-tuple-element.23.lift_ref.mine_ref, ...), custom_call_target="tpu_custom_call" | custom-call | flops 268435456 | bytes 1048576 | tf_op jit(solution)/shard_map/solve/pallas_call | solution.py:479
  44.2 0.0 collective-permute-done.1.a_ref
  44.3 0.0 collective-permute-done.2.b_ref
  44.3 1.8 %edge.1 = bf16[2,1,1024,128]{3,2,1,0:T(8,128)(2,1)} custom-call(f32[32,128]{1,0:T(8,128)S(1)} %collective-permute-done.1.a_ref, f32[32,128]{1,0:T(8,128)S(1)} %collective-permute-done.2.b_ref, bf16[1024,256]{1,0:T(8,128)(2,1)S(1)} %get-tuple-element.37.inject_ref, f32[16,1024]{1,0:T(8,128)S(1)} %get-tuple-element.22.coef_ref, ...), custom_call_target="tpu_custom_call", output_to_operand_aliasing={{}: (4, {})} | custom-call | flops 134217728 | bytes 1048576 | tf_op jit(solution)/shard_map/edge/pallas_call | solution.py:494
  (1 shorter events, 0.0 us)
Async XLA Ops:
  3.6 25.7 %all-to-all-start = ((bf16[64,3,4,128]{3,2,1,0:T(4,128)(2,1)}), bf16[64,3,4,128]{3,2,1,0:T(4,128)(2,1)S(1)}, u32[]{:S(2)}, u32[]{:S(2)}) async-start(bf16[64,3,4,128]{3,2,1,0:T(4,128)(2,1)} %bitcast.1), calls=%async_computation | async-start | bytes 393216 | tf_op jit(solution)/shard_map/all_to_all | solution.py:457
  17.4 3.8 %collective-permute-start = (bf16[528,128]{1,0:T(8,128)(2,1)S(1)}, bf16[528,128]{1,0:T(8,128)(2,1)S(1)}, u32[]{:S(2)}, u32[]{:S(2)}) collective-permute-start(bf16[528,128]{1,0:T(8,128)(2,1)S(1)} %get-tuple-element.23.lift_ref.mine_ref), channel_id=1, source_target_pairs={{0,8},{16,24},{32,40},{48,56},{64,72},{80,88},{96,104},{112,120},{... | collective-permute-start | bytes 405512 | tf_op jit(solution)/shard_map/ppermute | solution.py:459
  29.3 11.9 %collective-permute-start.3 = (bf16[592,128]{1,0:T(8,128)(2,1)S(1)}, bf16[592,128]{1,0:T(8,128)(2,1)S(1)}, u32[]{:S(2)}, u32[]{:S(2)}) collective-permute-start(bf16[592,128]{1,0:T(8,128)(2,1)S(1)} %get-tuple-element.32), channel_id=1, source_target_pairs={{8,16},{24,32},{40,48},{56,64},{72,80},{88,96},{104,112},{120,128}... | collective-permute-start | bytes 454664 | tf_op jit(solution)/shard_map/ppermute | solution.py:475
  32.5 11.7 %collective-permute-start.1 = (f32[32,128]{1,0:T(8,128)S(1)}, f32[32,128]{1,0:T(8,128)S(1)}, u32[]{:S(2)}, u32[]{:S(2)}) collective-permute-start(f32[32,128]{1,0:T(8,128)S(1)} %get-tuple-element.27), channel_id=1, source_target_pairs={{0,1},{2,3},{4,5},{6,7},{1,0},{3,2},{5,4},{7,6},{8,9},{10,11},{12,... | collective-permute-start | bytes 49160 | tf_op jit(solution)/shard_map/ppermute | solution.py:476
  36.0 8.3 %collective-permute-start.2 = (f32[32,128]{1,0:T(8,128)S(1)}, f32[32,128]{1,0:T(8,128)S(1)}, u32[]{:S(2)}, u32[]{:S(2)}) collective-permute-start(f32[32,128]{1,0:T(8,128)S(1)} %get-tuple-element.28), channel_id=1, source_target_pairs={{1,2},{3,4},{5,6},{2,1},{4,3},{6,5},{9,10},{11,12},{13,14},{10,9},... | collective-permute-start | bytes 49160 | tf_op jit(solution)/shard_map/ppermute | solution.py:477

commit v6 on v5

--- a/solution.py
+++ b/solution.py
@@ -69,7 +69,7 @@
     copies = [pltpu.make_async_copy(src, dst, sems.at[i]) for i, (src, dst) in enumerate(pairs)]
     for copy in copies:
         copy.start()
-    for copy in copies[:2]:
+    for copy in copies:
         copy.wait()
     inv_r, inv_i = adm[0, 0], adm[1, 0]
     steps = [product(inv_r, inv_i, adm[0, k], adm[1, k]) for k in range(1, 1 + LINKS)]
@@ -96,8 +96,6 @@
     rows[pl.ds(PAIR, H, stride=ROWS), :] = pair
     rows[pl.ds(SPAN, H, stride=ROWS), :] = jnp.broadcast_to(span, (H, 128))
 
-    for copy in copies[2:]:
-        copy.wait()
     lane = iota((1, 128), 1)
     column = lax.rem(harm, HALF)
     mark = jnp.zeros((1, 128), F32)
@@ -135,33 +133,43 @@
     out_ref[...] = rows[...].astype(BF16)
 
 
-def sweeps_matrix(coefs):
-    coefs = pltpu.roll(coefs, 3 * TILE - (TILE - EDGE), 1)[:, :WIN]
-    rows = iota((WIN, WIN), 0)
-    lanes = iota((1, WIN), 1)
-    turned_r = jnp.zeros((WIN, WIN), F32)
-    turned_i = jnp.zeros((WIN, WIN), F32)
+def sweeps_matrix(coefs, first, count):
+    width = coefs.shape[1]
+    rows = iota((width, width), 0)
+    lanes = iota((1, width), 1)
+    turned_r = jnp.zeros((width, width), F32)
+    turned_i = jnp.zeros((width, width), F32)
     for k in range(LINKS):
         here = rows == lanes + coefs[8 + k : 9 + k].astype(I32)
         turned_r += jnp.where(here, coefs[1 + k : 2 + k], 0.0)
         turned_i += jnp.where(here, coefs[5 + k : 6 + k], 0.0)
     step_r, step_i = turned_r.T, turned_i.T
-    mid_r, mid_i = step_r[EDGE : EDGE + TILE], step_i[EDGE : EDGE + TILE]
+    mid_r, mid_i = step_r[first : first + count], step_i[first : first + count]
     twice = jnp.dot(
         jnp.concatenate([mid_r, mid_i], axis=0).astype(BF16),
         jnp.concatenate([step_r, step_i], axis=1).astype(BF16),
         preferred_element_type=F32,
     )
-    same = iota((TILE, WIN), 0) + EDGE == iota((TILE, WIN), 1)
-    all_r = twice[:TILE, :WIN] - twice[TILE:, WIN:] + mid_r + jnp.where(same, 1.0, 0.0)
-    all_i = twice[:TILE, WIN:] + twice[TILE:, :WIN] + mid_i
+    same = iota((count, width), 0) + first == iota((count, width), 1)
+    all_r = twice[:count, :width] - twice[count:, width:] + mid_r + jnp.where(same, 1.0, 0.0)
+    all_i = twice[:count, width:] + twice[count:, :width] + mid_i
     q_r, q_i = product(all_r, all_i, coefs[0:1], coefs[4:5])
     return jnp.concatenate([q_r, q_i], axis=0).astype(BF16)
 
 
+def volt_of(matrix, inject):
+    count = matrix.shape[0] // 2
+    acc = jnp.dot(matrix, inject, preferred_element_type=F32)
+    return (acc[:count, :128] - acc[count:, 128:]).astype(BF16), (acc[:count, 128:] + acc[count:, :128]).astype(BF16)
+
+
 def sweeps_kernel(coef_ref, q_ref):
-    for b in range(q_ref.shape[0]):
-        q_ref[b] = sweeps_matrix(coef_ref[:, b * TILE : (b + 3) * TILE])
+    blank = jnp.zeros((coef_ref.shape[0], TILE), F32)
+    tiles = q_ref.shape[0]
+    for b in range(tiles):
+        around = [coef_ref[:, t * TILE : t * TILE + TILE] if 0 <= t < tiles else blank for t in (b - 1, b, b + 1)]
+        coefs = pltpu.roll(jnp.concatenate(around, axis=1), 2 * TILE + EDGE, 1)[:, :WIN]
+        q_ref[b] = sweeps_matrix(coefs, EDGE, TILE)
 
 
 def mix_kernel(got_ref, lift_ref, a_ref, b_ref, rows_ref, range_ref, out_a_ref, out_b_ref):
@@ -177,12 +185,7 @@
     out_b_ref[16:, :] = b_ref[...]
 
 
-def volt_of(matrix, inject):
-    acc = jnp.dot(matrix, inject, preferred_element_type=F32)
-    return (acc[:TILE, :128] - acc[TILE:, 128:]).astype(BF16), (acc[:TILE, 128:] + acc[TILE:, :128]).astype(BF16)
-
-
-def inner_network(rows, q_ref, inject, volt, volt_hbm, sems):
+def inner_kernel(rows, q_ref, inject, volt_hbm, volt, sems):
     def part(p):
         return jnp.concatenate(
             [
@@ -206,23 +209,29 @@
     buses = H * SUB
     owner = jnp.where(iota((buses, convs), 0) == target, 1.0, 0.0).astype(BF16)
     inject[...] = jnp.dot(owner, spectra, preferred_element_type=F32).astype(BF16)
-    for b in range(1, buses // TILE - 1):
-        window = inject[b * TILE - EDGE : b * TILE - EDGE + WIN, :]
+    tiles = q_ref.shape[0]
+    copies = []
+    for b in range(tiles):
+        first = max(b * TILE - EDGE, 0)
+        last = min(b * TILE - EDGE + WIN, buses)
+        pieces = [jnp.zeros((n, 256), BF16) for n in (first - b * TILE + EDGE, b * TILE - EDGE + WIN - last)]
+        pieces.insert(1, inject[first:last, :])
+        window = jnp.concatenate([x for x in pieces if x.shape[0]], axis=0)
         volt[0, 0, b * TILE : b * TILE + TILE, :], volt[1, 0, b * TILE : b * TILE + TILE, :] = volt_of(
-            q_ref[b - 1], window
+            q_ref[b], window
         )
-    inner = pl.ds(TILE, buses - 2 * TILE)
-    copies = [pltpu.make_async_copy(volt.at[p, 0, inner], volt_hbm.at[p, 0, inner], sems.at[p]) for p in range(2)]
+        if b % 2:
+            place = pl.ds(b * TILE - TILE, 2 * TILE)
+            for p in range(2):
+                copies.append(
+                    pltpu.make_async_copy(volt.at[p, 0, place], volt_hbm.at[p, 0, place], sems.at[b - 1 + p])
+                )
+                copies[-1].start()
     for copy in copies:
-        copy.start()
-    return copies
-
-
-def edge_kernel(a_ref, b_ref, inject_ref, coef_ref, done_hbm, volt_hbm, volt, sems):
-    del done_hbm
-    is_even = even("bus")
-    low = jnp.where(is_even, b_ref[...], a_ref[...])
-    high = jnp.where(is_even, a_ref[...], b_ref[...])
+        copy.wait()
+
+
+def edges(low, high, inject_ref, coef_ref, volt):
     buses = inject_ref.shape[0]
 
     def injected(edge, lane0):
@@ -236,26 +245,14 @@
             total_i += jnp.where(here, edge[2 * c + 1 : 2 * c + 2, :], 0.0)
         return jnp.concatenate([total_r, total_i], axis=1).astype(BF16)
 
-    rest = WIN - TILE - 2 * EDGE
-    windows = [
-        jnp.concatenate([injected(low, HALF - 1), inject_ref[: WIN - EDGE, :]], axis=0),
-        jnp.concatenate(
-            [inject_ref[buses - TILE - EDGE :, :], injected(high, 0), jnp.zeros((rest, 256), BF16)], axis=0
-        ),
-    ]
-    coefs = [
-        jnp.concatenate([low[16:], coef_ref[:, : 2 * TILE]], axis=1),
-        jnp.concatenate([coef_ref[:, buses - 2 * TILE :], high[16:]], axis=1),
-    ]
-    copies = []
-    for e in range(2):
-        volt[e, 0], volt[e, 1] = volt_of(sweeps_matrix(coefs[e]), windows[e])
-        for p in range(2):
-            place = volt_hbm.at[p, 0, pl.ds(e * (buses - TILE), TILE)]
-            copies.append(pltpu.make_async_copy(volt.at[e, p], place, sems.at[2 * e + p]))
-            copies[-1].start()
-    for copy in copies:
-        copy.wait()
+    coefs = jnp.concatenate([low[16:], coef_ref[:, :128]], axis=1)
+    coefs = pltpu.roll(coefs, 128 + EDGE, 1)[:, :128]
+    window = jnp.concatenate([injected(low, HALF - 1), inject_ref[: 128 - EDGE, :]], axis=0)
+    volt[0, 0], volt[0, 1] = volt_of(sweeps_matrix(coefs, EDGE, EDGE), window)
+    coefs = jnp.concatenate([coef_ref[:, buses - 128 :], high[16:]], axis=1)
+    coefs = pltpu.roll(coefs, 256 - EDGE, 1)[:, :128]
+    window = jnp.concatenate([inject_ref[buses - 128 + EDGE :, :], injected(high, 0)], axis=0)
+    volt[1, 0], volt[1, 1] = volt_of(sweeps_matrix(coefs, 128 - 2 * EDGE, EDGE), window)
 
 
 def swapped(x):
@@ -267,14 +264,24 @@
     return a * jnp.where(real, b, turned) + swapped(a) * jnp.where(real, -turned, b)
 
 
-def solve_kernel(
-    aux_ref, rows, mine_ref, a_ref, b_ref, q_ref, inject_ref, near_hbm, volt_hbm, near, volt, out, sems
+def finish_kernel(
+    aux_ref, rows, mine_ref, beside_a_ref, beside_b_ref, halo_a_ref, halo_b_ref, inject_ref, coef_ref, done_hbm,
+    near_hbm, volt_hbm, near, volt, out, sems,
 ):
-    copies = inner_network(rows, q_ref, inject_ref, volt, volt_hbm, sems)
-    near_converters(aux_ref, rows, (mine_ref, a_ref, b_ref), out)
+    del done_hbm
+    is_even = even("bus")
+    low = jnp.where(is_even, halo_b_ref[...], halo_a_ref[...])
+    high = jnp.where(is_even, halo_a_ref[...], halo_b_ref[...])
+    edges(low, high, inject_ref, coef_ref, volt)
+    near_converters(aux_ref, rows, (mine_ref, beside_a_ref, beside_b_ref), out)
     near[...] = out[...].astype(BF16)
-    copies.append(pltpu.make_async_copy(near, near_hbm, sems.at[2]))
-    copies[-1].start()
+    copies = [pltpu.make_async_copy(near, near_hbm, sems.at[4])]
+    for e in range(2):
+        for p in range(2):
+            place = volt_hbm.at[p, 0, pl.ds(e * (inject_ref.shape[0] - EDGE), EDGE)]
+            copies.append(pltpu.make_async_copy(volt.at[e, p], place, sems.at[2 * e + p]))
+    for copy in copies:
+        copy.start()
     for copy in copies:
         copy.wait()
 
@@ -460,7 +467,7 @@
     q = call(
         sweeps_kernel,
         "sweeps",
-        S((tiles - 2, 2 * TILE, WIN), BF16),
+        S((tiles, 2 * TILE, WIN), BF16),
         [VMEM],
         cost=(2 * tiles * 256 * 256 * 512, 2**20, 0),
     )(coef)
@@ -476,31 +483,31 @@
     halo_a = lax.ppermute(halo_a, "bus", over_bus[0])
     halo_b = lax.ppermute(halo_b, "bus", over_bus[1])
     out_volt = S((2, 1, block, snapshots), BF16)
-    inject, near, bus_volt = call(
-        solve_kernel,
-        "solve",
-        (S((block, 256), BF16), S((kinds * CONV, snapshots), BF16), out_volt),
-        [VMEM] * 6,
+    inject, bus_volt = call(
+        inner_kernel,
+        "inner",
+        (S((block, 256), BF16), out_volt),
+        [VMEM] * 2,
+        [pltpu.VMEM((2, 1, block, snapshots), BF16), pltpu.SemaphoreType.DMA((tiles,))],
+        (2 * tiles * 256 * 256 * 256, 2**20, 0),
+        (VMEM, HBM),
+    )(rows, q)
+    beside_b, halo_a, halo_b, inject, bus_volt = lax.optimization_barrier((beside_b, halo_a, halo_b, inject, bus_volt))
+    near, bus_volt = call(
+        finish_kernel,
+        "finish",
+        (S((kinds * CONV, snapshots), BF16), out_volt),
+        [VMEM] * 9 + [HBM],
         [
             pltpu.VMEM((kinds * CONV, snapshots), BF16),
-            pltpu.VMEM((2, 1, block, snapshots), BF16),
+            pltpu.VMEM((2, 2, EDGE, snapshots), BF16),
             pltpu.VMEM((kinds * CONV, 128), F32),
-            pltpu.SemaphoreType.DMA((3,)),
+            pltpu.SemaphoreType.DMA((5,)),
         ],
-        (2 * tiles * 256 * 256 * 256, 2**20, 0),
-        (VMEM, HBM, HBM),
-    )(aux, rows, lift, beside_a, beside_b, q)
-    halo_a, halo_b, near = lax.optimization_barrier((halo_a, halo_b, near))
-    bus_volt = call(
-        edge_kernel,
-        "edge",
-        out_volt,
-        [VMEM] * 4 + [HBM],
-        [pltpu.VMEM((2, 2, TILE, snapshots), BF16), pltpu.SemaphoreType.DMA((4,))],
-        (4 * 256 * 256 * 512, 2**20, 0),
-        HBM,
-        {4: 0},
-    )(halo_a, halo_b, inject, coef, bus_volt)
+        (2 * 10**7, 2**20, 0),
+        (HBM, HBM),
+        {9: 1},
+    )(aux, rows, lift, beside_a, beside_b, halo_a, halo_b, inject, coef, bus_volt)
     return (bus_volt, near.reshape(2, H, CONV, snapshots))
 
 

time: 46.3 us -> 46 us (level)
  waiting for transfers between devices: 11.5 us -> 11 us
    ppermute x1, waiting for transfers between devices: 0.01 us -> 3.43 us  [local(): halo_b = lax.ppermute(halo_b, 'bus', over_bus[1])]
    ppermute x1, waiting for transfers between devices: 3.35 us -> 0.01 us  [local(): beside_b = lax.ppermute(beside_b, ('harm', 'bus'), over_ranges[1])]
    all_to_all x1, waiting for transfers between devices: 8.13 us -> 7.61 us  [local(): lax.all_to_all(payload.reshape(four), 'harm', split_axis=0, concat_axis=0...]
  transfers between devices with their start and end apart: 5 -> 5, of which waited for: 2 -> 2; matrix products, arithmetic and copies ran while one was open for 0% -> 0% of each run, Pallas kernels for 10% -> 8%
where the time goes in v6:
time: 46 us; the launch traced here: 45.7 us
  starting transfers between devices  24.3 us (53%)
  waiting for transfers between devices  11 us (24%)
  Pallas kernels  9.6 us (21%)
  between operations  0.71 us (2%)
    all_to_all x1, starting transfers between devices, local(): lax.all_to_all(payload.reshape(four), 'harm', split_axis=0, concat_axis=0...  13.8 us
    all_to_all x1, waiting for transfers between devices, local(): lax.all_to_all(payload.reshape(four), 'harm', split_axis=0, concat_axis=0...  7.61 us
    ppermute x1, starting transfers between devices, local(): halo_a = lax.ppermute(halo_a, 'bus', over_bus[0])  3.48 us
    ppermute x1, waiting for transfers between devices, local(): halo_b = lax.ppermute(halo_b, 'bus', over_bus[1])  3.43 us
    ppermute x1, starting transfers between devices, local(): beside_b = lax.ppermute(beside_b, ('harm', 'bus'), over_ranges[1])  3.16 us
    pallas_call x1, Pallas kernels, local(): call(begin_kernel, 'begin', (S((16, block), F32), S((16, 128), F32), S((1...  2.93 us
    pallas_call x1, Pallas kernels, local(): call(finish_kernel, 'finish', (S((kinds * CONV, snapshots), BF16), out_vo...  2.82 us
    pallas_call x1, Pallas kernels, local(): call(sweeps_kernel, 'sweeps', S((tiles, 2 * TILE, WIN), BF16), [VMEM], co...  2.34 us
  transfers between devices with their start and end apart: 5, of which 2 were waited for; matrix products, arithmetic and copies ran while one was open for 0% of the time, Pallas kernels for 8%

profile of v6, /device:TPU:32, one launch (start us, length us, event | category | flops | bytes accessed | tf_op | source)
XLA Modules:
  0.0 45.7 jit_solution(13918916427145317765)
XLA Ops:
  0.6 2.9 %begin.1 = (f32[16,1024]{1,0:T(8,128)S(1)}, f32[16,128]{1,0:T(8,128)S(1)}, f32[16,128]{1,0:T(8,128)S(1)}, f32[8,128]{1,0:T(8,128)S(1)}, bf16[768,128]{1,0:T(8,128)(2,1)}, /*index=5*/bf16[528,128]{1,0:T(8,128)(2,1)S(1)}) custom-call(f32[2,4,1,1024]{3,2,1,0:T(1,128)} %adm_hbm.1, s32[3,1024]{1,0:T(4,128)} %off_hbm.1, s32[4]{0:T(128)} %type_hbm.1, f32[8]{0:T(128)} %steep_hbm.1, ...), custom_call_target="tpu_custom_call" | custom-call | flops 268435456 | bytes 1048576 | tf_op jit(solution)/shard_map/begin/pallas_call | solution.py:417
  3.6 13.8 %all-to-all-start = ((bf16[64,3,4,128]{3,2,1,0:T(4,128)(2,1)}), bf16[64,3,4,128]{3,2,1,0:T(4,128)(2,1)S(1)}, u32[]{:S(2)}, u32[]{:S(2)}) async-start(bf16[64,3,4,128]{3,2,1,0:T(4,128)(2,1)} %bitcast.1), calls=%async_computation | async-start | bytes 393216 | tf_op jit(solution)/shard_map/all_to_all | solution.py:464
  17.4 2.0 %collective-permute-start = (bf16[528,128]{1,0:T(8,128)(2,1)S(1)}, bf16[528,128]{1,0:T(8,128)(2,1)S(1)}, u32[]{:S(2)}, u32[]{:S(2)}) collective-permute-start(bf16[528,128]{1,0:T(8,128)(2,1)S(1)} %get-tuple-element.27.lift_ref.mine_ref), channel_id=1, source_target_pairs={{0,8},{16,24},{32,40},{48,56},{64,72},{80,88},{96,104},{112,120},{... | collective-permute-start | bytes 405512 | tf_op jit(solution)/shard_map/ppermute | solution.py:466
  19.3 2.3 %sweeps.1.q_ref = bf16[8,256,256]{2,1,0:T(8,128)(2,1)S(1)} custom-call(f32[16,1024]{1,0:T(8,128)S(1)} %get-tuple-element.26.coef_ref), custom_call_target="tpu_custom_call" | custom-call | flops 536870912 | bytes 1048576 | tf_op jit(solution)/shard_map/sweeps/pallas_call | solution.py:467
  21.7 0.0 collective-permute-done.beside_a_ref
  21.7 7.6 %all-to-all-done = bf16[64,3,4,128]{3,2,1,0:T(4,128)(2,1)S(1)} async-done(((bf16[64,3,4,128]{3,2,1,0:T(4,128)(2,1)}), bf16[64,3,4,128]{3,2,1,0:T(4,128)(2,1)S(1)}, u32[]{:S(2)}, u32[]{:S(2)}) %all-to-all-start) | async-done | bytes 196640 | tf_op jit(solution)/shard_map/all_to_all | solution.py:464
  29.4 3.2 %collective-permute-start.1 = (bf16[592,128]{1,0:T(8,128)(2,1)S(1)}, bf16[592,128]{1,0:T(8,128)(2,1)S(1)}, u32[]{:S(2)}, u32[]{:S(2)}) collective-permute-start(bf16[592,128]{1,0:T(8,128)(2,1)S(1)} %get-tuple-element.33), channel_id=1, source_target_pairs={{8,16},{24,32},{40,48},{56,64},{72,80},{88,96},{104,112},{120,128}... | collective-permute-start | bytes 454664 | tf_op jit(solution)/shard_map/ppermute | solution.py:482
  32.5 3.5 %collective-permute-start.2 = (f32[32,128]{1,0:T(8,128)S(1)}, f32[32,128]{1,0:T(8,128)S(1)}, u32[]{:S(2)}, u32[]{:S(2)}) collective-permute-start(f32[32,128]{1,0:T(8,128)S(1)} %get-tuple-element.34), channel_id=1, source_target_pairs={{0,1},{2,3},{4,5},{6,7},{1,0},{3,2},{5,4},{7,6},{8,9},{10,11},{12,... | collective-permute-start | bytes 49160 | tf_op jit(solution)/shard_map/ppermute | solution.py:483
  36.0 1.9 %collective-permute-start.3 = (f32[32,128]{1,0:T(8,128)S(1)}, f32[32,128]{1,0:T(8,128)S(1)}, u32[]{:S(2)}, u32[]{:S(2)}) collective-permute-start(f32[32,128]{1,0:T(8,128)S(1)} %get-tuple-element.35), channel_id=1, source_target_pairs={{1,2},{3,4},{5,6},{2,1},{4,3},{6,5},{9,10},{11,12},{13,14},{10,9},... | collective-permute-start | bytes 49160 | tf_op jit(solution)/shard_map/ppermute | solution.py:484
  37.9 1.5 %inner.1 = (bf16[1024,256]{1,0:T(8,128)(2,1)S(1)}, bf16[2,1,1024,128]{3,2,1,0:T(8,128)(2,1)}) custom-call(f32[768,128]{1,0:T(8,128)S(1)} %get-tuple-element.31.rows, bf16[8,256,256]{2,1,0:T(8,128)(2,1)S(1)} %sweeps.1.q_ref), custom_call_target="tpu_custom_call" | custom-call | flops 268435456 | bytes 1048576 | tf_op jit(solution)/shard_map/inner/pallas_call | solution.py:486
  39.4 0.0 collective-permute-done.2.halo_a_ref
  39.4 3.4 %collective-permute-done.3.halo_b_ref = f32[32,128]{1,0:T(8,128)S(1)} collective-permute-done((f32[32,128]{1,0:T(8,128)S(1)}, f32[32,128]{1,0:T(8,128)S(1)}, u32[]{:S(2)}, u32[]{:S(2)}) %collective-permute-start.3) | collective-permute-done | bytes 16416 | tf_op jit(solution)/shard_map/ppermute | solution.py:484
  42.9 0.0 collective-permute-done.1.beside_b_ref
  42.9 2.8 %finish.1 = (bf16[512,128]{1,0:T(8,128)(2,1)}, bf16[2,1,1024,128]{3,2,1,0:T(8,128)(2,1)}) custom-call(f32[8,128]{1,0:T(8,128)S(1)} %get-tuple-element.24.aux_ref, f32[768,128]{1,0:T(8,128)S(1)} %get-tuple-element.31.rows, bf16[528,128]{1,0:T(8,128)(2,1)S(1)} %get-tuple-element.27.lift_ref.mine_ref, ...), custom_call_target="tpu_custom_call", output_to_operand_aliasing={{1}: (9, {})} | custom-call | flops 20000000 | bytes 1048576 | tf_op jit(solution)/shard_map/finish/pallas_call | solution.py:496
  (1 shorter events, 0.0 us)
Async XLA Ops:
  3.6 25.7 %all-to-all-start = ((bf16[64,3,4,128]{3,2,1,0:T(4,128)(2,1)}), bf16[64,3,4,128]{3,2,1,0:T(4,128)(2,1)S(1)}, u32[]{:S(2)}, u32[]{:S(2)}) async-start(bf16[64,3,4,128]{3,2,1,0:T(4,128)(2,1)} %bitcast.1), calls=%async_computation | async-start | bytes 393216 | tf_op jit(solution)/shard_map/all_to_all | solution.py:464
  17.4 4.3 %collective-permute-start = (bf16[528,128]{1,0:T(8,128)(2,1)S(1)}, bf16[528,128]{1,0:T(8,128)(2,1)S(1)}, u32[]{:S(2)}, u32[]{:S(2)}) collective-permute-start(bf16[528,128]{1,0:T(8,128)(2,1)S(1)} %get-tuple-element.27.lift_ref.mine_ref), channel_id=1, source_target_pairs={{0,8},{16,24},{32,40},{48,56},{64,72},{80,88},{96,104},{112,120},{... | collective-permute-start | bytes 405512 | tf_op jit(solution)/shard_map/ppermute | solution.py:466
  29.4 13.5 %collective-permute-start.1 = (bf16[592,128]{1,0:T(8,128)(2,1)S(1)}, bf16[592,128]{1,0:T(8,128)(2,1)S(1)}, u32[]{:S(2)}, u32[]{:S(2)}) collective-permute-start(bf16[592,128]{1,0:T(8,128)(2,1)S(1)} %get-tuple-element.33), channel_id=1, source_target_pairs={{8,16},{24,32},{40,48},{56,64},{72,80},{88,96},{104,112},{120,128}... | collective-permute-start | bytes 454664 | tf_op jit(solution)/shard_map/ppermute | solution.py:482
  32.5 6.9 %collective-permute-start.2 = (f32[32,128]{1,0:T(8,128)S(1)}, f32[32,128]{1,0:T(8,128)S(1)}, u32[]{:S(2)}, u32[]{:S(2)}) collective-permute-start(f32[32,128]{1,0:T(8,128)S(1)} %get-tuple-element.34), channel_id=1, source_target_pairs={{0,1},{2,3},{4,5},{6,7},{1,0},{3,2},{5,4},{7,6},{8,9},{10,11},{12,... | collective-permute-start | bytes 49160 | tf_op jit(solution)/shard_map/ppermute | solution.py:483
  36.0 6.8 %collective-permute-start.3 = (f32[32,128]{1,0:T(8,128)S(1)}, f32[32,128]{1,0:T(8,128)S(1)}, u32[]{:S(2)}, u32[]{:S(2)}) collective-permute-start(f32[32,128]{1,0:T(8,128)S(1)} %get-tuple-element.35), channel_id=1, source_target_pairs={{1,2},{3,4},{5,6},{2,1},{4,3},{6,5},{9,10},{11,12},{13,14},{10,9},... | collective-permute-start | bytes 49160 | tf_op jit(solution)/shard_map/ppermute | solution.py:484

commit v7 on v6

--- a/solution.py
+++ b/solution.py
@@ -20,7 +20,7 @@
 ROWS = 12
 COEF = 8
 PAIR = 9
-SPAN = 10
+FAR = 10
 MARK = 11
 LIFT = 8 * H
 HALF = 32
@@ -91,10 +91,12 @@
     aux_ref[1:2, :] = span
     aux_ref[2:3, :] = spans[pl.ds(harm + jnp.where(even("harm"), 1, -1), 1), :]
     group = groups[...]
-    pair = jnp.where(iota((H, 128), 0) % 2 == 0, pltpu.roll(group, H - 1, 0), pltpu.roll(group, 1, 0))
+    after, before = pltpu.roll(group, H - 1, 0), pltpu.roll(group, 1, 0)
+    first_core = iota((H, 128), 0) % 2 == 0
+    pair, far = jnp.where(first_core, after, before), jnp.where(first_core, before, after)
     rows[pl.ds(COEF, H, stride=ROWS), :] = group
     rows[pl.ds(PAIR, H, stride=ROWS), :] = pair
-    rows[pl.ds(SPAN, H, stride=ROWS), :] = jnp.broadcast_to(span, (H, 128))
+    rows[pl.ds(FAR, H, stride=ROWS), :] = far
 
     lane = iota((1, 128), 1)
     column = lax.rem(harm, HALF)
@@ -172,17 +174,19 @@
         q_ref[b] = sweeps_matrix(coefs, EDGE, TILE)
 
 
-def mix_kernel(got_ref, lift_ref, a_ref, b_ref, rows_ref, range_ref, out_a_ref, out_b_ref):
+def mix_kernel(got_ref, a_ref, b_ref, rows_ref, out_a_ref, out_b_ref):
     size = got_ref.shape[0]
     rows_ref[...] = got_ref[...].astype(F32)
-    range_ref[: LIFT + 16, :] = lift_ref[...]
-    range_ref[LIFT + 16 :, :] = rows_ref[pl.ds(COEF, H, stride=ROWS), :].astype(BF16)
     first, last = rows_ref[:16, :], pltpu.roll(rows_ref[size - 16 :, :], ROWS, 0)
+    far = rows_ref[pl.ds(FAR, H, stride=ROWS), :]
     is_even = even("bus")
-    out_a_ref[:16, :] = jnp.where(is_even, last, first)
-    out_b_ref[:16, :] = jnp.where(is_even, first, last)
-    out_a_ref[16:, :] = a_ref[...]
-    out_b_ref[16:, :] = b_ref[...]
+    for ref, edge, range_rows in (
+        (out_a_ref, a_ref, jnp.where(is_even, last, first)),
+        (out_b_ref, b_ref, jnp.where(is_even, first, last)),
+    ):
+        ref[:16, :] = range_rows
+        ref[16:32, :] = edge[...]
+        ref[32:, :] = far
 
 
 def inner_kernel(rows, q_ref, inject, volt_hbm, volt, sems):
@@ -245,11 +249,11 @@
             total_i += jnp.where(here, edge[2 * c + 1 : 2 * c + 2, :], 0.0)
         return jnp.concatenate([total_r, total_i], axis=1).astype(BF16)
 
-    coefs = jnp.concatenate([low[16:], coef_ref[:, :128]], axis=1)
+    coefs = jnp.concatenate([low[16:32], coef_ref[:, :128]], axis=1)
     coefs = pltpu.roll(coefs, 128 + EDGE, 1)[:, :128]
     window = jnp.concatenate([injected(low, HALF - 1), inject_ref[: 128 - EDGE, :]], axis=0)
     volt[0, 0], volt[0, 1] = volt_of(sweeps_matrix(coefs, EDGE, EDGE), window)
-    coefs = jnp.concatenate([coef_ref[:, buses - 128 :], high[16:]], axis=1)
+    coefs = jnp.concatenate([coef_ref[:, buses - 128 :], high[16:32]], axis=1)
     coefs = pltpu.roll(coefs, 256 - EDGE, 1)[:, :128]
     window = jnp.concatenate([inject_ref[buses - 128 + EDGE :, :], injected(high, 0)], axis=0)
     volt[1, 0], volt[1, 1] = volt_of(sweeps_matrix(coefs, 128 - 2 * EDGE, EDGE), window)
@@ -273,7 +277,10 @@
     low = jnp.where(is_even, halo_b_ref[...], halo_a_ref[...])
     high = jnp.where(is_even, halo_a_ref[...], halo_b_ref[...])
     edges(low, high, inject_ref, coef_ref, volt)
-    near_converters(aux_ref, rows, (mine_ref, beside_a_ref, beside_b_ref), out)
+    harm = lax.axis_index("harm")
+    far = rows[pl.ds(FAR, H, stride=ROWS), :]
+    far = jnp.where(harm == 0, low[32:], jnp.where(harm == H - 1, high[32:], far))
+    near_converters(aux_ref, rows, far, (mine_ref, beside_a_ref, beside_b_ref), out)
     near[...] = out[...].astype(BF16)
     copies = [pltpu.make_async_copy(near, near_hbm, sems.at[4])]
     for e in range(2):
@@ -286,7 +293,7 @@
         copy.wait()
 
 
-def near_converters(aux_ref, rows, lifts, out):
+def near_converters(aux_ref, rows, far, lifts, out):
     harm = lax.axis_index("harm")
     is_even = even("harm")
     a_at = jnp.where(is_even, 2, 0)
@@ -328,7 +335,7 @@
         [
             rows[pl.ds(COEF, H, stride=ROWS), :].astype(BF16),
             rows[pl.ds(PAIR, H, stride=ROWS), :].astype(BF16),
-            lifts[2][LIFT + 16 :, :],
+            far.astype(BF16),
         ],
         axis=1,
     )
@@ -359,18 +366,22 @@
     table = lax.dot_general(high, match, dims, preferred_element_type=F32)
     table += lax.dot_general(rest, match, dims, preferred_element_type=F32)
 
-    total = [[jnp.zeros((H, 128), F32) for _ in range(2)] for _ in range(CONV)]
-    for q in range(3):
-        for o in range(CONV):
-            spec_r, spec_i = (lifts[q][(2 * o + p) * H : (2 * o + p + 1) * H, :].astype(F32) for p in range(2))
-            for c in range(CONV):
-                at = c * 3 * CONV + q * CONV + o
-                add_r, add_i = product(table[:, at : at + 1], table[:, 64 + at : 65 + at], spec_r, spec_i)
-                total[c][0] += add_r
-                total[c][1] += add_i
-    for c in range(CONV):
-        for p in range(2):
-            out[pl.ds(p * H * CONV + c, H, stride=CONV), :] = total[c][p]
+    step = 16
+    for h in range(0, H, step):
+        total = [[jnp.zeros((step, 128), F32) for _ in range(2)] for _ in range(CONV)]
+        for q in range(3):
+            for o in range(CONV):
+                at = 2 * o * H + h
+                spec_r, spec_i = (lifts[q][at + p * H : at + p * H + step, :].astype(F32) for p in range(2))
+                for c in range(CONV):
+                    at = c * 3 * CONV + q * CONV + o
+                    weights = (table[h : h + step, n : n + 1] for n in (at, 64 + at))
+                    add_r, add_i = product(*weights, spec_r, spec_i)
+                    total[c][0] += add_r
+                    total[c][1] += add_i
+        for c in range(CONV):
+            for p in range(2):
+                out[pl.ds((p * H + h) * CONV + c, step, stride=CONV), :] = total[c][p]
 
 
 VMEM = pl.BlockSpec(memory_space=pltpu.VMEM)
@@ -471,15 +482,17 @@
         [VMEM],
         cost=(2 * tiles * 256 * 256 * 512, 2**20, 0),
     )(coef)
+    lift_b, q = lax.optimization_barrier((lift, q))
+    beside_b = lax.ppermute(lift_b, ("harm", "bus"), over_ranges[1])
     got, q, beside_a = lax.optimization_barrier((got, q, beside_a))
 
-    rows, beside_b, halo_a, halo_b = call(
+    halo = S((32 + harm_count, 128), F32)
+    rows, halo_a, halo_b = call(
         mix_kernel,
         "mix",
-        (S((size, 128), F32), S((LIFT + 16 + H, 128), BF16), S((32, 128), F32), S((32, 128), F32)),
-        [VMEM] * 4,
-    )(got.reshape(size, snapshots), lift, edge_a, edge_b)
-    beside_b = lax.ppermute(beside_b, ("harm", "bus"), over_ranges[1])
+        (S((size, 128), F32), halo, halo),
+        [VMEM] * 3,
+    )(got.reshape(size, snapshots), edge_a, edge_b)
     halo_a = lax.ppermute(halo_a, "bus", over_bus[0])
     halo_b = lax.ppermute(halo_b, "bus", over_bus[1])
     out_volt = S((2, 1, block, snapshots), BF16)

time: 46 us -> 42.8 us (0.930)
  waiting for transfers between devices: 11 us -> 4.33 us
  starting transfers between devices: 24.3 us -> 27.7 us
    all_to_all x1, waiting for transfers between devices: 7.61 us -> 0.56 us  [local(): lax.all_to_all(payload.reshape(four), 'harm', split_axis=0, concat_axis=0...]
    ppermute x1, starting transfers between devices: 3.16 us -> 7.05 us  [local(): beside_b = lax.ppermute(lift_b, ('harm', 'bus'), over_ranges[1])]
    ppermute x1, starting transfers between devices: 3.48 us -> 2.94 us  [local(): halo_a = lax.ppermute(halo_a, 'bus', over_bus[0])]
  transfers between devices with their start and end apart: 5 -> 5, of which waited for: 2 -> 2; matrix products, arithmetic and copies ran while one was open for 0% -> 0% of each run, Pallas kernels for 8% -> 9%
where the time goes in v7:
time: 42.8 us; the launch traced here: 42.6 us
  starting transfers between devices  27.7 us (65%)
  Pallas kernels  9.83 us (23%)
  waiting for transfers between devices  4.33 us (10%)
  between operations  0.72 us (2%)
    all_to_all x1, starting transfers between devices, local(): lax.all_to_all(payload.reshape(four), 'harm', split_axis=0, concat_axis=0...  13.8 us
    ppermute x1, starting transfers between devices, local(): beside_b = lax.ppermute(lift_b, ('harm', 'bus'), over_ranges[1])  7.05 us
    ppermute x1, waiting for transfers between devices, local(): halo_b = lax.ppermute(halo_b, 'bus', over_bus[1])  3.76 us
    pallas_call x1, Pallas kernels, local(): call(finish_kernel, 'finish', (S((kinds * CONV, snapshots), BF16), out_vo...  3.05 us
    ppermute x1, starting transfers between devices, local(): halo_a = lax.ppermute(halo_a, 'bus', over_bus[0])  2.94 us
    pallas_call x1, Pallas kernels, local(): call(begin_kernel, 'begin', (S((16, block), F32), S((16, 128), F32), S((1...  2.93 us
    pallas_call x1, Pallas kernels, local(): call(sweeps_kernel, 'sweeps', S((tiles, 2 * TILE, WIN), BF16), [VMEM], co...  2.34 us
    ppermute x1, starting transfers between devices, local(): beside_a = lax.ppermute(lift, ('harm', 'bus'), over_ranges[0])  1.96 us
  transfers between devices with their start and end apart: 5, of which 2 were waited for; matrix products, arithmetic and copies ran while one was open for 0% of the time, Pallas kernels for 9%

profile of v7, /device:TPU:32, one launch (start us, length us, event | category | flops | bytes accessed | tf_op | source)
XLA Modules:
  0.0 42.6 jit_solution(8088781770202507756)
XLA Ops:
  0.6 2.9 %begin.1 = (f32[16,1024]{1,0:T(8,128)S(1)}, f32[16,128]{1,0:T(8,128)S(1)}, f32[16,128]{1,0:T(8,128)S(1)}, f32[8,128]{1,0:T(8,128)S(1)}, bf16[768,128]{1,0:T(8,128)(2,1)}, /*index=5*/bf16[528,128]{1,0:T(8,128)(2,1)S(1)}) custom-call(f32[2,4,1,1024]{3,2,1,0:T(1,128)} %adm_hbm.1, s32[3,1024]{1,0:T(4,128)} %off_hbm.1, s32[4]{0:T(128)} %type_hbm.1, f32[8]{0:T(128)} %steep_hbm.1, ...), custom_call_target="tpu_custom_call" | custom-call | flops 268435456 | bytes 1048576 | tf_op jit(solution)/shard_map/begin/pallas_call | solution.py:428
  3.6 13.8 %all-to-all-start = ((bf16[64,3,4,128]{3,2,1,0:T(4,128)(2,1)}), bf16[64,3,4,128]{3,2,1,0:T(4,128)(2,1)S(1)}, u32[]{:S(2)}, u32[]{:S(2)}) async-start(bf16[64,3,4,128]{3,2,1,0:T(4,128)(2,1)} %bitcast.1), calls=%async_computation | async-start | bytes 393216 | tf_op jit(solution)/shard_map/all_to_all | solution.py:475
  17.4 2.0 %collective-permute-start = (bf16[528,128]{1,0:T(8,128)(2,1)S(1)}, bf16[528,128]{1,0:T(8,128)(2,1)S(1)}, u32[]{:S(2)}, u32[]{:S(2)}) collective-permute-start(bf16[528,128]{1,0:T(8,128)(2,1)S(1)} %get-tuple-element.35.mine_ref), channel_id=1, source_target_pairs={{0,8},{16,24},{32,40},{48,56},{64,72},{80,88},{96,104},{112,120},{... | collective-permute-start | bytes 405512 | tf_op jit(solution)/shard_map/ppermute | solution.py:477
  19.3 2.3 %sweeps.1.q_ref = bf16[8,256,256]{2,1,0:T(8,128)(2,1)S(1)} custom-call(f32[16,1024]{1,0:T(8,128)S(1)} %get-tuple-element.28.coef_ref), custom_call_target="tpu_custom_call" | custom-call | flops 536870912 | bytes 1048576 | tf_op jit(solution)/shard_map/sweeps/pallas_call | solution.py:478
  21.7 7.0 %collective-permute-start.1 = (bf16[528,128]{1,0:T(8,128)(2,1)S(1)}, bf16[528,128]{1,0:T(8,128)(2,1)S(1)}, u32[]{:S(2)}, u32[]{:S(2)}) collective-permute-start(bf16[528,128]{1,0:T(8,128)(2,1)S(1)} %get-tuple-element.35.mine_ref), channel_id=1, source_target_pairs={{8,16},{24,32},{40,48},{56,64},{72,80},{88,96},{104,112},{120,128}... | collective-permute-start | bytes 405512 | tf_op jit(solution)/shard_map/ppermute | solution.py:486
  28.7 0.0 collective-permute-done.beside_a_ref
  28.8 0.6 %all-to-all-done = bf16[64,3,4,128]{3,2,1,0:T(4,128)(2,1)S(1)} async-done(((bf16[64,3,4,128]{3,2,1,0:T(4,128)(2,1)}), bf16[64,3,4,128]{3,2,1,0:T(4,128)(2,1)S(1)}, u32[]{:S(2)}, u32[]{:S(2)}) %all-to-all-start) | async-done | bytes 196640 | tf_op jit(solution)/shard_map/all_to_all | solution.py:475
  29.4 2.9 %collective-permute-start.2 = (f32[96,128]{1,0:T(8,128)S(1)}, f32[96,128]{1,0:T(8,128)S(1)}, u32[]{:S(2)}, u32[]{:S(2)}) collective-permute-start(f32[96,128]{1,0:T(8,128)S(1)} %get-tuple-element.36), channel_id=1, source_target_pairs={{0,1},{2,3},{4,5},{6,7},{1,0},{3,2},{5,4},{7,6},{8,9},{10,11},{12,... | collective-permute-start | bytes 147464 | tf_op jit(solution)/shard_map/ppermute | solution.py:496
  32.3 1.9 %collective-permute-start.3 = (f32[96,128]{1,0:T(8,128)S(1)}, f32[96,128]{1,0:T(8,128)S(1)}, u32[]{:S(2)}, u32[]{:S(2)}) collective-permute-start(f32[96,128]{1,0:T(8,128)S(1)} %get-tuple-element.37), channel_id=1, source_target_pairs={{1,2},{3,4},{5,6},{2,1},{4,3},{6,5},{9,10},{11,12},{13,14},{10,9},... | collective-permute-start | bytes 147464 | tf_op jit(solution)/shard_map/ppermute | solution.py:497
  34.2 1.5 %inner.1 = (bf16[1024,256]{1,0:T(8,128)(2,1)S(1)}, bf16[2,1,1024,128]{3,2,1,0:T(8,128)(2,1)}) custom-call(f32[768,128]{1,0:T(8,128)S(1)} %get-tuple-element.33.rows, bf16[8,256,256]{2,1,0:T(8,128)(2,1)S(1)} %sweeps.1.q_ref), custom_call_target="tpu_custom_call" | custom-call | flops 268435456 | bytes 1048576 | tf_op jit(solution)/shard_map/inner/pallas_call | solution.py:499
  35.7 0.0 collective-permute-done.1.beside_b_ref
  35.7 0.0 collective-permute-done.2.halo_a_ref
  35.7 3.8 %collective-permute-done.3.halo_b_ref = f32[96,128]{1,0:T(8,128)S(1)} collective-permute-done((f32[96,128]{1,0:T(8,128)S(1)}, f32[96,128]{1,0:T(8,128)S(1)}, u32[]{:S(2)}, u32[]{:S(2)}) %collective-permute-start.3) | collective-permute-done | bytes 49184 | tf_op jit(solution)/shard_map/ppermute | solution.py:497
  39.5 3.0 %finish.1 = (bf16[512,128]{1,0:T(8,128)(2,1)}, bf16[2,1,1024,128]{3,2,1,0:T(8,128)(2,1)}) custom-call(f32[8,128]{1,0:T(8,128)S(1)} %get-tuple-element.25.aux_ref, f32[768,128]{1,0:T(8,128)S(1)} %get-tuple-element.33.rows, bf16[528,128]{1,0:T(8,128)(2,1)S(1)} %get-tuple-element.35.mine_ref, ...), custom_call_target="tpu_custom_call", output_to_operand_aliasing={{1}: (9, {})} | custom-call | flops 20000000 | bytes 1048576 | tf_op jit(solution)/shard_map/finish/pallas_call | solution.py:509
  (1 shorter events, 0.0 us)
Async XLA Ops:
  3.6 25.8 %all-to-all-start = ((bf16[64,3,4,128]{3,2,1,0:T(4,128)(2,1)}), bf16[64,3,4,128]{3,2,1,0:T(4,128)(2,1)S(1)}, u32[]{:S(2)}, u32[]{:S(2)}) async-start(bf16[64,3,4,128]{3,2,1,0:T(4,128)(2,1)} %bitcast.1), calls=%async_computation | async-start | bytes 393216 | tf_op jit(solution)/shard_map/all_to_all | solution.py:475
  17.4 11.4 %collective-permute-start = (bf16[528,128]{1,0:T(8,128)(2,1)S(1)}, bf16[528,128]{1,0:T(8,128)(2,1)S(1)}, u32[]{:S(2)}, u32[]{:S(2)}) collective-permute-start(bf16[528,128]{1,0:T(8,128)(2,1)S(1)} %get-tuple-element.35.mine_ref), channel_id=1, source_target_pairs={{0,8},{16,24},{32,40},{48,56},{64,72},{80,88},{96,104},{112,120},{... | collective-permute-start | bytes 405512 | tf_op jit(solution)/shard_map/ppermute | solution.py:477
  21.7 14.0 %collective-permute-start.1 = (bf16[528,128]{1,0:T(8,128)(2,1)S(1)}, bf16[528,128]{1,0:T(8,128)(2,1)S(1)}, u32[]{:S(2)}, u32[]{:S(2)}) collective-permute-start(bf16[528,128]{1,0:T(8,128)(2,1)S(1)} %get-tuple-element.35.mine_ref), channel_id=1, source_target_pairs={{8,16},{24,32},{40,48},{56,64},{72,80},{88,96},{104,112},{120,128}... | collective-permute-start | bytes 405512 | tf_op jit(solution)/shard_map/ppermute | solution.py:486
  29.4 6.4 %collective-permute-start.2 = (f32[96,128]{1,0:T(8,128)S(1)}, f32[96,128]{1,0:T(8,128)S(1)}, u32[]{:S(2)}, u32[]{:S(2)}) collective-permute-start(f32[96,128]{1,0:T(8,128)S(1)} %get-tuple-element.36), channel_id=1, source_target_pairs={{0,1},{2,3},{4,5},{6,7},{1,0},{3,2},{5,4},{7,6},{8,9},{10,11},{12,... | collective-permute-start | bytes 147464 | tf_op jit(solution)/shard_map/ppermute | solution.py:496
  32.3 7.2 %collective-permute-start.3 = (f32[96,128]{1,0:T(8,128)S(1)}, f32[96,128]{1,0:T(8,128)S(1)}, u32[]{:S(2)}, u32[]{:S(2)}) collective-permute-start(f32[96,128]{1,0:T(8,128)S(1)} %get-tuple-element.37), channel_id=1, source_target_pairs={{1,2},{3,4},{5,6},{2,1},{4,3},{6,5},{9,10},{11,12},{13,14},{10,9},... | collective-permute-start | bytes 147464 | tf_op jit(solution)/shard_map/ppermute | solution.py:497

commit v8 on v7

--- a/solution.py
+++ b/solution.py
@@ -83,9 +83,9 @@
         groups[v * 8 : v * 8 + 8, :] = grouped(coefs[:8, v * 128 : v * 128 + 128])
         spans[v * 8 : v * 8 + 8, :] = grouped(coefs[8:, v * 128 : v * 128 + 128])
     first, last = coefs[:, :128], coefs[:, tiles * 128 - 128 :]
-    is_even = even("bus")
-    a_ref[...] = jnp.where(is_even, last, first)
-    b_ref[...] = jnp.where(is_even, first, last)
+    is_odd = ~even("bus")
+    a_ref[...] = jnp.where(is_odd, last, first)
+    b_ref[...] = jnp.where(is_odd, first, last)
     harm = lax.axis_index("harm")
     span = spans[pl.ds(harm, 1), :]
     aux_ref[1:2, :] = span
@@ -179,10 +179,10 @@
     rows_ref[...] = got_ref[...].astype(F32)
     first, last = rows_ref[:16, :], pltpu.roll(rows_ref[size - 16 :, :], ROWS, 0)
     far = rows_ref[pl.ds(FAR, H, stride=ROWS), :]
-    is_even = even("bus")
+    is_odd = ~even("bus")
     for ref, edge, range_rows in (
-        (out_a_ref, a_ref, jnp.where(is_even, last, first)),
-        (out_b_ref, b_ref, jnp.where(is_even, first, last)),
+        (out_a_ref, a_ref, jnp.where(is_odd, last, first)),
+        (out_b_ref, b_ref, jnp.where(is_odd, first, last)),
     ):
         ref[:16, :] = range_rows
         ref[16:32, :] = edge[...]
@@ -273,9 +273,9 @@
     near_hbm, volt_hbm, near, volt, out, sems,
 ):
     del done_hbm
-    is_even = even("bus")
-    low = jnp.where(is_even, halo_b_ref[...], halo_a_ref[...])
-    high = jnp.where(is_even, halo_a_ref[...], halo_b_ref[...])
+    is_odd = ~even("bus")
+    low = jnp.where(is_odd, halo_b_ref[...], halo_a_ref[...])
+    high = jnp.where(is_odd, halo_a_ref[...], halo_b_ref[...])
     edges(low, high, inject_ref, coef_ref, volt)
     harm = lax.axis_index("harm")
     far = rows[pl.ds(FAR, H, stride=ROWS), :]
@@ -366,22 +366,18 @@
     table = lax.dot_general(high, match, dims, preferred_element_type=F32)
     table += lax.dot_general(rest, match, dims, preferred_element_type=F32)
 
-    step = 16
-    for h in range(0, H, step):
-        total = [[jnp.zeros((step, 128), F32) for _ in range(2)] for _ in range(CONV)]
-        for q in range(3):
-            for o in range(CONV):
-                at = 2 * o * H + h
-                spec_r, spec_i = (lifts[q][at + p * H : at + p * H + step, :].astype(F32) for p in range(2))
-                for c in range(CONV):
-                    at = c * 3 * CONV + q * CONV + o
-                    weights = (table[h : h + step, n : n + 1] for n in (at, 64 + at))
-                    add_r, add_i = product(*weights, spec_r, spec_i)
-                    total[c][0] += add_r
-                    total[c][1] += add_i
-        for c in range(CONV):
-            for p in range(2):
-                out[pl.ds((p * H + h) * CONV + c, step, stride=CONV), :] = total[c][p]
+    total = [[jnp.zeros((H, 128), F32) for _ in range(2)] for _ in range(CONV)]
+    for q in range(3):
+        for o in range(CONV):
+            spec_r, spec_i = (lifts[q][(2 * o + p) * H : (2 * o + p + 1) * H, :].astype(F32) for p in range(2))
+            for c in range(CONV):
+                at = c * 3 * CONV + q * CONV + o
+                add_r, add_i = product(table[:, at : at + 1], table[:, 64 + at : 65 + at], spec_r, spec_i)
+                total[c][0] += add_r
+                total[c][1] += add_i
+    for c in range(CONV):
+        for p in range(2):
+            out[pl.ds(p * H * CONV + c, H, stride=CONV), :] = total[c][p]
 
 
 VMEM = pl.BlockSpec(memory_space=pltpu.VMEM)
@@ -420,7 +416,7 @@
     size = harm_count * ROWS
     kinds = 2 * H
     S = jax.ShapeDtypeStruct
-    over_bus = swaps(bus_count)
+    over_bus = swaps(bus_count)[::-1]
     number = lambda r: r % harm_count * bus_count + r // harm_count
     over_ranges = [[(number(s), number(d)) for s, d in pairs] for pairs in swaps(harm_count * bus_count)]
 

time: 42.8 us -> 43.1 us (level)
  the two profiles are of different devices: /device:TPU:32 before, /device:TPU:24 now
where the time goes in v8:
time: 43.1 us; the launch traced here: 42.9 us
  starting transfers between devices  29.4 us (68%)
  Pallas kernels  9.62 us (22%)
  waiting for transfers between devices  3.11 us (7%)
  between operations  0.72 us (2%)
    all_to_all x1, starting transfers between devices, local(): lax.all_to_all(payload.reshape(four), 'harm', split_axis=0, concat_axis=0...  13.8 us
    ppermute x1, starting transfers between devices, local(): beside_b = lax.ppermute(lift_b, ('harm', 'bus'), over_ranges[1])  7.05 us
    ppermute x1, starting transfers between devices, local(): halo_a = lax.ppermute(halo_a, 'bus', over_bus[0])  4.69 us
    pallas_call x1, Pallas kernels, local(): call(begin_kernel, 'begin', (S((16, block), F32), S((16, 128), F32), S((1...  2.92 us
    pallas_call x1, Pallas kernels, local(): call(finish_kernel, 'finish', (S((kinds * CONV, snapshots), BF16), out_vo...  2.83 us
    ppermute x1, waiting for transfers between devices, local(): halo_b = lax.ppermute(halo_b, 'bus', over_bus[1])  2.55 us
    pallas_call x1, Pallas kernels, local(): call(sweeps_kernel, 'sweeps', S((tiles, 2 * TILE, WIN), BF16), [VMEM], co...  2.34 us
    ppermute x1, starting transfers between devices, local(): beside_a = lax.ppermute(lift, ('harm', 'bus'), over_ranges[0])  1.96 us
  transfers between devices with their start and end apart: 5, of which 2 were waited for; matrix products, arithmetic and copies ran while one was open for 0% of the time, Pallas kernels for 9%

profile of v8, /device:TPU:24, one launch (start us, length us, event | category | flops | bytes accessed | tf_op | source)
XLA Modules:
  0.0 42.9 jit_solution(6745482686744958892)
XLA Ops:
  0.6 2.9 %begin.1 = (f32[16,1024]{1,0:T(8,128)S(1)}, f32[16,128]{1,0:T(8,128)S(1)}, f32[16,128]{1,0:T(8,128)S(1)}, f32[8,128]{1,0:T(8,128)S(1)}, bf16[768,128]{1,0:T(8,128)(2,1)}, /*index=5*/bf16[528,128]{1,0:T(8,128)(2,1)S(1)}) custom-call(f32[2,4,1,1024]{3,2,1,0:T(1,128)} %adm_hbm.1, s32[3,1024]{1,0:T(4,128)} %off_hbm.1, s32[4]{0:T(128)} %type_hbm.1, f32[8]{0:T(128)} %steep_hbm.1, ...), custom_call_target="tpu_custom_call" | custom-call | flops 268435456 | bytes 1048576 | tf_op jit(solution)/shard_map/begin/pallas_call | solution.py:424
  3.6 13.8 %all-to-all-start = ((bf16[64,3,4,128]{3,2,1,0:T(4,128)(2,1)}), bf16[64,3,4,128]{3,2,1,0:T(4,128)(2,1)S(1)}, u32[]{:S(2)}, u32[]{:S(2)}) async-start(bf16[64,3,4,128]{3,2,1,0:T(4,128)(2,1)} %bitcast.1), calls=%async_computation | async-start | bytes 393216 | tf_op jit(solution)/shard_map/all_to_all | solution.py:471
  17.4 2.0 %collective-permute-start = (bf16[528,128]{1,0:T(8,128)(2,1)S(1)}, bf16[528,128]{1,0:T(8,128)(2,1)S(1)}, u32[]{:S(2)}, u32[]{:S(2)}) collective-permute-start(bf16[528,128]{1,0:T(8,128)(2,1)S(1)} %get-tuple-element.35.mine_ref), channel_id=1, source_target_pairs={{0,8},{16,24},{32,40},{48,56},{64,72},{80,88},{96,104},{112,120},{... | collective-permute-start | bytes 405512 | tf_op jit(solution)/shard_map/ppermute | solution.py:473
  19.3 2.3 %sweeps.1.q_ref = bf16[8,256,256]{2,1,0:T(8,128)(2,1)S(1)} custom-call(f32[16,1024]{1,0:T(8,128)S(1)} %get-tuple-element.28.coef_ref), custom_call_target="tpu_custom_call" | custom-call | flops 536870912 | bytes 1048576 | tf_op jit(solution)/shard_map/sweeps/pallas_call | solution.py:474
  21.7 7.0 %collective-permute-start.1 = (bf16[528,128]{1,0:T(8,128)(2,1)S(1)}, bf16[528,128]{1,0:T(8,128)(2,1)S(1)}, u32[]{:S(2)}, u32[]{:S(2)}) collective-permute-start(bf16[528,128]{1,0:T(8,128)(2,1)S(1)} %get-tuple-element.35.mine_ref), channel_id=1, source_target_pairs={{8,16},{24,32},{40,48},{56,64},{72,80},{88,96},{104,112},{120,128}... | collective-permute-start | bytes 405512 | tf_op jit(solution)/shard_map/ppermute | solution.py:482
  28.7 0.0 collective-permute-done.beside_a_ref
  28.8 0.6 %all-to-all-done = bf16[64,3,4,128]{3,2,1,0:T(4,128)(2,1)S(1)} async-done(((bf16[64,3,4,128]{3,2,1,0:T(4,128)(2,1)}), bf16[64,3,4,128]{3,2,1,0:T(4,128)(2,1)S(1)}, u32[]{:S(2)}, u32[]{:S(2)}) %all-to-all-start) | async-done | bytes 196640 | tf_op jit(solution)/shard_map/all_to_all | solution.py:471
  29.4 4.7 %collective-permute-start.2 = (f32[96,128]{1,0:T(8,128)S(1)}, f32[96,128]{1,0:T(8,128)S(1)}, u32[]{:S(2)}, u32[]{:S(2)}) collective-permute-start(f32[96,128]{1,0:T(8,128)S(1)} %get-tuple-element.36), channel_id=1, source_target_pairs={{1,2},{3,4},{5,6},{2,1},{4,3},{6,5},{9,10},{11,12},{13,14},{10,9},... | collective-permute-start | bytes 147464 | tf_op jit(solution)/shard_map/ppermute | solution.py:492
  34.1 1.9 %collective-permute-start.3 = (f32[96,128]{1,0:T(8,128)S(1)}, f32[96,128]{1,0:T(8,128)S(1)}, u32[]{:S(2)}, u32[]{:S(2)}) collective-permute-start(f32[96,128]{1,0:T(8,128)S(1)} %get-tuple-element.37), channel_id=1, source_target_pairs={{0,1},{2,3},{4,5},{6,7},{1,0},{3,2},{5,4},{7,6},{8,9},{10,11},{12,... | collective-permute-start | bytes 147464 | tf_op jit(solution)/shard_map/ppermute | solution.py:493
  36.0 1.5 %inner.1 = (bf16[1024,256]{1,0:T(8,128)(2,1)S(1)}, bf16[2,1,1024,128]{3,2,1,0:T(8,128)(2,1)}) custom-call(f32[768,128]{1,0:T(8,128)S(1)} %get-tuple-element.33.rows, bf16[8,256,256]{2,1,0:T(8,128)(2,1)S(1)} %sweeps.1.q_ref), custom_call_target="tpu_custom_call" | custom-call | flops 268435456 | bytes 1048576 | tf_op jit(solution)/shard_map/inner/pallas_call | solution.py:495
  37.5 0.0 collective-permute-done.1.beside_b_ref
  37.5 0.0 collective-permute-done.2.halo_a_ref
  37.5 2.5 %collective-permute-done.3.halo_b_ref = f32[96,128]{1,0:T(8,128)S(1)} collective-permute-done((f32[96,128]{1,0:T(8,128)S(1)}, f32[96,128]{1,0:T(8,128)S(1)}, u32[]{:S(2)}, u32[]{:S(2)}) %collective-permute-start.3) | collective-permute-done | bytes 49184 | tf_op jit(solution)/shard_map/ppermute | solution.py:493
  40.0 2.8 %finish.1 = (bf16[512,128]{1,0:T(8,128)(2,1)}, bf16[2,1,1024,128]{3,2,1,0:T(8,128)(2,1)}) custom-call(f32[8,128]{1,0:T(8,128)S(1)} %get-tuple-element.25.aux_ref, f32[768,128]{1,0:T(8,128)S(1)} %get-tuple-element.33.rows, bf16[528,128]{1,0:T(8,128)(2,1)S(1)} %get-tuple-element.35.mine_ref, ...), custom_call_target="tpu_custom_call", output_to_operand_aliasing={{1}: (9, {})} | custom-call | flops 20000000 | bytes 1048576 | tf_op jit(solution)/shard_map/finish/pallas_call | solution.py:505
  (1 shorter events, 0.0 us)
Async XLA Ops:
  3.6 25.8 %all-to-all-start = ((bf16[64,3,4,128]{3,2,1,0:T(4,128)(2,1)}), bf16[64,3,4,128]{3,2,1,0:T(4,128)(2,1)S(1)}, u32[]{:S(2)}, u32[]{:S(2)}) async-start(bf16[64,3,4,128]{3,2,1,0:T(4,128)(2,1)} %bitcast.1), calls=%async_computation | async-start | bytes 393216 | tf_op jit(solution)/shard_map/all_to_all | solution.py:471
  17.4 11.4 %collective-permute-start = (bf16[528,128]{1,0:T(8,128)(2,1)S(1)}, bf16[528,128]{1,0:T(8,128)(2,1)S(1)}, u32[]{:S(2)}, u32[]{:S(2)}) collective-permute-start(bf16[528,128]{1,0:T(8,128)(2,1)S(1)} %get-tuple-element.35.mine_ref), channel_id=1, source_target_pairs={{0,8},{16,24},{32,40},{48,56},{64,72},{80,88},{96,104},{112,120},{... | collective-permute-start | bytes 405512 | tf_op jit(solution)/shard_map/ppermute | solution.py:473
  21.7 15.8 %collective-permute-start.1 = (bf16[528,128]{1,0:T(8,128)(2,1)S(1)}, bf16[528,128]{1,0:T(8,128)(2,1)S(1)}, u32[]{:S(2)}, u32[]{:S(2)}) collective-permute-start(bf16[528,128]{1,0:T(8,128)(2,1)S(1)} %get-tuple-element.35.mine_ref), channel_id=1, source_target_pairs={{8,16},{24,32},{40,48},{56,64},{72,80},{88,96},{104,112},{120,128}... | collective-permute-start | bytes 405512 | tf_op jit(solution)/shard_map/ppermute | solution.py:482
  29.4 8.1 %collective-permute-start.2 = (f32[96,128]{1,0:T(8,128)S(1)}, f32[96,128]{1,0:T(8,128)S(1)}, u32[]{:S(2)}, u32[]{:S(2)}) collective-permute-start(f32[96,128]{1,0:T(8,128)S(1)} %get-tuple-element.36), channel_id=1, source_target_pairs={{1,2},{3,4},{5,6},{2,1},{4,3},{6,5},{9,10},{11,12},{13,14},{10,9},... | collective-permute-start | bytes 147464 | tf_op jit(solution)/shard_map/ppermute | solution.py:492
  34.1 6.0 %collective-permute-start.3 = (f32[96,128]{1,0:T(8,128)S(1)}, f32[96,128]{1,0:T(8,128)S(1)}, u32[]{:S(2)}, u32[]{:S(2)}) collective-permute-start(f32[96,128]{1,0:T(8,128)S(1)} %get-tuple-element.37), channel_id=1, source_target_pairs={{0,1},{2,3},{4,5},{6,7},{1,0},{3,2},{5,4},{7,6},{8,9},{10,11},{12,... | collective-permute-start | bytes 147464 | tf_op jit(solution)/shard_map/ppermute | solution.py:493

commit v9 on v8

--- a/solution.py
+++ b/solution.py
@@ -22,7 +22,7 @@
 PAIR = 9
 FAR = 10
 MARK = 11
-LIFT = 8 * H
+LIFT = CONV * 128
 HALF = 32
 F32 = jnp.float32
 BF16 = jnp.bfloat16
@@ -112,23 +112,23 @@
     volts[...] = volt_in[...].astype(F32)
     kinds = 2 * H
     volt = jnp.concatenate(
-        [volts[pl.ds(c, kinds, stride=CONV), :] for c in range(CONV)], axis=1
+        [volts[pl.ds(c, kinds, stride=CONV), :].T for c in range(CONV)], axis=0
     ).astype(BF16)
-    sharp = jnp.concatenate([jnp.full((1, 128), steep[kind[c]], F32) for c in range(CONV)], axis=1)
-    strong = jnp.concatenate([power[c : c + 1, :] for c in range(CONV)], axis=1)
-    spectra = jnp.zeros((kinds, CONV * 128), F32)
+    sharp = jnp.concatenate([jnp.full((128, 1), steep[kind[c]], F32) for c in range(CONV)], axis=0)
+    strong = jnp.concatenate([power[...], jnp.zeros((8 - CONV, 128), F32)], axis=0).T
+    strong = jnp.concatenate([strong[:, c : c + 1] for c in range(CONV)], axis=0)
+    spectra = jnp.zeros((CONV * 128, kinds), F32)
     step = 256
     for n in range(0, NT, step):
-        wave = jnp.dot(turned[n : n + step, :], volt, preferred_element_type=F32)
+        wave = jnp.dot(volt, basis[:, n : n + step], preferred_element_type=F32)
         current = (strong * jnp.tanh(sharp * wave)).astype(BF16)
-        spectra += jnp.dot(basis[:, n : n + step], current, preferred_element_type=F32)
+        spectra += jnp.dot(current, turned[n : n + step, :], preferred_element_type=F32)
     spectra = spectra * NT ** (-0.5)
+    lift_ref[:LIFT, :] = spectra.astype(BF16)
     for c in range(CONV):
+        piece = spectra[c * 128 : c * 128 + 128].T
         for p in range(2):
-            piece = spectra[p * H : p * H + H, c * 128 : c * 128 + 128]
-            at = (2 * c + p) * H
-            rows[pl.ds(2 * c + p, H, stride=ROWS), :] = piece
-            lift_ref[at : at + H, :] = piece.astype(BF16)
+            rows[pl.ds(2 * c + p, H, stride=ROWS), :] = piece[p * H : p * H + H]
     row = iota((16, 128), 0)
     notes = jnp.where(row == 0, span, jnp.where(row == 1, mark, 0.0))
     lift_ref[LIFT:, :] = notes.astype(BF16)
@@ -184,9 +184,9 @@
         (out_a_ref, a_ref, jnp.where(is_odd, last, first)),
         (out_b_ref, b_ref, jnp.where(is_odd, first, last)),
     ):
-        ref[:16, :] = range_rows
-        ref[16:32, :] = edge[...]
-        ref[32:, :] = far
+        ref[:16, :] = range_rows.astype(BF16)
+        ref[16:32, :] = edge[...].astype(BF16)
+        ref[32:, :] = far.astype(BF16)
 
 
 def inner_kernel(rows, q_ref, inject, volt_hbm, volt, sems):
@@ -270,17 +270,17 @@
 
 def finish_kernel(
     aux_ref, rows, mine_ref, beside_a_ref, beside_b_ref, halo_a_ref, halo_b_ref, inject_ref, coef_ref, done_hbm,
-    near_hbm, volt_hbm, near, volt, out, sems,
+    near_hbm, volt_hbm, near, volt, table, sums, out, sems,
 ):
     del done_hbm
     is_odd = ~even("bus")
-    low = jnp.where(is_odd, halo_b_ref[...], halo_a_ref[...])
-    high = jnp.where(is_odd, halo_a_ref[...], halo_b_ref[...])
+    halo_a, halo_b = halo_a_ref[...].astype(F32), halo_b_ref[...].astype(F32)
+    low, high = jnp.where(is_odd, halo_b, halo_a), jnp.where(is_odd, halo_a, halo_b)
     edges(low, high, inject_ref, coef_ref, volt)
     harm = lax.axis_index("harm")
     far = rows[pl.ds(FAR, H, stride=ROWS), :]
     far = jnp.where(harm == 0, low[32:], jnp.where(harm == H - 1, high[32:], far))
-    near_converters(aux_ref, rows, far, (mine_ref, beside_a_ref, beside_b_ref), out)
+    near_converters(aux_ref, rows, far, (mine_ref, beside_a_ref, beside_b_ref), table, sums, out)
     near[...] = out[...].astype(BF16)
     copies = [pltpu.make_async_copy(near, near_hbm, sems.at[4])]
     for e in range(2):
@@ -293,7 +293,7 @@
         copy.wait()
 
 
-def near_converters(aux_ref, rows, far, lifts, out):
+def near_converters(aux_ref, rows, far, lifts, table, sums, out):
     harm = lax.axis_index("harm")
     is_even = even("harm")
     a_at = jnp.where(is_even, 2, 0)
@@ -360,24 +360,31 @@
     wide = iota(many, 1)
     match = (row // 64 == wide // 64) & (row % 64 // (3 * CONV) == wide % 64 // 16) & (bus_of == bus2[:1])
     match = jnp.where(match, 1.0, 0.0).astype(BF16)
+    weight = jnp.concatenate([weight, weight], axis=0)
     high = weight.astype(BF16)
     rest = (weight - high.astype(F32)).astype(BF16)
     dims = (((1,), (1,)), ((), ()))
-    table = lax.dot_general(high, match, dims, preferred_element_type=F32)
-    table += lax.dot_general(rest, match, dims, preferred_element_type=F32)
-
-    total = [[jnp.zeros((H, 128), F32) for _ in range(2)] for _ in range(CONV)]
-    for q in range(3):
-        for o in range(CONV):
-            spec_r, spec_i = (lifts[q][(2 * o + p) * H : (2 * o + p + 1) * H, :].astype(F32) for p in range(2))
-            for c in range(CONV):
-                at = c * 3 * CONV + q * CONV + o
-                add_r, add_i = product(table[:, at : at + 1], table[:, 64 + at : 65 + at], spec_r, spec_i)
-                total[c][0] += add_r
-                total[c][1] += add_i
+    found = lax.dot_general(match, high, dims, preferred_element_type=F32)
+    found += lax.dot_general(match, rest, dims, preferred_element_type=F32)
+    table[:64, :] = found[:64]
+    table[64:, :] = jnp.where(iota((64, 128), 1) < 64, -found[64:], found[64:])
+
+    step = 32
+    for at in range(0, 128, step):
+        total = [jnp.zeros((step, 128), F32) for _ in range(CONV)]
+        for q in range(3):
+            for o in range(CONV):
+                spec = lifts[q][o * 128 + at : o * 128 + at + step, :].astype(F32)
+                turned = swapped(spec)
+                for c in range(CONV):
+                    n = c * 3 * CONV + q * CONV + o
+                    total[c] += table[n : n + 1, :] * spec + table[64 + n : 65 + n, :] * turned
+        for c in range(CONV):
+            sums[c * 128 + at : c * 128 + at + step, :] = total[c]
     for c in range(CONV):
+        turned = sums[c * 128 : c * 128 + 128, :].T
         for p in range(2):
-            out[pl.ds(p * H * CONV + c, H, stride=CONV), :] = total[c][p]
+            out[pl.ds(p * H * CONV + c, H, stride=CONV), :] = turned[p * H : p * H + H]
 
 
 VMEM = pl.BlockSpec(memory_space=pltpu.VMEM)
@@ -482,7 +489,7 @@
     beside_b = lax.ppermute(lift_b, ("harm", "bus"), over_ranges[1])
     got, q, beside_a = lax.optimization_barrier((got, q, beside_a))
 
-    halo = S((32 + harm_count, 128), F32)
+    halo = S((32 + harm_count, 128), BF16)
     rows, halo_a, halo_b = call(
         mix_kernel,
         "mix",
@@ -510,6 +517,8 @@
         [
             pltpu.VMEM((kinds * CONV, snapshots), BF16),
             pltpu.VMEM((2, 2, EDGE, snapshots), BF16),
+            pltpu.VMEM((128, 128), F32),
+            pltpu.VMEM((CONV * 128, 128), F32),
             pltpu.VMEM((kinds * CONV, 128), F32),
             pltpu.SemaphoreType.DMA((5,)),
         ],

time: 43.1 us -> 44 us (1.021)
  Pallas kernels: 9.62 us -> 10.7 us
    pallas_call x1, Pallas kernels: 2.92 us -> 4.32 us  [local(): call(begin_kernel, 'begin', (S((16, block), F32), S((16, 128), F32), S((1...]
where the time goes in v9:
time: 44 us; the launch traced here: 43.7 us
  starting transfers between devices  29.4 us (67%)
  Pallas kernels  10.7 us (24%)
  waiting for transfers between devices  2.85 us (6%)
  between operations  0.72 us (2%)
    all_to_all x1, starting transfers between devices, local(): lax.all_to_all(payload.reshape(four), 'harm', split_axis=0, concat_axis=0...  13.8 us
    ppermute x1, starting transfers between devices, local(): beside_b = lax.ppermute(lift_b, ('harm', 'bus'), over_ranges[1])  7.05 us
    ppermute x1, starting transfers between devices, local(): halo_a = lax.ppermute(halo_a, 'bus', over_bus[0])  4.7 us
    pallas_call x1, Pallas kernels, local(): call(begin_kernel, 'begin', (S((16, block), F32), S((16, 128), F32), S((1...  4.32 us
    pallas_call x1, Pallas kernels, local(): call(finish_kernel, 'finish', (S((kinds * CONV, snapshots), BF16), out_vo...  2.57 us
    pallas_call x1, Pallas kernels, local(): call(sweeps_kernel, 'sweeps', S((tiles, 2 * TILE, WIN), BF16), [VMEM], co...  2.34 us
    ppermute x1, waiting for transfers between devices, local(): halo_b = lax.ppermute(halo_b, 'bus', over_bus[1])  2.29 us
    ppermute x1, starting transfers between devices, local(): beside_a = lax.ppermute(lift, ('harm', 'bus'), over_ranges[0])  1.96 us
  transfers between devices with their start and end apart: 5, of which 2 were waited for; matrix products, arithmetic and copies ran while one was open for 0% of the time, Pallas kernels for 9%

profile of v9, /device:TPU:24, one launch (start us, length us, event | category | flops | bytes accessed | tf_op | source)
XLA Modules:
  0.0 43.7 jit_solution(2098652717909623416)
XLA Ops:
  0.6 4.3 %begin.1 = (f32[16,1024]{1,0:T(8,128)S(1)}, f32[16,128]{1,0:T(8,128)S(1)}, f32[16,128]{1,0:T(8,128)S(1)}, f32[8,128]{1,0:T(8,128)S(1)}, bf16[768,128]{1,0:T(8,128)(2,1)}, /*index=5*/bf16[528,128]{1,0:T(8,128)(2,1)S(1)}) custom-call(f32[2,4,1,1024]{3,2,1,0:T(1,128)} %adm_hbm.1, s32[3,1024]{1,0:T(4,128)} %off_hbm.1, s32[4]{0:T(128)} %type_hbm.1, f32[8]{0:T(128)} %steep_hbm.1, ...), custom_call_target="tpu_custom_call" | custom-call | flops 268435456 | bytes 1048576 | tf_op jit(solution)/shard_map/begin/pallas_call | solution.py:431
  5.0 13.8 %all-to-all-start = ((bf16[64,3,4,128]{3,2,1,0:T(4,128)(2,1)}), bf16[64,3,4,128]{3,2,1,0:T(4,128)(2,1)S(1)}, u32[]{:S(2)}, u32[]{:S(2)}) async-start(bf16[64,3,4,128]{3,2,1,0:T(4,128)(2,1)} %bitcast.1), calls=%async_computation | async-start | bytes 393216 | tf_op jit(solution)/shard_map/all_to_all | solution.py:478
  18.8 2.0 %collective-permute-start = (bf16[528,128]{1,0:T(8,128)(2,1)S(1)}, bf16[528,128]{1,0:T(8,128)(2,1)S(1)}, u32[]{:S(2)}, u32[]{:S(2)}) collective-permute-start(bf16[528,128]{1,0:T(8,128)(2,1)S(1)} %get-tuple-element.35.mine_ref), channel_id=1, source_target_pairs={{0,8},{16,24},{32,40},{48,56},{64,72},{80,88},{96,104},{112,120},{... | collective-permute-start | bytes 405512 | tf_op jit(solution)/shard_map/ppermute | solution.py:480
  20.7 2.3 %sweeps.1.q_ref = bf16[8,256,256]{2,1,0:T(8,128)(2,1)S(1)} custom-call(f32[16,1024]{1,0:T(8,128)S(1)} %get-tuple-element.28.coef_ref), custom_call_target="tpu_custom_call" | custom-call | flops 536870912 | bytes 1048576 | tf_op jit(solution)/shard_map/sweeps/pallas_call | solution.py:481
  23.1 7.0 %collective-permute-start.1 = (bf16[528,128]{1,0:T(8,128)(2,1)S(1)}, bf16[528,128]{1,0:T(8,128)(2,1)S(1)}, u32[]{:S(2)}, u32[]{:S(2)}) collective-permute-start(bf16[528,128]{1,0:T(8,128)(2,1)S(1)} %get-tuple-element.35.mine_ref), channel_id=1, source_target_pairs={{8,16},{24,32},{40,48},{56,64},{72,80},{88,96},{104,112},{120,128}... | collective-permute-start | bytes 405512 | tf_op jit(solution)/shard_map/ppermute | solution.py:489
  30.1 0.0 collective-permute-done.beside_a_ref
  30.2 0.6 %all-to-all-done = bf16[64,3,4,128]{3,2,1,0:T(4,128)(2,1)S(1)} async-done(((bf16[64,3,4,128]{3,2,1,0:T(4,128)(2,1)}), bf16[64,3,4,128]{3,2,1,0:T(4,128)(2,1)S(1)}, u32[]{:S(2)}, u32[]{:S(2)}) %all-to-all-start) | async-done | bytes 196640 | tf_op jit(solution)/shard_map/all_to_all | solution.py:478
  30.7 4.7 %collective-permute-start.2 = (bf16[96,128]{1,0:T(8,128)(2,1)S(1)}, bf16[96,128]{1,0:T(8,128)(2,1)S(1)}, u32[]{:S(2)}, u32[]{:S(2)}) collective-permute-start(bf16[96,128]{1,0:T(8,128)(2,1)S(1)} %get-tuple-element.36), channel_id=1, source_target_pairs={{1,2},{3,4},{5,6},{2,1},{4,3},{6,5},{9,10},{11,12},{13,14},{10,9},... | collective-permute-start | bytes 73736 | tf_op jit(solution)/shard_map/ppermute | solution.py:499
  35.5 1.9 %collective-permute-start.3 = (bf16[96,128]{1,0:T(8,128)(2,1)S(1)}, bf16[96,128]{1,0:T(8,128)(2,1)S(1)}, u32[]{:S(2)}, u32[]{:S(2)}) collective-permute-start(bf16[96,128]{1,0:T(8,128)(2,1)S(1)} %get-tuple-element.37), channel_id=1, source_target_pairs={{0,1},{2,3},{4,5},{6,7},{1,0},{3,2},{5,4},{7,6},{8,9},{10,11},{12,... | collective-permute-start | bytes 73736 | tf_op jit(solution)/shard_map/ppermute | solution.py:500
  37.4 1.5 %inner.1 = (bf16[1024,256]{1,0:T(8,128)(2,1)S(1)}, bf16[2,1,1024,128]{3,2,1,0:T(8,128)(2,1)}) custom-call(f32[768,128]{1,0:T(8,128)S(1)} %get-tuple-element.33.rows, bf16[8,256,256]{2,1,0:T(8,128)(2,1)S(1)} %sweeps.1.q_ref), custom_call_target="tpu_custom_call" | custom-call | flops 268435456 | bytes 1048576 | tf_op jit(solution)/shard_map/inner/pallas_call | solution.py:502
  38.9 0.0 collective-permute-done.1.beside_b_ref
  38.9 0.0 collective-permute-done.2.halo_a_ref
  38.9 2.3 %collective-permute-done.3.halo_b_ref = bf16[96,128]{1,0:T(8,128)(2,1)S(1)} collective-permute-done((bf16[96,128]{1,0:T(8,128)(2,1)S(1)}, bf16[96,128]{1,0:T(8,128)(2,1)S(1)}, u32[]{:S(2)}, u32[]{:S(2)}) %collective-permute-start.3) | collective-permute-done | bytes 24608 | tf_op jit(solution)/shard_map/ppermute | solution.py:500
  41.2 2.6 %finish.1 = (bf16[512,128]{1,0:T(8,128)(2,1)}, bf16[2,1,1024,128]{3,2,1,0:T(8,128)(2,1)}) custom-call(f32[8,128]{1,0:T(8,128)S(1)} %get-tuple-element.25.aux_ref, f32[768,128]{1,0:T(8,128)S(1)} %get-tuple-element.33.rows, bf16[528,128]{1,0:T(8,128)(2,1)S(1)} %get-tuple-element.35.mine_ref, ...), custom_call_target="tpu_custom_call", output_to_operand_aliasing={{1}: (9, {})} | custom-call | flops 20000000 | bytes 1048576 | tf_op jit(solution)/shard_map/finish/pallas_call | solution.py:512
  (1 shorter events, 0.0 us)
Async XLA Ops:
  5.0 25.8 %all-to-all-start = ((bf16[64,3,4,128]{3,2,1,0:T(4,128)(2,1)}), bf16[64,3,4,128]{3,2,1,0:T(4,128)(2,1)S(1)}, u32[]{:S(2)}, u32[]{:S(2)}) async-start(bf16[64,3,4,128]{3,2,1,0:T(4,128)(2,1)} %bitcast.1), calls=%async_computation | async-start | bytes 393216 | tf_op jit(solution)/shard_map/all_to_all | solution.py:478
  18.8 11.4 %collective-permute-start = (bf16[528,128]{1,0:T(8,128)(2,1)S(1)}, bf16[528,128]{1,0:T(8,128)(2,1)S(1)}, u32[]{:S(2)}, u32[]{:S(2)}) collective-permute-start(bf16[528,128]{1,0:T(8,128)(2,1)S(1)} %get-tuple-element.35.mine_ref), channel_id=1, source_target_pairs={{0,8},{16,24},{32,40},{48,56},{64,72},{80,88},{96,104},{112,120},{... | collective-permute-start | bytes 405512 | tf_op jit(solution)/shard_map/ppermute | solution.py:480
  23.1 15.8 %collective-permute-start.1 = (bf16[528,128]{1,0:T(8,128)(2,1)S(1)}, bf16[528,128]{1,0:T(8,128)(2,1)S(1)}, u32[]{:S(2)}, u32[]{:S(2)}) collective-permute-start(bf16[528,128]{1,0:T(8,128)(2,1)S(1)} %get-tuple-element.35.mine_ref), channel_id=1, source_target_pairs={{8,16},{24,32},{40,48},{56,64},{72,80},{88,96},{104,112},{120,128}... | collective-permute-start | bytes 405512 | tf_op jit(solution)/shard_map/ppermute | solution.py:489
  30.7 8.1 %collective-permute-start.2 = (bf16[96,128]{1,0:T(8,128)(2,1)S(1)}, bf16[96,128]{1,0:T(8,128)(2,1)S(1)}, u32[]{:S(2)}, u32[]{:S(2)}) collective-permute-start(bf16[96,128]{1,0:T(8,128)(2,1)S(1)} %get-tuple-element.36), channel_id=1, source_target_pairs={{1,2},{3,4},{5,6},{2,1},{4,3},{6,5},{9,10},{11,12},{13,14},{10,9},... | collective-permute-start | bytes 73736 | tf_op jit(solution)/shard_map/ppermute | solution.py:499
  35.5 5.7 %collective-permute-start.3 = (bf16[96,128]{1,0:T(8,128)(2,1)S(1)}, bf16[96,128]{1,0:T(8,128)(2,1)S(1)}, u32[]{:S(2)}, u32[]{:S(2)}) collective-permute-start(bf16[96,128]{1,0:T(8,128)(2,1)S(1)} %get-tuple-element.37), channel_id=1, source_target_pairs={{0,1},{2,3},{4,5},{6,7},{1,0},{3,2},{5,4},{7,6},{8,9},{10,11},{12,... | collective-permute-start | bytes 73736 | tf_op jit(solution)/shard_map/ppermute | solution.py:500

commit v10 on v9

--- a/solution.py
+++ b/solution.py
@@ -59,13 +59,17 @@
 
 def begin_kernel(
     adm_hbm, off_hbm, type_hbm, steep_hbm, bus_hbm, power_hbm, volt_hbm, turned_hbm, basis_hbm,
-    coef_ref, a_ref, b_ref, aux_ref, out_ref, lift_ref,
-    adm, off, kind, steep, bus, power, volt_in, turned, basis, volts, groups, spans, rows, sems,
+    coef_ref, a_ref, b_ref, aux_ref, spec_ref, out_hbm,
+    adm, off, kind, steep, bus, power, volt_in, turned, basis, volts, groups, spans, rows, sent, sems,
 ):
     pairs = [
         (adm_hbm, adm), (off_hbm, off), (type_hbm, kind), (steep_hbm, steep), (bus_hbm, bus), (power_hbm, power),
-        (volt_hbm, volt_in), (turned_hbm, turned), (basis_hbm, basis),
+        (volt_hbm, volt_in),
     ]
+    for at in range(0, NT, NT // 2):
+        pairs.append((turned_hbm.at[pl.ds(at, NT // 2)], turned.at[pl.ds(at, NT // 2)]))
+    for at in (0, H):
+        pairs.append((basis_hbm.at[pl.ds(at, H)], basis.at[pl.ds(at, H)]))
     copies = [pltpu.make_async_copy(src, dst, sems.at[i]) for i, (src, dst) in enumerate(pairs)]
     for copy in copies:
         copy.start()
@@ -112,27 +116,31 @@
     volts[...] = volt_in[...].astype(F32)
     kinds = 2 * H
     volt = jnp.concatenate(
-        [volts[pl.ds(c, kinds, stride=CONV), :].T for c in range(CONV)], axis=0
+        [volts[pl.ds(c, kinds, stride=CONV), :] for c in range(CONV)], axis=1
     ).astype(BF16)
-    sharp = jnp.concatenate([jnp.full((128, 1), steep[kind[c]], F32) for c in range(CONV)], axis=0)
-    strong = jnp.concatenate([power[...], jnp.zeros((8 - CONV, 128), F32)], axis=0).T
-    strong = jnp.concatenate([strong[:, c : c + 1] for c in range(CONV)], axis=0)
-    spectra = jnp.zeros((CONV * 128, kinds), F32)
+    sharp = jnp.concatenate([jnp.full((1, 128), steep[kind[c]], F32) for c in range(CONV)], axis=1)
+    strong = jnp.concatenate([power[c : c + 1, :] for c in range(CONV)], axis=1)
+    spectra = jnp.zeros((kinds, CONV * 128), F32)
     step = 256
     for n in range(0, NT, step):
-        wave = jnp.dot(volt, basis[:, n : n + step], preferred_element_type=F32)
+        wave = jnp.dot(turned[n : n + step, :], volt, preferred_element_type=F32)
         current = (strong * jnp.tanh(sharp * wave)).astype(BF16)
-        spectra += jnp.dot(current, turned[n : n + step, :], preferred_element_type=F32)
+        spectra += jnp.dot(basis[:, n : n + step], current, preferred_element_type=F32)
     spectra = spectra * NT ** (-0.5)
-    lift_ref[:LIFT, :] = spectra.astype(BF16)
+    spec_ref[...] = spectra
     for c in range(CONV):
-        piece = spectra[c * 128 : c * 128 + 128].T
         for p in range(2):
-            rows[pl.ds(2 * c + p, H, stride=ROWS), :] = piece[p * H : p * H + H]
-    row = iota((16, 128), 0)
-    notes = jnp.where(row == 0, span, jnp.where(row == 1, mark, 0.0))
-    lift_ref[LIFT:, :] = notes.astype(BF16)
-    out_ref[...] = rows[...].astype(BF16)
+            rows[pl.ds(2 * c + p, H, stride=ROWS), :] = spectra[p * H : p * H + H, c * 128 : c * 128 + 128]
+    aux_ref[3:4, :] = mark
+    size = rows.shape[0] // 4
+    copies = []
+    for at in range(0, 4 * size, size):
+        part = pl.ds(at, size)
+        sent[part, :] = rows[part, :].astype(BF16)
+        copies.append(pltpu.make_async_copy(sent.at[part], out_hbm.at[part], sems.at[at // size]))
+        copies[-1].start()
+    for copy in copies:
+        copy.wait()
 
 
 def sweeps_matrix(coefs, first, count):
@@ -165,7 +173,12 @@
     return (acc[:count, :128] - acc[count:, 128:]).astype(BF16), (acc[:count, 128:] + acc[count:, :128]).astype(BF16)
 
 
-def sweeps_kernel(coef_ref, q_ref):
+def sweeps_kernel(coef_ref, spec_ref, aux_ref, q_ref, lift_ref):
+    for c in range(CONV):
+        lift_ref[c * 128 : c * 128 + 128, :] = spec_ref[:, c * 128 : c * 128 + 128].T.astype(BF16)
+    row = iota((16, 128), 0)
+    notes = jnp.where(row == 0, aux_ref[1:2, :], jnp.where(row == 1, aux_ref[3:4, :], 0.0))
+    lift_ref[LIFT:, :] = notes.astype(BF16)
     blank = jnp.zeros((coef_ref.shape[0], TILE), F32)
     tiles = q_ref.shape[0]
     for b in range(tiles):
@@ -428,7 +441,7 @@
     over_ranges = [[(number(s), number(d)) for s, d in pairs] for pairs in swaps(harm_count * bus_count)]
 
     basis = make_basis()
-    coef, edge_a, edge_b, aux, payload, lift = call(
+    coef, edge_a, edge_b, aux, spectra, payload = call(
         begin_kernel,
         "begin",
         (
@@ -436,8 +449,8 @@
             S((16, 128), F32),
             S((16, 128), F32),
             S((8, 128), F32),
+            S((kinds, CONV * 128), F32),
             S((size, 128), BF16),
-            S((LIFT + 16, 128), BF16),
         ),
         [HBM] * 9,
         [
@@ -454,9 +467,11 @@
             pltpu.VMEM((harm_count, 128), F32),
             pltpu.VMEM((harm_count, 128), F32),
             pltpu.VMEM((size, 128), F32),
-            pltpu.SemaphoreType.DMA((9,)),
+            pltpu.VMEM((size, 128), BF16),
+            pltpu.SemaphoreType.DMA((11,)),
         ],
         (2 * 2 * 128 * 1024 * 512, 2**20, 2**19),
+        (VMEM,) * 5 + (HBM,),
     )(
         *(
             pltpu.with_memory_space_constraint(array, pltpu.HBM)
@@ -477,16 +492,15 @@
     four = (harm_count, ROWS // 4, 4, snapshots)
     got = lax.all_to_all(payload.reshape(four), "harm", split_axis=0, concat_axis=0, tiled=True)
 
-    beside_a = lax.ppermute(lift, ("harm", "bus"), over_ranges[0])
-    q = call(
+    q, lift = call(
         sweeps_kernel,
         "sweeps",
-        S((tiles, 2 * TILE, WIN), BF16),
-        [VMEM],
+        (S((tiles, 2 * TILE, WIN), BF16), S((LIFT + 16, 128), BF16)),
+        [VMEM] * 3,
         cost=(2 * tiles * 256 * 256 * 512, 2**20, 0),
-    )(coef)
-    lift_b, q = lax.optimization_barrier((lift, q))
-    beside_b = lax.ppermute(lift_b, ("harm", "bus"), over_ranges[1])
+    )(coef, spectra, aux)
+    beside_a = lax.ppermute(lift, ("harm", "bus"), over_ranges[0])
+    beside_b = lax.ppermute(lift, ("harm", "bus"), over_ranges[1])
     got, q, beside_a = lax.optimization_barrier((got, q, beside_a))
 
     halo = S((32 + harm_count, 128), BF16)

time: 44 us -> 42.7 us (0.970)
  Pallas kernels: 10.7 us -> 9.45 us
    pallas_call x1, Pallas kernels: 4.32 us -> 2.98 us  [local(): call(begin_kernel, 'begin', (S((16, block), F32), S((16, 128), F32), S((1...]
where the time goes in v10:
time: 42.7 us; the launch traced here: 42.4 us
  starting transfers between devices  29.4 us (69%)
  Pallas kernels  9.45 us (22%)
  waiting for transfers between devices  2.81 us (7%)
  between operations  0.72 us (2%)
    all_to_all x1, starting transfers between devices, local(): lax.all_to_all(payload.reshape(four), 'harm', split_axis=0, concat_axis=0...  13.8 us
    ppermute x1, starting transfers between devices, local(): beside_b = lax.ppermute(lift, ('harm', 'bus'), over_ranges[1])  7.05 us
    ppermute x1, starting transfers between devices, local(): halo_a = lax.ppermute(halo_a, 'bus', over_bus[0])  4.69 us
    pallas_call x1, Pallas kernels, local(): call(begin_kernel, 'begin', (S((16, block), F32), S((16, 128), F32), S((1...  2.98 us
    pallas_call x1, Pallas kernels, local(): call(finish_kernel, 'finish', (S((kinds * CONV, snapshots), BF16), out_vo...  2.58 us
    pallas_call x1, Pallas kernels, local(): call(sweeps_kernel, 'sweeps', (S((tiles, 2 * TILE, WIN), BF16), S((LIFT +...  2.38 us
    ppermute x1, waiting for transfers between devices, local(): halo_b = lax.ppermute(halo_b, 'bus', over_bus[1])  2.29 us
    ppermute x1, starting transfers between devices, local(): beside_a = lax.ppermute(lift, ('harm', 'bus'), over_ranges[0])  1.96 us
  transfers between devices with their start and end apart: 5, of which 2 were waited for; matrix products, arithmetic and copies ran while one was open for 0% of the time, Pallas kernels for 9%

profile of v10, /device:TPU:24, one launch (start us, length us, event | category | flops | bytes accessed | tf_op | source)
XLA Modules:
  0.0 42.4 jit_solution(3395473047541824675)
XLA Ops:
  0.6 3.0 %begin.1 = (f32[16,1024]{1,0:T(8,128)S(1)}, f32[16,128]{1,0:T(8,128)S(1)}, f32[16,128]{1,0:T(8,128)S(1)}, f32[8,128]{1,0:T(8,128)S(1)}, f32[128,512]{1,0:T(8,128)S(1)}, /*index=5*/bf16[768,128]{1,0:T(8,128)(2,1)}) custom-call(f32[2,4,1,1024]{3,2,1,0:T(1,128)} %adm_hbm.1, s32[3,1024]{1,0:T(4,128)} %off_hbm.1, s32[4]{0:T(128)} %type_hbm.1, f32[8]{0:T(128)} %steep_hbm.1, ...), custom_call_target="tpu_custom_call" | custom-call | flops 268435456 | bytes 1048576 | tf_op jit(solution)/shard_map/begin/pallas_call | solution.py:444
  3.6 13.8 %all-to-all-start = ((bf16[64,3,4,128]{3,2,1,0:T(4,128)(2,1)}), bf16[64,3,4,128]{3,2,1,0:T(4,128)(2,1)S(1)}, u32[]{:S(2)}, u32[]{:S(2)}) async-start(bf16[64,3,4,128]{3,2,1,0:T(4,128)(2,1)} %bitcast.1), calls=%async_computation | async-start | bytes 393216 | tf_op jit(solution)/shard_map/all_to_all | solution.py:493
  17.4 2.4 %sweeps.1 = (bf16[8,256,256]{2,1,0:T(8,128)(2,1)S(1)}, bf16[528,128]{1,0:T(8,128)(2,1)S(1)}) custom-call(f32[16,1024]{1,0:T(8,128)S(1)} %get-tuple-element.27.coef_ref, f32[128,512]{1,0:T(8,128)S(1)} %get-tuple-element.28.spec_ref, f32[8,128]{1,0:T(8,128)S(1)} %get-tuple-element.25.aux_ref), custom_call_target="tpu_custom_call" | custom-call | flops 536870912 | bytes 1048576 | tf_op jit(solution)/shard_map/sweeps/pallas_call | solution.py:495
  19.8 2.0 %collective-permute-start = (bf16[528,128]{1,0:T(8,128)(2,1)S(1)}, bf16[528,128]{1,0:T(8,128)(2,1)S(1)}, u32[]{:S(2)}, u32[]{:S(2)}) collective-permute-start(bf16[528,128]{1,0:T(8,128)(2,1)S(1)} %get-tuple-element.30.mine_ref), channel_id=1, source_target_pairs={{0,8},{16,24},{32,40},{48,56},{64,72},{80,88},{96,104},{112,120},{... | collective-permute-start | bytes 405512 | tf_op jit(solution)/shard_map/ppermute | solution.py:502
  21.8 7.0 %collective-permute-start.1 = (bf16[528,128]{1,0:T(8,128)(2,1)S(1)}, bf16[528,128]{1,0:T(8,128)(2,1)S(1)}, u32[]{:S(2)}, u32[]{:S(2)}) collective-permute-start(bf16[528,128]{1,0:T(8,128)(2,1)S(1)} %get-tuple-element.30.mine_ref), channel_id=1, source_target_pairs={{8,16},{24,32},{40,48},{56,64},{72,80},{88,96},{104,112},{120,128}... | collective-permute-start | bytes 405512 | tf_op jit(solution)/shard_map/ppermute | solution.py:503
  28.9 0.0 collective-permute-done.beside_a_ref
  28.9 0.5 %all-to-all-done = bf16[64,3,4,128]{3,2,1,0:T(4,128)(2,1)S(1)} async-done(((bf16[64,3,4,128]{3,2,1,0:T(4,128)(2,1)}), bf16[64,3,4,128]{3,2,1,0:T(4,128)(2,1)S(1)}, u32[]{:S(2)}, u32[]{:S(2)}) %all-to-all-start) | async-done | bytes 196640 | tf_op jit(solution)/shard_map/all_to_all | solution.py:493
  29.4 4.7 %collective-permute-start.2 = (bf16[96,128]{1,0:T(8,128)(2,1)S(1)}, bf16[96,128]{1,0:T(8,128)(2,1)S(1)}, u32[]{:S(2)}, u32[]{:S(2)}) collective-permute-start(bf16[96,128]{1,0:T(8,128)(2,1)S(1)} %get-tuple-element.36), channel_id=1, source_target_pairs={{1,2},{3,4},{5,6},{2,1},{4,3},{6,5},{9,10},{11,12},{13,14},{10,9},... | collective-permute-start | bytes 73736 | tf_op jit(solution)/shard_map/ppermute | solution.py:513
  34.1 1.9 %collective-permute-start.3 = (bf16[96,128]{1,0:T(8,128)(2,1)S(1)}, bf16[96,128]{1,0:T(8,128)(2,1)S(1)}, u32[]{:S(2)}, u32[]{:S(2)}) collective-permute-start(bf16[96,128]{1,0:T(8,128)(2,1)S(1)} %get-tuple-element.37), channel_id=1, source_target_pairs={{0,1},{2,3},{4,5},{6,7},{1,0},{3,2},{5,4},{7,6},{8,9},{10,11},{12,... | collective-permute-start | bytes 73736 | tf_op jit(solution)/shard_map/ppermute | solution.py:514
  36.0 1.5 %inner.1 = (bf16[1024,256]{1,0:T(8,128)(2,1)S(1)}, bf16[2,1,1024,128]{3,2,1,0:T(8,128)(2,1)}) custom-call(f32[768,128]{1,0:T(8,128)S(1)} %get-tuple-element.34.rows, bf16[8,256,256]{2,1,0:T(8,128)(2,1)S(1)} %get-tuple-element.38.q_ref), custom_call_target="tpu_custom_call" | custom-call | flops 268435456 | bytes 1048576 | tf_op jit(solution)/shard_map/inner/pallas_call | solution.py:516
  37.5 0.0 collective-permute-done.1.beside_b_ref
  37.5 0.0 collective-permute-done.2.halo_a_ref
  37.5 2.3 %collective-permute-done.3.halo_b_ref = bf16[96,128]{1,0:T(8,128)(2,1)S(1)} collective-permute-done((bf16[96,128]{1,0:T(8,128)(2,1)S(1)}, bf16[96,128]{1,0:T(8,128)(2,1)S(1)}, u32[]{:S(2)}, u32[]{:S(2)}) %collective-permute-start.3) | collective-permute-done | bytes 24608 | tf_op jit(solution)/shard_map/ppermute | solution.py:514
  39.8 2.6 %finish.1 = (bf16[512,128]{1,0:T(8,128)(2,1)}, bf16[2,1,1024,128]{3,2,1,0:T(8,128)(2,1)}) custom-call(f32[8,128]{1,0:T(8,128)S(1)} %get-tuple-element.25.aux_ref, f32[768,128]{1,0:T(8,128)S(1)} %get-tuple-element.34.rows, bf16[528,128]{1,0:T(8,128)(2,1)S(1)} %get-tuple-element.30.mine_ref, ...), custom_call_target="tpu_custom_call", output_to_operand_aliasing={{1}: (9, {})} | custom-call | flops 20000000 | bytes 1048576 | tf_op jit(solution)/shard_map/finish/pallas_call | solution.py:526
  (1 shorter events, 0.0 us)
Async XLA Ops:
  3.6 25.8 %all-to-all-start = ((bf16[64,3,4,128]{3,2,1,0:T(4,128)(2,1)}), bf16[64,3,4,128]{3,2,1,0:T(4,128)(2,1)S(1)}, u32[]{:S(2)}, u32[]{:S(2)}) async-start(bf16[64,3,4,128]{3,2,1,0:T(4,128)(2,1)} %bitcast.1), calls=%async_computation | async-start | bytes 393216 | tf_op jit(solution)/shard_map/all_to_all | solution.py:493
  19.8 9.0 %collective-permute-start = (bf16[528,128]{1,0:T(8,128)(2,1)S(1)}, bf16[528,128]{1,0:T(8,128)(2,1)S(1)}, u32[]{:S(2)}, u32[]{:S(2)}) collective-permute-start(bf16[528,128]{1,0:T(8,128)(2,1)S(1)} %get-tuple-element.30.mine_ref), channel_id=1, source_target_pairs={{0,8},{16,24},{32,40},{48,56},{64,72},{80,88},{96,104},{112,120},{... | collective-permute-start | bytes 405512 | tf_op jit(solution)/shard_map/ppermute | solution.py:502
  21.8 15.7 %collective-permute-start.1 = (bf16[528,128]{1,0:T(8,128)(2,1)S(1)}, bf16[528,128]{1,0:T(8,128)(2,1)S(1)}, u32[]{:S(2)}, u32[]{:S(2)}) collective-permute-start(bf16[528,128]{1,0:T(8,128)(2,1)S(1)} %get-tuple-element.30.mine_ref), channel_id=1, source_target_pairs={{8,16},{24,32},{40,48},{56,64},{72,80},{88,96},{104,112},{120,128}... | collective-permute-start | bytes 405512 | tf_op jit(solution)/shard_map/ppermute | solution.py:503
  29.4 8.1 %collective-permute-start.2 = (bf16[96,128]{1,0:T(8,128)(2,1)S(1)}, bf16[96,128]{1,0:T(8,128)(2,1)S(1)}, u32[]{:S(2)}, u32[]{:S(2)}) collective-permute-start(bf16[96,128]{1,0:T(8,128)(2,1)S(1)} %get-tuple-element.36), channel_id=1, source_target_pairs={{1,2},{3,4},{5,6},{2,1},{4,3},{6,5},{9,10},{11,12},{13,14},{10,9},... | collective-permute-start | bytes 73736 | tf_op jit(solution)/shard_map/ppermute | solution.py:513
  34.1 5.7 %collective-permute-start.3 = (bf16[96,128]{1,0:T(8,128)(2,1)S(1)}, bf16[96,128]{1,0:T(8,128)(2,1)S(1)}, u32[]{:S(2)}, u32[]{:S(2)}) collective-permute-start(bf16[96,128]{1,0:T(8,128)(2,1)S(1)} %get-tuple-element.37), channel_id=1, source_target_pairs={{0,1},{2,3},{4,5},{6,7},{1,0},{3,2},{5,4},{7,6},{8,9},{10,11},{12,... | collective-permute-start | bytes 73736 | tf_op jit(solution)/shard_map/ppermute | solution.py:514

commit v11 on v10

--- a/solution.py
+++ b/solution.py
@@ -202,7 +202,11 @@
         ref[32:, :] = far.astype(BF16)
 
 
-def inner_kernel(rows, q_ref, inject, volt_hbm, volt, sems):
+def inner_kernel(
+    rows, q_ref, aux_ref, mine_ref, beside_a_ref, beside_b_ref, inject, found_ref, pick_ref, match_ref, volt_hbm, volt, sems
+):
+    aim(aux_ref, rows, (mine_ref, beside_a_ref, beside_b_ref), found_ref, pick_ref, match_ref)
+
     def part(p):
         return jnp.concatenate(
             [
@@ -282,7 +286,8 @@
 
 
 def finish_kernel(
-    aux_ref, rows, mine_ref, beside_a_ref, beside_b_ref, halo_a_ref, halo_b_ref, inject_ref, coef_ref, done_hbm,
+    found_ref, pick_ref, match_ref, rows, mine_ref, beside_a_ref, beside_b_ref, halo_a_ref, halo_b_ref, inject_ref,
+    coef_ref, done_hbm,
     near_hbm, volt_hbm, near, volt, table, sums, out, sems,
 ):
     del done_hbm
@@ -293,7 +298,7 @@
     harm = lax.axis_index("harm")
     far = rows[pl.ds(FAR, H, stride=ROWS), :]
     far = jnp.where(harm == 0, low[32:], jnp.where(harm == H - 1, high[32:], far))
-    near_converters(aux_ref, rows, far, (mine_ref, beside_a_ref, beside_b_ref), table, sums, out)
+    near_converters(found_ref, pick_ref, match_ref, far, (mine_ref, beside_a_ref, beside_b_ref), table, sums, out)
     near[...] = out[...].astype(BF16)
     copies = [pltpu.make_async_copy(near, near_hbm, sems.at[4])]
     for e in range(2):
@@ -306,7 +311,7 @@
         copy.wait()
 
 
-def near_converters(aux_ref, rows, far, lifts, table, sums, out):
+def aim(aux_ref, rows, lifts, found_ref, pick_ref, match_ref):
     harm = lax.axis_index("harm")
     is_even = even("harm")
     a_at = jnp.where(is_even, 2, 0)
@@ -344,19 +349,11 @@
     bus2 = hop(bus1, line2)
     places = [coef_at(bus0, line1, valid & (path >= 1)), coef_at(bus1, line2, two), coef_at(bus2, 0, valid)]
     pick = jnp.where(iota((3 * 128, 3 * 128), 0) == jnp.concatenate(places, axis=1), 1.0, 0.0).astype(BF16)
+    pick_ref[...] = pick[256:]
     window = jnp.concatenate(
-        [
-            rows[pl.ds(COEF, H, stride=ROWS), :].astype(BF16),
-            rows[pl.ds(PAIR, H, stride=ROWS), :].astype(BF16),
-            far.astype(BF16),
-        ],
-        axis=1,
-    )
-    found = jnp.dot(window, pick, preferred_element_type=F32)
-    real, path = real[:1], path[:1]
-    first = found[:, :128] + jnp.where(real & (path == 0), 1.0, 0.0)
-    second = found[:, 128:256] + jnp.where(real & (path <= LINKS), 1.0, 0.0)
-    weight = packed_product(packed_product(first, second, real), found[:, 256:], real)
+        [rows[pl.ds(COEF, H, stride=ROWS), :], rows[pl.ds(PAIR, H, stride=ROWS), :]], axis=1
+    ).astype(BF16)
+    found_ref[...] = jnp.dot(window, pick[:256], preferred_element_type=F32)
 
     many = (128, 128)
     row = iota(many, 0)
@@ -372,13 +369,23 @@
             bus_of = jnp.where(other == q * CONV + c, bus, bus_of)
     wide = iota(many, 1)
     match = (row // 64 == wide // 64) & (row % 64 // (3 * CONV) == wide % 64 // 16) & (bus_of == bus2[:1])
-    match = jnp.where(match, 1.0, 0.0).astype(BF16)
+    match_ref[...] = jnp.where(match, 1.0, 0.0).astype(BF16)
+
+
+def near_converters(found_ref, pick_ref, match_ref, far, lifts, table, sums, out):
+    lane = iota((1, 128), 1)
+    real, path = lane < 64, lane % 16
+    found = found_ref[...] + jnp.dot(far.astype(BF16), pick_ref[...], preferred_element_type=F32)
+    first = found[:, :128] + jnp.where(real & (path == 0), 1.0, 0.0)
+    second = found[:, 128:256] + jnp.where(real & (path <= LINKS), 1.0, 0.0)
+    weight = packed_product(packed_product(first, second, real), found[:, 256:], real)
+
     weight = jnp.concatenate([weight, weight], axis=0)
     high = weight.astype(BF16)
     rest = (weight - high.astype(F32)).astype(BF16)
     dims = (((1,), (1,)), ((), ()))
-    found = lax.dot_general(match, high, dims, preferred_element_type=F32)
-    found += lax.dot_general(match, rest, dims, preferred_element_type=F32)
+    found = lax.dot_general(match_ref[...], high, dims, preferred_element_type=F32)
+    found += lax.dot_general(match_ref[...], rest, dims, preferred_element_type=F32)
     table[:64, :] = found[:64]
     table[64:, :] = jnp.where(iota((64, 128), 1) < 64, -found[64:], found[64:])
 
@@ -513,21 +520,21 @@
     halo_a = lax.ppermute(halo_a, "bus", over_bus[0])
     halo_b = lax.ppermute(halo_b, "bus", over_bus[1])
     out_volt = S((2, 1, block, snapshots), BF16)
-    inject, bus_volt = call(
+    inject, found, pick, match, bus_volt = call(
         inner_kernel,
         "inner",
-        (S((block, 256), BF16), out_volt),
-        [VMEM] * 2,
+        (S((block, 256), BF16), S((harm_count, 384), F32), S((128, 384), BF16), S((128, 128), BF16), out_volt),
+        [VMEM] * 6,
         [pltpu.VMEM((2, 1, block, snapshots), BF16), pltpu.SemaphoreType.DMA((tiles,))],
         (2 * tiles * 256 * 256 * 256, 2**20, 0),
-        (VMEM, HBM),
-    )(rows, q)
-    beside_b, halo_a, halo_b, inject, bus_volt = lax.optimization_barrier((beside_b, halo_a, halo_b, inject, bus_volt))
+        (VMEM,) * 4 + (HBM,),
+    )(rows, q, aux, lift, beside_a, beside_b)
+    halo_a, halo_b, inject, bus_volt = lax.optimization_barrier((halo_a, halo_b, inject, bus_volt))
     near, bus_volt = call(
         finish_kernel,
         "finish",
         (S((kinds * CONV, snapshots), BF16), out_volt),
-        [VMEM] * 9 + [HBM],
+        [VMEM] * 11 + [HBM],
         [
             pltpu.VMEM((kinds * CONV, snapshots), BF16),
             pltpu.VMEM((2, 2, EDGE, snapshots), BF16),
@@ -538,8 +545,8 @@
         ],
         (2 * 10**7, 2**20, 0),
         (HBM, HBM),
-        {9: 1},
-    )(aux, rows, lift, beside_a, beside_b, halo_a, halo_b, inject, coef, bus_volt)
+        {11: 1},
+    )(found, pick, match, rows, lift, beside_a, beside_b, halo_a, halo_b, inject, coef, bus_volt)
     return (bus_volt, near.reshape(2, H, CONV, snapshots))
 
 

time: 42.7 us -> 42.4 us (level)
  transfers between devices with their start and end apart: 5 -> 5, of which waited for: 2 -> 2; matrix products, arithmetic and copies ran while one was open for 0% -> 0% of each run, Pallas kernels for 9% -> 10%
where the time goes in v11:
time: 42.4 us; the launch traced here: 42.1 us
  starting transfers between devices  29.4 us (69%)
  Pallas kernels  9.4 us (22%)
  waiting for transfers between devices  2.57 us (6%)
  between operations  0.72 us (2%)
    all_to_all x1, starting transfers between devices, local(): lax.all_to_all(payload.reshape(four), 'harm', split_axis=0, concat_axis=0...  13.8 us
    ppermute x1, starting transfers between devices, local(): beside_b = lax.ppermute(lift, ('harm', 'bus'), over_ranges[1])  7.05 us
    ppermute x1, starting transfers between devices, local(): halo_a = lax.ppermute(halo_a, 'bus', over_bus[0])  4.69 us
    pallas_call x1, Pallas kernels, local(): call(begin_kernel, 'begin', (S((16, block), F32), S((16, 128), F32), S((1...  2.98 us
    pallas_call x1, Pallas kernels, local(): call(sweeps_kernel, 'sweeps', (S((tiles, 2 * TILE, WIN), BF16), S((LIFT +...  2.38 us
    pallas_call x1, Pallas kernels, local(): call(finish_kernel, 'finish', (S((kinds * CONV, snapshots), BF16), out_vo...  2.28 us
    ppermute x1, waiting for transfers between devices, local(): halo_b = lax.ppermute(halo_b, 'bus', over_bus[1])  2.05 us
    ppermute x1, starting transfers between devices, local(): beside_a = lax.ppermute(lift, ('harm', 'bus'), over_ranges[0])  1.96 us
  transfers between devices with their start and end apart: 5, of which 2 were waited for; matrix products, arithmetic and copies ran while one was open for 0% of the time, Pallas kernels for 10%

profile of v11, /device:TPU:24, one launch (start us, length us, event | category | flops | bytes accessed | tf_op | source)
XLA Modules:
  0.0 42.1 jit_solution(2745579795322449757)
XLA Ops:
  0.6 3.0 %begin.1 = (f32[16,1024]{1,0:T(8,128)S(1)}, f32[16,128]{1,0:T(8,128)S(1)}, f32[16,128]{1,0:T(8,128)S(1)}, f32[8,128]{1,0:T(8,128)S(1)}, f32[128,512]{1,0:T(8,128)S(1)}, /*index=5*/bf16[768,128]{1,0:T(8,128)(2,1)}) custom-call(f32[2,4,1,1024]{3,2,1,0:T(1,128)} %adm_hbm.1, s32[3,1024]{1,0:T(4,128)} %off_hbm.1, s32[4]{0:T(128)} %type_hbm.1, f32[8]{0:T(128)} %steep_hbm.1, ...), custom_call_target="tpu_custom_call" | custom-call | flops 268435456 | bytes 1048576 | tf_op jit(solution)/shard_map/begin/pallas_call | solution.py:451
  3.6 13.8 %all-to-all-start = ((bf16[64,3,4,128]{3,2,1,0:T(4,128)(2,1)}), bf16[64,3,4,128]{3,2,1,0:T(4,128)(2,1)S(1)}, u32[]{:S(2)}, u32[]{:S(2)}) async-start(bf16[64,3,4,128]{3,2,1,0:T(4,128)(2,1)} %bitcast.1), calls=%async_computation | async-start | bytes 393216 | tf_op jit(solution)/shard_map/all_to_all | solution.py:500
  17.4 2.4 %sweeps.1 = (bf16[8,256,256]{2,1,0:T(8,128)(2,1)S(1)}, bf16[528,128]{1,0:T(8,128)(2,1)S(1)}) custom-call(f32[16,1024]{1,0:T(8,128)S(1)} %get-tuple-element.28.coef_ref, f32[128,512]{1,0:T(8,128)S(1)} %get-tuple-element.29.spec_ref, f32[8,128]{1,0:T(8,128)S(1)} %get-tuple-element.30.aux_ref), custom_call_target="tpu_custom_call" | custom-call | flops 536870912 | bytes 1048576 | tf_op jit(solution)/shard_map/sweeps/pallas_call | solution.py:502
  19.8 2.0 %collective-permute-start = (bf16[528,128]{1,0:T(8,128)(2,1)S(1)}, bf16[528,128]{1,0:T(8,128)(2,1)S(1)}, u32[]{:S(2)}, u32[]{:S(2)}) collective-permute-start(bf16[528,128]{1,0:T(8,128)(2,1)S(1)} %get-tuple-element.32.mine_ref), channel_id=1, source_target_pairs={{0,8},{16,24},{32,40},{48,56},{64,72},{80,88},{96,104},{112,120},{... | collective-permute-start | bytes 405512 | tf_op jit(solution)/shard_map/ppermute | solution.py:509
  21.8 7.0 %collective-permute-start.1 = (bf16[528,128]{1,0:T(8,128)(2,1)S(1)}, bf16[528,128]{1,0:T(8,128)(2,1)S(1)}, u32[]{:S(2)}, u32[]{:S(2)}) collective-permute-start(bf16[528,128]{1,0:T(8,128)(2,1)S(1)} %get-tuple-element.32.mine_ref), channel_id=1, source_target_pairs={{8,16},{24,32},{40,48},{56,64},{72,80},{88,96},{104,112},{120,128}... | collective-permute-start | bytes 405512 | tf_op jit(solution)/shard_map/ppermute | solution.py:510
  28.9 0.0 collective-permute-done.beside_a_ref
  28.9 0.5 %all-to-all-done = bf16[64,3,4,128]{3,2,1,0:T(4,128)(2,1)S(1)} async-done(((bf16[64,3,4,128]{3,2,1,0:T(4,128)(2,1)}), bf16[64,3,4,128]{3,2,1,0:T(4,128)(2,1)S(1)}, u32[]{:S(2)}, u32[]{:S(2)}) %all-to-all-start) | async-done | bytes 196640 | tf_op jit(solution)/shard_map/all_to_all | solution.py:500
  29.4 4.7 %collective-permute-start.2 = (bf16[96,128]{1,0:T(8,128)(2,1)S(1)}, bf16[96,128]{1,0:T(8,128)(2,1)S(1)}, u32[]{:S(2)}, u32[]{:S(2)}) collective-permute-start(bf16[96,128]{1,0:T(8,128)(2,1)S(1)} %get-tuple-element.42), channel_id=1, source_target_pairs={{1,2},{3,4},{5,6},{2,1},{4,3},{6,5},{9,10},{11,12},{13,14},{10,9},... | collective-permute-start | bytes 73736 | tf_op jit(solution)/shard_map/ppermute | solution.py:520
  34.1 1.9 %collective-permute-start.3 = (bf16[96,128]{1,0:T(8,128)(2,1)S(1)}, bf16[96,128]{1,0:T(8,128)(2,1)S(1)}, u32[]{:S(2)}, u32[]{:S(2)}) collective-permute-start(bf16[96,128]{1,0:T(8,128)(2,1)S(1)} %get-tuple-element.43), channel_id=1, source_target_pairs={{0,1},{2,3},{4,5},{6,7},{1,0},{3,2},{5,4},{7,6},{8,9},{10,11},{12,... | collective-permute-start | bytes 73736 | tf_op jit(solution)/shard_map/ppermute | solution.py:521
  36.0 0.0 collective-permute-done.1.beside_b_ref
  36.1 1.7 %inner.1 = (bf16[1024,256]{1,0:T(8,128)(2,1)S(1)}, f32[64,384]{1,0:T(8,128)S(1)}, bf16[128,384]{1,0:T(8,128)(2,1)S(1)}, bf16[128,128]{1,0:T(8,128)(2,1)S(1)}, bf16[2,1,1024,128]{3,2,1,0:T(8,128)(2,1)}) custom-call(f32[768,128]{1,0:T(8,128)S(1)} %get-tuple-element.36.rows, bf16[8,256,256]{2,1,0:T(8,128)(2,1)S(1)} %get-tuple-element.37.q_ref, ...), custom_call_target="tpu_custom_call" | custom-call | flops 268435456 | bytes 1048576 | tf_op jit(solution)/shard_map/inner/pallas_call | solution.py:523
  37.8 0.0 collective-permute-done.2.halo_a_ref
  37.8 2.0 %collective-permute-done.3.halo_b_ref = bf16[96,128]{1,0:T(8,128)(2,1)S(1)} collective-permute-done((bf16[96,128]{1,0:T(8,128)(2,1)S(1)}, bf16[96,128]{1,0:T(8,128)(2,1)S(1)}, u32[]{:S(2)}, u32[]{:S(2)}) %collective-permute-start.3) | collective-permute-done | bytes 24608 | tf_op jit(solution)/shard_map/ppermute | solution.py:521
  39.8 2.3 %finish.1 = (bf16[512,128]{1,0:T(8,128)(2,1)}, bf16[2,1,1024,128]{3,2,1,0:T(8,128)(2,1)}) custom-call(f32[64,384]{1,0:T(8,128)S(1)} %get-tuple-element.39.found_ref, bf16[128,384]{1,0:T(8,128)(2,1)S(1)} %get-tuple-element.40.pick_ref, bf16[128,128]{1,0:T(8,128)(2,1)S(1)} %get-tuple-element.41.match_ref, ...), custom_call_target="tpu_custom_call", output_to_operand_aliasing={{1}: (11, {})} | custom-call | flops 20000000 | bytes 1048576 | tf_op jit(solution)/shard_map/finish/pallas_call | solution.py:533
  (1 shorter events, 0.0 us)
Async XLA Ops:
  3.6 25.8 %all-to-all-start = ((bf16[64,3,4,128]{3,2,1,0:T(4,128)(2,1)}), bf16[64,3,4,128]{3,2,1,0:T(4,128)(2,1)S(1)}, u32[]{:S(2)}, u32[]{:S(2)}) async-start(bf16[64,3,4,128]{3,2,1,0:T(4,128)(2,1)} %bitcast.1), calls=%async_computation | async-start | bytes 393216 | tf_op jit(solution)/shard_map/all_to_all | solution.py:500
  19.8 9.0 %collective-permute-start = (bf16[528,128]{1,0:T(8,128)(2,1)S(1)}, bf16[528,128]{1,0:T(8,128)(2,1)S(1)}, u32[]{:S(2)}, u32[]{:S(2)}) collective-permute-start(bf16[528,128]{1,0:T(8,128)(2,1)S(1)} %get-tuple-element.32.mine_ref), channel_id=1, source_target_pairs={{0,8},{16,24},{32,40},{48,56},{64,72},{80,88},{96,104},{112,120},{... | collective-permute-start | bytes 405512 | tf_op jit(solution)/shard_map/ppermute | solution.py:509
  21.8 14.2 %collective-permute-start.1 = (bf16[528,128]{1,0:T(8,128)(2,1)S(1)}, bf16[528,128]{1,0:T(8,128)(2,1)S(1)}, u32[]{:S(2)}, u32[]{:S(2)}) collective-permute-start(bf16[528,128]{1,0:T(8,128)(2,1)S(1)} %get-tuple-element.32.mine_ref), channel_id=1, source_target_pairs={{8,16},{24,32},{40,48},{56,64},{72,80},{88,96},{104,112},{120,128}... | collective-permute-start | bytes 405512 | tf_op jit(solution)/shard_map/ppermute | solution.py:510
  29.4 8.4 %collective-permute-start.2 = (bf16[96,128]{1,0:T(8,128)(2,1)S(1)}, bf16[96,128]{1,0:T(8,128)(2,1)S(1)}, u32[]{:S(2)}, u32[]{:S(2)}) collective-permute-start(bf16[96,128]{1,0:T(8,128)(2,1)S(1)} %get-tuple-element.42), channel_id=1, source_target_pairs={{1,2},{3,4},{5,6},{2,1},{4,3},{6,5},{9,10},{11,12},{13,14},{10,9},... | collective-permute-start | bytes 73736 | tf_op jit(solution)/shard_map/ppermute | solution.py:520
  34.1 5.7 %collective-permute-start.3 = (bf16[96,128]{1,0:T(8,128)(2,1)S(1)}, bf16[96,128]{1,0:T(8,128)(2,1)S(1)}, u32[]{:S(2)}, u32[]{:S(2)}) collective-permute-start(bf16[96,128]{1,0:T(8,128)(2,1)S(1)} %get-tuple-element.43), channel_id=1, source_target_pairs={{0,1},{2,3},{4,5},{6,7},{1,0},{3,2},{5,4},{7,6},{8,9},{10,11},{12,... | collective-permute-start | bytes 73736 | tf_op jit(solution)/shard_map/ppermute | solution.py:521

commit v12 on v11

--- a/solution.py
+++ b/solution.py
@@ -87,7 +87,7 @@
         groups[v * 8 : v * 8 + 8, :] = grouped(coefs[:8, v * 128 : v * 128 + 128])
         spans[v * 8 : v * 8 + 8, :] = grouped(coefs[8:, v * 128 : v * 128 + 128])
     first, last = coefs[:, :128], coefs[:, tiles * 128 - 128 :]
-    is_odd = ~even("bus")
+    is_odd = even("bus")
     a_ref[...] = jnp.where(is_odd, last, first)
     b_ref[...] = jnp.where(is_odd, first, last)
     harm = lax.axis_index("harm")
@@ -192,7 +192,7 @@
     rows_ref[...] = got_ref[...].astype(F32)
     first, last = rows_ref[:16, :], pltpu.roll(rows_ref[size - 16 :, :], ROWS, 0)
     far = rows_ref[pl.ds(FAR, H, stride=ROWS), :]
-    is_odd = ~even("bus")
+    is_odd = even("bus")
     for ref, edge, range_rows in (
         (out_a_ref, a_ref, jnp.where(is_odd, last, first)),
         (out_b_ref, b_ref, jnp.where(is_odd, first, last)),
@@ -291,7 +291,7 @@
     near_hbm, volt_hbm, near, volt, table, sums, out, sems,
 ):
     del done_hbm
-    is_odd = ~even("bus")
+    is_odd = even("bus")
     halo_a, halo_b = halo_a_ref[...].astype(F32), halo_b_ref[...].astype(F32)
     low, high = jnp.where(is_odd, halo_b, halo_a), jnp.where(is_odd, halo_a, halo_b)
     edges(low, high, inject_ref, coef_ref, volt)
@@ -443,7 +443,7 @@
     size = harm_count * ROWS
     kinds = 2 * H
     S = jax.ShapeDtypeStruct
-    over_bus = swaps(bus_count)[::-1]
+    over_bus = swaps(bus_count)
     number = lambda r: r % harm_count * bus_count + r // harm_count
     over_ranges = [[(number(s), number(d)) for s, d in pairs] for pairs in swaps(harm_count * bus_count)]
 

time: 42.4 us -> 41.9 us (0.988)
  the two profiles are of different devices: /device:TPU:24 before, /device:TPU:32 now
where the time goes in v12:
time: 41.9 us; the launch traced here: 41.6 us
  starting transfers between devices  27.7 us (66%)
  Pallas kernels  9.4 us (22%)
  waiting for transfers between devices  3.77 us (9%)
  between operations  0.72 us (2%)
    all_to_all x1, starting transfers between devices, local(): lax.all_to_all(payload.reshape(four), 'harm', split_axis=0, concat_axis=0...  13.8 us
    ppermute x1, starting transfers between devices, local(): beside_b = lax.ppermute(lift, ('harm', 'bus'), over_ranges[1])  7.06 us
    ppermute x1, waiting for transfers between devices, local(): halo_b = lax.ppermute(halo_b, 'bus', over_bus[1])  3.26 us
    ppermute x1, starting transfers between devices, local(): halo_a = lax.ppermute(halo_a, 'bus', over_bus[0])  2.99 us
    pallas_call x1, Pallas kernels, local(): call(begin_kernel, 'begin', (S((16, block), F32), S((16, 128), F32), S((1...  2.98 us
    pallas_call x1, Pallas kernels, local(): call(sweeps_kernel, 'sweeps', (S((tiles, 2 * TILE, WIN), BF16), S((LIFT +...  2.38 us
    pallas_call x1, Pallas kernels, local(): call(finish_kernel, 'finish', (S((kinds * CONV, snapshots), BF16), out_vo...  2.28 us
    ppermute x1, starting transfers between devices, local(): beside_a = lax.ppermute(lift, ('harm', 'bus'), over_ranges[0])  1.96 us
  transfers between devices with their start and end apart: 5, of which 2 were waited for; matrix products, arithmetic and copies ran while one was open for 0% of the time, Pallas kernels for 10%

profile of v12, /device:TPU:32, one launch (start us, length us, event | category | flops | bytes accessed | tf_op | source)
XLA Modules:
  0.0 41.6 jit_solution(9750193697933716748)
XLA Ops:
  0.6 3.0 %begin.1 = (f32[16,1024]{1,0:T(8,128)S(1)}, f32[16,128]{1,0:T(8,128)S(1)}, f32[16,128]{1,0:T(8,128)S(1)}, f32[8,128]{1,0:T(8,128)S(1)}, f32[128,512]{1,0:T(8,128)S(1)}, /*index=5*/bf16[768,128]{1,0:T(8,128)(2,1)}) custom-call(f32[2,4,1,1024]{3,2,1,0:T(1,128)} %adm_hbm.1, s32[3,1024]{1,0:T(4,128)} %off_hbm.1, s32[4]{0:T(128)} %type_hbm.1, f32[8]{0:T(128)} %steep_hbm.1, ...), custom_call_target="tpu_custom_call" | custom-call | flops 268435456 | bytes 1048576 | tf_op jit(solution)/shard_map/begin/pallas_call | solution.py:451
  3.6 13.8 %all-to-all-start = ((bf16[64,3,4,128]{3,2,1,0:T(4,128)(2,1)}), bf16[64,3,4,128]{3,2,1,0:T(4,128)(2,1)S(1)}, u32[]{:S(2)}, u32[]{:S(2)}) async-start(bf16[64,3,4,128]{3,2,1,0:T(4,128)(2,1)} %bitcast.1), calls=%async_computation | async-start | bytes 393216 | tf_op jit(solution)/shard_map/all_to_all | solution.py:500
  17.4 2.4 %sweeps.1 = (bf16[8,256,256]{2,1,0:T(8,128)(2,1)S(1)}, bf16[528,128]{1,0:T(8,128)(2,1)S(1)}) custom-call(f32[16,1024]{1,0:T(8,128)S(1)} %get-tuple-element.28.coef_ref, f32[128,512]{1,0:T(8,128)S(1)} %get-tuple-element.29.spec_ref, f32[8,128]{1,0:T(8,128)S(1)} %get-tuple-element.30.aux_ref), custom_call_target="tpu_custom_call" | custom-call | flops 536870912 | bytes 1048576 | tf_op jit(solution)/shard_map/sweeps/pallas_call | solution.py:502
  19.8 2.0 %collective-permute-start = (bf16[528,128]{1,0:T(8,128)(2,1)S(1)}, bf16[528,128]{1,0:T(8,128)(2,1)S(1)}, u32[]{:S(2)}, u32[]{:S(2)}) collective-permute-start(bf16[528,128]{1,0:T(8,128)(2,1)S(1)} %get-tuple-element.32.mine_ref), channel_id=1, source_target_pairs={{0,8},{16,24},{32,40},{48,56},{64,72},{80,88},{96,104},{112,120},{... | collective-permute-start | bytes 405512 | tf_op jit(solution)/shard_map/ppermute | solution.py:509
  21.8 7.1 %collective-permute-start.1 = (bf16[528,128]{1,0:T(8,128)(2,1)S(1)}, bf16[528,128]{1,0:T(8,128)(2,1)S(1)}, u32[]{:S(2)}, u32[]{:S(2)}) collective-permute-start(bf16[528,128]{1,0:T(8,128)(2,1)S(1)} %get-tuple-element.32.mine_ref), channel_id=1, source_target_pairs={{8,16},{24,32},{40,48},{56,64},{72,80},{88,96},{104,112},{120,128}... | collective-permute-start | bytes 405512 | tf_op jit(solution)/shard_map/ppermute | solution.py:510
  28.9 0.0 collective-permute-done.beside_a_ref
  28.9 0.5 %all-to-all-done = bf16[64,3,4,128]{3,2,1,0:T(4,128)(2,1)S(1)} async-done(((bf16[64,3,4,128]{3,2,1,0:T(4,128)(2,1)}), bf16[64,3,4,128]{3,2,1,0:T(4,128)(2,1)S(1)}, u32[]{:S(2)}, u32[]{:S(2)}) %all-to-all-start) | async-done | bytes 196640 | tf_op jit(solution)/shard_map/all_to_all | solution.py:500
  29.4 3.0 %collective-permute-start.2 = (bf16[96,128]{1,0:T(8,128)(2,1)S(1)}, bf16[96,128]{1,0:T(8,128)(2,1)S(1)}, u32[]{:S(2)}, u32[]{:S(2)}) collective-permute-start(bf16[96,128]{1,0:T(8,128)(2,1)S(1)} %get-tuple-element.42), channel_id=1, source_target_pairs={{0,1},{2,3},{4,5},{6,7},{1,0},{3,2},{5,4},{7,6},{8,9},{10,11},{12,... | collective-permute-start | bytes 73736 | tf_op jit(solution)/shard_map/ppermute | solution.py:520
  32.4 1.9 %collective-permute-start.3 = (bf16[96,128]{1,0:T(8,128)(2,1)S(1)}, bf16[96,128]{1,0:T(8,128)(2,1)S(1)}, u32[]{:S(2)}, u32[]{:S(2)}) collective-permute-start(bf16[96,128]{1,0:T(8,128)(2,1)S(1)} %get-tuple-element.43), channel_id=1, source_target_pairs={{1,2},{3,4},{5,6},{2,1},{4,3},{6,5},{9,10},{11,12},{13,14},{10,9},... | collective-permute-start | bytes 73736 | tf_op jit(solution)/shard_map/ppermute | solution.py:521
  34.3 0.0 collective-permute-done.1.beside_b_ref
  34.3 1.7 %inner.1 = (bf16[1024,256]{1,0:T(8,128)(2,1)S(1)}, f32[64,384]{1,0:T(8,128)S(1)}, bf16[128,384]{1,0:T(8,128)(2,1)S(1)}, bf16[128,128]{1,0:T(8,128)(2,1)S(1)}, bf16[2,1,1024,128]{3,2,1,0:T(8,128)(2,1)}) custom-call(f32[768,128]{1,0:T(8,128)S(1)} %get-tuple-element.36.rows, bf16[8,256,256]{2,1,0:T(8,128)(2,1)S(1)} %get-tuple-element.37.q_ref, ...), custom_call_target="tpu_custom_call" | custom-call | flops 268435456 | bytes 1048576 | tf_op jit(solution)/shard_map/inner/pallas_call | solution.py:523
  36.1 0.0 collective-permute-done.2.halo_a_ref
  36.1 3.3 %collective-permute-done.3.halo_b_ref = bf16[96,128]{1,0:T(8,128)(2,1)S(1)} collective-permute-done((bf16[96,128]{1,0:T(8,128)(2,1)S(1)}, bf16[96,128]{1,0:T(8,128)(2,1)S(1)}, u32[]{:S(2)}, u32[]{:S(2)}) %collective-permute-start.3) | collective-permute-done | bytes 24608 | tf_op jit(solution)/shard_map/ppermute | solution.py:521
  39.3 2.3 %finish.1 = (bf16[512,128]{1,0:T(8,128)(2,1)}, bf16[2,1,1024,128]{3,2,1,0:T(8,128)(2,1)}) custom-call(f32[64,384]{1,0:T(8,128)S(1)} %get-tuple-element.39.found_ref, bf16[128,384]{1,0:T(8,128)(2,1)S(1)} %get-tuple-element.40.pick_ref, bf16[128,128]{1,0:T(8,128)(2,1)S(1)} %get-tuple-element.41.match_ref, ...), custom_call_target="tpu_custom_call", output_to_operand_aliasing={{1}: (11, {})} | custom-call | flops 20000000 | bytes 1048576 | tf_op jit(solution)/shard_map/finish/pallas_call | solution.py:533
  (1 shorter events, 0.0 us)
Async XLA Ops:
  3.6 25.7 %all-to-all-start = ((bf16[64,3,4,128]{3,2,1,0:T(4,128)(2,1)}), bf16[64,3,4,128]{3,2,1,0:T(4,128)(2,1)S(1)}, u32[]{:S(2)}, u32[]{:S(2)}) async-start(bf16[64,3,4,128]{3,2,1,0:T(4,128)(2,1)} %bitcast.1), calls=%async_computation | async-start | bytes 393216 | tf_op jit(solution)/shard_map/all_to_all | solution.py:500
  19.8 9.0 %collective-permute-start = (bf16[528,128]{1,0:T(8,128)(2,1)S(1)}, bf16[528,128]{1,0:T(8,128)(2,1)S(1)}, u32[]{:S(2)}, u32[]{:S(2)}) collective-permute-start(bf16[528,128]{1,0:T(8,128)(2,1)S(1)} %get-tuple-element.32.mine_ref), channel_id=1, source_target_pairs={{0,8},{16,24},{32,40},{48,56},{64,72},{80,88},{96,104},{112,120},{... | collective-permute-start | bytes 405512 | tf_op jit(solution)/shard_map/ppermute | solution.py:509
  21.8 12.5 %collective-permute-start.1 = (bf16[528,128]{1,0:T(8,128)(2,1)S(1)}, bf16[528,128]{1,0:T(8,128)(2,1)S(1)}, u32[]{:S(2)}, u32[]{:S(2)}) collective-permute-start(bf16[528,128]{1,0:T(8,128)(2,1)S(1)} %get-tuple-element.32.mine_ref), channel_id=1, source_target_pairs={{8,16},{24,32},{40,48},{56,64},{72,80},{88,96},{104,112},{120,128}... | collective-permute-start | bytes 405512 | tf_op jit(solution)/shard_map/ppermute | solution.py:510
  29.4 6.7 %collective-permute-start.2 = (bf16[96,128]{1,0:T(8,128)(2,1)S(1)}, bf16[96,128]{1,0:T(8,128)(2,1)S(1)}, u32[]{:S(2)}, u32[]{:S(2)}) collective-permute-start(bf16[96,128]{1,0:T(8,128)(2,1)S(1)} %get-tuple-element.42), channel_id=1, source_target_pairs={{0,1},{2,3},{4,5},{6,7},{1,0},{3,2},{5,4},{7,6},{8,9},{10,11},{12,... | collective-permute-start | bytes 73736 | tf_op jit(solution)/shard_map/ppermute | solution.py:520
  32.4 6.9 %collective-permute-start.3 = (bf16[96,128]{1,0:T(8,128)(2,1)S(1)}, bf16[96,128]{1,0:T(8,128)(2,1)S(1)}, u32[]{:S(2)}, u32[]{:S(2)}) collective-permute-start(bf16[96,128]{1,0:T(8,128)(2,1)S(1)} %get-tuple-element.43), channel_id=1, source_target_pairs={{1,2},{3,4},{5,6},{2,1},{4,3},{6,5},{9,10},{11,12},{13,14},{10,9},... | collective-permute-start | bytes 73736 | tf_op jit(solution)/shard_map/ppermute | solution.py:521

commit v13 on v12

--- a/solution.py
+++ b/solution.py
@@ -73,7 +73,7 @@
     copies = [pltpu.make_async_copy(src, dst, sems.at[i]) for i, (src, dst) in enumerate(pairs)]
     for copy in copies:
         copy.start()
-    for copy in copies:
+    for copy in copies[:7]:
         copy.wait()
     inv_r, inv_i = adm[0, 0], adm[1, 0]
     steps = [product(inv_r, inv_i, adm[0, k], adm[1, k]) for k in range(1, 1 + LINKS)]
@@ -120,6 +120,8 @@
     ).astype(BF16)
     sharp = jnp.concatenate([jnp.full((1, 128), steep[kind[c]], F32) for c in range(CONV)], axis=1)
     strong = jnp.concatenate([power[c : c + 1, :] for c in range(CONV)], axis=1)
+    for copy in copies[7:]:
+        copy.wait()
     spectra = jnp.zeros((kinds, CONV * 128), F32)
     step = 256
     for n in range(0, NT, step):
@@ -132,9 +134,9 @@
         for p in range(2):
             rows[pl.ds(2 * c + p, H, stride=ROWS), :] = spectra[p * H : p * H + H, c * 128 : c * 128 + 128]
     aux_ref[3:4, :] = mark
-    size = rows.shape[0] // 4
+    size = rows.shape[0] // 2
     copies = []
-    for at in range(0, 4 * size, size):
+    for at in range(0, 2 * size, size):
         part = pl.ds(at, size)
         sent[part, :] = rows[part, :].astype(BF16)
         copies.append(pltpu.make_async_copy(sent.at[part], out_hbm.at[part], sems.at[at // size]))

time: 41.9 us -> 41.9 us (level)
  no operation moved by 1% of the time
where the time goes in v13:
time: 41.9 us; the launch traced here: 41.6 us
  starting transfers between devices  27.7 us (66%)
  Pallas kernels  9.42 us (22%)
  waiting for transfers between devices  3.78 us (9%)
  between operations  0.72 us (2%)
    all_to_all x1, starting transfers between devices, local(): lax.all_to_all(payload.reshape(four), 'harm', split_axis=0, concat_axis=0...  13.8 us
    ppermute x1, starting transfers between devices, local(): beside_b = lax.ppermute(lift, ('harm', 'bus'), over_ranges[1])  7.05 us
    ppermute x1, waiting for transfers between devices, local(): halo_b = lax.ppermute(halo_b, 'bus', over_bus[1])  3.26 us
    pallas_call x1, Pallas kernels, local(): call(begin_kernel, 'begin', (S((16, block), F32), S((16, 128), F32), S((1...  3.01 us
    ppermute x1, starting transfers between devices, local(): halo_a = lax.ppermute(halo_a, 'bus', over_bus[0])  2.99 us
    pallas_call x1, Pallas kernels, local(): call(sweeps_kernel, 'sweeps', (S((tiles, 2 * TILE, WIN), BF16), S((LIFT +...  2.38 us
    pallas_call x1, Pallas kernels, local(): call(finish_kernel, 'finish', (S((kinds * CONV, snapshots), BF16), out_vo...  2.28 us
    ppermute x1, starting transfers between devices, local(): beside_a = lax.ppermute(lift, ('harm', 'bus'), over_ranges[0])  1.96 us
  transfers between devices with their start and end apart: 5, of which 2 were waited for; matrix products, arithmetic and copies ran while one was open for 0% of the time, Pallas kernels for 10%

profile of v13, /device:TPU:32, one launch (start us, length us, event | category | flops | bytes accessed | tf_op | source)
XLA Modules:
  0.0 41.6 jit_solution(17102023673131502844)
XLA Ops:
  0.6 3.0 %begin.1 = (f32[16,1024]{1,0:T(8,128)S(1)}, f32[16,128]{1,0:T(8,128)S(1)}, f32[16,128]{1,0:T(8,128)S(1)}, f32[8,128]{1,0:T(8,128)S(1)}, f32[128,512]{1,0:T(8,128)S(1)}, /*index=5*/bf16[768,128]{1,0:T(8,128)(2,1)}) custom-call(f32[2,4,1,1024]{3,2,1,0:T(1,128)} %adm_hbm.1, s32[3,1024]{1,0:T(4,128)} %off_hbm.1, s32[4]{0:T(128)} %type_hbm.1, f32[8]{0:T(128)} %steep_hbm.1, ...), custom_call_target="tpu_custom_call" | custom-call | flops 268435456 | bytes 1048576 | tf_op jit(solution)/shard_map/begin/pallas_call | solution.py:453
  3.6 13.8 %all-to-all-start = ((bf16[64,3,4,128]{3,2,1,0:T(4,128)(2,1)}), bf16[64,3,4,128]{3,2,1,0:T(4,128)(2,1)S(1)}, u32[]{:S(2)}, u32[]{:S(2)}) async-start(bf16[64,3,4,128]{3,2,1,0:T(4,128)(2,1)} %bitcast.1), calls=%async_computation | async-start | bytes 393216 | tf_op jit(solution)/shard_map/all_to_all | solution.py:502
  17.5 2.4 %sweeps.1 = (bf16[8,256,256]{2,1,0:T(8,128)(2,1)S(1)}, bf16[528,128]{1,0:T(8,128)(2,1)S(1)}) custom-call(f32[16,1024]{1,0:T(8,128)S(1)} %get-tuple-element.28.coef_ref, f32[128,512]{1,0:T(8,128)S(1)} %get-tuple-element.29.spec_ref, f32[8,128]{1,0:T(8,128)S(1)} %get-tuple-element.30.aux_ref), custom_call_target="tpu_custom_call" | custom-call | flops 536870912 | bytes 1048576 | tf_op jit(solution)/shard_map/sweeps/pallas_call | solution.py:504
  19.8 2.0 %collective-permute-start = (bf16[528,128]{1,0:T(8,128)(2,1)S(1)}, bf16[528,128]{1,0:T(8,128)(2,1)S(1)}, u32[]{:S(2)}, u32[]{:S(2)}) collective-permute-start(bf16[528,128]{1,0:T(8,128)(2,1)S(1)} %get-tuple-element.32.mine_ref), channel_id=1, source_target_pairs={{0,8},{16,24},{32,40},{48,56},{64,72},{80,88},{96,104},{112,120},{... | collective-permute-start | bytes 405512 | tf_op jit(solution)/shard_map/ppermute | solution.py:511
  21.8 7.0 %collective-permute-start.1 = (bf16[528,128]{1,0:T(8,128)(2,1)S(1)}, bf16[528,128]{1,0:T(8,128)(2,1)S(1)}, u32[]{:S(2)}, u32[]{:S(2)}) collective-permute-start(bf16[528,128]{1,0:T(8,128)(2,1)S(1)} %get-tuple-element.32.mine_ref), channel_id=1, source_target_pairs={{8,16},{24,32},{40,48},{56,64},{72,80},{88,96},{104,112},{120,128}... | collective-permute-start | bytes 405512 | tf_op jit(solution)/shard_map/ppermute | solution.py:512
  28.9 0.0 collective-permute-done.beside_a_ref
  28.9 0.5 %all-to-all-done = bf16[64,3,4,128]{3,2,1,0:T(4,128)(2,1)S(1)} async-done(((bf16[64,3,4,128]{3,2,1,0:T(4,128)(2,1)}), bf16[64,3,4,128]{3,2,1,0:T(4,128)(2,1)S(1)}, u32[]{:S(2)}, u32[]{:S(2)}) %all-to-all-start) | async-done | bytes 196640 | tf_op jit(solution)/shard_map/all_to_all | solution.py:502
  29.4 3.0 %collective-permute-start.2 = (bf16[96,128]{1,0:T(8,128)(2,1)S(1)}, bf16[96,128]{1,0:T(8,128)(2,1)S(1)}, u32[]{:S(2)}, u32[]{:S(2)}) collective-permute-start(bf16[96,128]{1,0:T(8,128)(2,1)S(1)} %get-tuple-element.42), channel_id=1, source_target_pairs={{0,1},{2,3},{4,5},{6,7},{1,0},{3,2},{5,4},{7,6},{8,9},{10,11},{12,... | collective-permute-start | bytes 73736 | tf_op jit(solution)/shard_map/ppermute | solution.py:522
  32.4 1.9 %collective-permute-start.3 = (bf16[96,128]{1,0:T(8,128)(2,1)S(1)}, bf16[96,128]{1,0:T(8,128)(2,1)S(1)}, u32[]{:S(2)}, u32[]{:S(2)}) collective-permute-start(bf16[96,128]{1,0:T(8,128)(2,1)S(1)} %get-tuple-element.43), channel_id=1, source_target_pairs={{1,2},{3,4},{5,6},{2,1},{4,3},{6,5},{9,10},{11,12},{13,14},{10,9},... | collective-permute-start | bytes 73736 | tf_op jit(solution)/shard_map/ppermute | solution.py:523
  34.4 0.0 collective-permute-done.1.beside_b_ref
  34.4 1.7 %inner.1 = (bf16[1024,256]{1,0:T(8,128)(2,1)S(1)}, f32[64,384]{1,0:T(8,128)S(1)}, bf16[128,384]{1,0:T(8,128)(2,1)S(1)}, bf16[128,128]{1,0:T(8,128)(2,1)S(1)}, bf16[2,1,1024,128]{3,2,1,0:T(8,128)(2,1)}) custom-call(f32[768,128]{1,0:T(8,128)S(1)} %get-tuple-element.36.rows, bf16[8,256,256]{2,1,0:T(8,128)(2,1)S(1)} %get-tuple-element.37.q_ref, ...), custom_call_target="tpu_custom_call" | custom-call | flops 268435456 | bytes 1048576 | tf_op jit(solution)/shard_map/inner/pallas_call | solution.py:525
  36.1 0.0 collective-permute-done.2.halo_a_ref
  36.1 3.3 %collective-permute-done.3.halo_b_ref = bf16[96,128]{1,0:T(8,128)(2,1)S(1)} collective-permute-done((bf16[96,128]{1,0:T(8,128)(2,1)S(1)}, bf16[96,128]{1,0:T(8,128)(2,1)S(1)}, u32[]{:S(2)}, u32[]{:S(2)}) %collective-permute-start.3) | collective-permute-done | bytes 24608 | tf_op jit(solution)/shard_map/ppermute | solution.py:523
  39.4 2.3 %finish.1 = (bf16[512,128]{1,0:T(8,128)(2,1)}, bf16[2,1,1024,128]{3,2,1,0:T(8,128)(2,1)}) custom-call(f32[64,384]{1,0:T(8,128)S(1)} %get-tuple-element.39.found_ref, bf16[128,384]{1,0:T(8,128)(2,1)S(1)} %get-tuple-element.40.pick_ref, bf16[128,128]{1,0:T(8,128)(2,1)S(1)} %get-tuple-element.41.match_ref, ...), custom_call_target="tpu_custom_call", output_to_operand_aliasing={{1}: (11, {})} | custom-call | flops 20000000 | bytes 1048576 | tf_op jit(solution)/shard_map/finish/pallas_call | solution.py:535
  (1 shorter events, 0.0 us)
Async XLA Ops:
  3.6 25.7 %all-to-all-start = ((bf16[64,3,4,128]{3,2,1,0:T(4,128)(2,1)}), bf16[64,3,4,128]{3,2,1,0:T(4,128)(2,1)S(1)}, u32[]{:S(2)}, u32[]{:S(2)}) async-start(bf16[64,3,4,128]{3,2,1,0:T(4,128)(2,1)} %bitcast.1), calls=%async_computation | async-start | bytes 393216 | tf_op jit(solution)/shard_map/all_to_all | solution.py:502
  19.8 9.0 %collective-permute-start = (bf16[528,128]{1,0:T(8,128)(2,1)S(1)}, bf16[528,128]{1,0:T(8,128)(2,1)S(1)}, u32[]{:S(2)}, u32[]{:S(2)}) collective-permute-start(bf16[528,128]{1,0:T(8,128)(2,1)S(1)} %get-tuple-element.32.mine_ref), channel_id=1, source_target_pairs={{0,8},{16,24},{32,40},{48,56},{64,72},{80,88},{96,104},{112,120},{... | collective-permute-start | bytes 405512 | tf_op jit(solution)/shard_map/ppermute | solution.py:511
  21.8 12.5 %collective-permute-start.1 = (bf16[528,128]{1,0:T(8,128)(2,1)S(1)}, bf16[528,128]{1,0:T(8,128)(2,1)S(1)}, u32[]{:S(2)}, u32[]{:S(2)}) collective-permute-start(bf16[528,128]{1,0:T(8,128)(2,1)S(1)} %get-tuple-element.32.mine_ref), channel_id=1, source_target_pairs={{8,16},{24,32},{40,48},{56,64},{72,80},{88,96},{104,112},{120,128}... | collective-permute-start | bytes 405512 | tf_op jit(solution)/shard_map/ppermute | solution.py:512
  29.4 6.7 %collective-permute-start.2 = (bf16[96,128]{1,0:T(8,128)(2,1)S(1)}, bf16[96,128]{1,0:T(8,128)(2,1)S(1)}, u32[]{:S(2)}, u32[]{:S(2)}) collective-permute-start(bf16[96,128]{1,0:T(8,128)(2,1)S(1)} %get-tuple-element.42), channel_id=1, source_target_pairs={{0,1},{2,3},{4,5},{6,7},{1,0},{3,2},{5,4},{7,6},{8,9},{10,11},{12,... | collective-permute-start | bytes 73736 | tf_op jit(solution)/shard_map/ppermute | solution.py:522
  32.4 6.9 %collective-permute-start.3 = (bf16[96,128]{1,0:T(8,128)(2,1)S(1)}, bf16[96,128]{1,0:T(8,128)(2,1)S(1)}, u32[]{:S(2)}, u32[]{:S(2)}) collective-permute-start(bf16[96,128]{1,0:T(8,128)(2,1)S(1)} %get-tuple-element.43), channel_id=1, source_target_pairs={{1,2},{3,4},{5,6},{2,1},{4,3},{6,5},{9,10},{11,12},{13,14},{10,9},... | collective-permute-start | bytes 73736 | tf_op jit(solution)/shard_map/ppermute | solution.py:523
